TPU v7x, 32 devices: a whole 2x2x4 slice. The times are simulated.
32 devices in a mesh: grp: 4 (over y, x), tile: 8 (over z, core).
Axes of the slice: x: 2, y: 2, z: 4, core: 2. Of those that a mesh axis runs over, the one named last changes fastest.
Arguments:
- state: float32 [64, 256, 512], P(None, ('grp', 'tile')), may hold values from -6 to 6
- vert_coef: float32 [63, 256, 512], P(None, ('grp', 'tile')), may hold values from 0.0004 to 1200
- horiz_coef: float32 [256, 512], P(('grp', 'tile')), may hold values from 0.02 to 0.24
- wet_mask: int32 [64, 512], P('tile'), may hold values 0 or 1
- coupling: float32 [4, 256, 512], P(None, ('grp', 'tile')), may hold values from 0.1 to 1
- surface_in: float32 [4, 256, 512], P(None, ('grp', 'tile')), may hold values from -6 to 6
- remap_w: bfloat16 [1024, 4, 128, 128], P(('grp', 'tile')), may hold values from -0.25 to 0.25
- dest_tile: int32 [1024, 4], P(('grp', 'tile')), may hold values from 0 to 7, all different within a row; in each aligned block of 32 rows (0 to 31, 32 to 63, ...) at most 32 rows name the same one
- dest_block: int32 [1024, 4], P(('grp', 'tile')), may hold values from 0 to 31
- dest_group: int32 [1024, 4], P(('grp', 'tile')), may hold values from 0 to 2
Outputs:
- state_out: float32 [64, 256, 512], P(None, ('grp', 'tile'))
- received: float32 [4, 256, 512], P(None, ('grp', 'tile'))
Inputs may be any that keep to these rules, and one draw needn't show every extreme that they name: `dest_tile`: A row's 4 strip indices differ; within the 32 rows of one device no strip index appears more than 32 times, and some device reaches 32.
All inputs are finite; a program needn't handle non-finite values. No bound on the sum of `wet_mask` on one device may be relied on, other than what follows from the above.
Results may differ from a plain program's by a relative error of at most 0.0029.
Values sent between devices are 32-bit elements; how exact they have to be, the bound alone decides.
No kernel may reach another device: no remote copies, remote signals or barrier semaphores. Data moves between devices by JAX's collectives and lax.ppermute only.
A program may use at most 64 MiB of HBM per device.

v0:
```python
import jax
import jax.numpy as jnp
from jax import lax
from jax.sharding import PartitionSpec as P

F = 4
K = 4
STEPS = 2


FORCING_GAIN = 0.25


def padded_2(block, sides, width):
    for axis, dim in sides:
        count = lax.axis_size(axis)
        forward = [(i, i + 1) for i in range(count - 1)]
        backward = [(target, source) for source, target in forward]
        low = lax.ppermute(
            lax.slice_in_dim(block, block.shape[dim] - width, None, axis=dim), axis, forward
        )
        high = lax.ppermute(lax.slice_in_dim(block, 0, width, axis=dim), axis, backward)
        block = jnp.concatenate([low, block, high], axis=dim)
    return block


def vertical_solve(column_rhs, lower, upper):

    def forward(carry, items):
        c_prev, r_prev = carry
        low, upp, rhs = items
        denom = 1.0 + low + upp + low * c_prev
        c_now = -upp / denom
        r_now = (rhs + low * r_prev) / denom
        return ((c_now, r_now), (c_now, r_now))

    zero = jnp.zeros(column_rhs.shape[1:], jnp.float32)
    _, (c_all, r_all) = lax.scan(forward, (zero, zero), (lower, upper, column_rhs), unroll=True)

    def backward(x_next, items):
        c_now, r_now = items
        x_now = r_now - c_now * x_next
        return (x_now, x_now)

    _, solved = lax.scan(backward, zero, (c_all, r_all), reverse=True, unroll=True)
    return solved


def horizontal(field, nu, wet, above, below, wet_above, wet_underneath, keep_above, keep_below):
    left = jnp.pad(field[:, :, :-1], ((0, 0), (0, 0), (1, 0)))
    right = jnp.pad(field[:, :, 1:], ((0, 0), (0, 0), (0, 1)))
    wet_left = jnp.pad(wet[:, :-1], ((0, 0), (1, 0)))
    wet_right = jnp.pad(wet[:, 1:], ((0, 0), (0, 1)))
    total = wet_left * (left - field) + wet_right * (right - field)
    total = (
        total
        + keep_above * wet_above * (above - field)
        + keep_below * wet_underneath * (below - field)
    )
    return field + nu * wet * total


def place_terms(terms, bucket, label, bucket_slots, slots):
    hits = (bucket[:, None] == jnp.arange(bucket_slots, dtype=jnp.int32)[None, :]).astype(jnp.int32)
    before = jnp.cumsum(hits, 0) - hits
    position = jnp.sum(before * hits, 1)
    slot_id = bucket * slots + position
    chooser = (
        slot_id[None, :] == jnp.arange(bucket_slots * slots, dtype=jnp.int32)[:, None]
    ).astype(jnp.float32)
    packed = jnp.dot(chooser, terms, precision=lax.Precision.HIGHEST)
    tags = jnp.dot(chooser, (label + 1).astype(jnp.float32), precision=lax.Precision.HIGHEST) - 1.0
    return (packed, tags)


def local(
    state,
    vert_coef,
    horiz_coef,
    wet_mask,
    coupling,
    surface_in,
    remap_w,
    dest_tile,
    dest_block,
    dest_group,
):
    levels, height, width = state.shape
    groups = lax.axis_size("grp")
    tiles = lax.axis_size("tile")
    group_id = lax.axis_index("grp")
    device_id = group_id * tiles + lax.axis_index("tile")
    ocean = group_id == 3
    ocean_start = 3 * tiles * height
    total_rows = groups * tiles * height
    wet = jnp.where(ocean, wet_mask.astype(jnp.float32), jnp.ones((height, width), jnp.float32))
    blocks = height * width // 128
    slots = max(2, 2 * blocks * K // tiles)
    send = (coupling * (state[0][None] - surface_in) * wet[None]).astype(jnp.bfloat16)
    send = send.reshape(F, blocks, 128).transpose(1, 0, 2)
    terms = jnp.einsum("bfi,bkij->bkfj", send, remap_w, preferred_element_type=jnp.float32)
    terms = terms.reshape(blocks * K, F * 128)
    tile_flat = dest_tile.reshape(-1)
    block_flat = dest_block.reshape(-1)
    group_flat = jnp.where(ocean, dest_group, 3).reshape(-1)
    packed, tags = place_terms(
        terms, group_flat * tiles + tile_flat, block_flat, groups * tiles, slots
    )
    got, got_tags = (
        lax.all_to_all(
            packed.reshape(groups * tiles, slots, F * 128),
            ("grp", "tile"),
            split_axis=0,
            concat_axis=0,
            tiled=True,
        ),
        lax.all_to_all(
            tags.reshape(groups * tiles, slots),
            ("grp", "tile"),
            split_axis=0,
            concat_axis=0,
            tiled=True,
        ),
    )
    requested_items = jnp.arange(blocks, dtype=jnp.int32).astype(jnp.float32)
    chooser = (got_tags.reshape(-1)[None, :] == requested_items[:, None]).astype(jnp.float32)
    gathered = jnp.dot(chooser, got.reshape(-1, F * 128), precision=lax.Precision.HIGHEST)
    received = gathered.reshape(blocks, F, 128).transpose(1, 0, 2).reshape(F, height, width)
    row_ids = device_id * height + jnp.arange(height, dtype=jnp.int32)
    keep_above = ((row_ids > 0) & (row_ids != ocean_start)).astype(jnp.float32)[:, None]
    keep_below = ((row_ids < total_rows - 1) & (row_ids + 1 != ocean_start)).astype(jnp.float32)[
        :, None
    ]
    forcing = FORCING_GAIN * wet * jnp.sum(received, 0)
    scaled = vert_coef * wet[None]
    edge = jnp.zeros((1, height, width), jnp.float32)
    lower = jnp.concatenate([edge, scaled], 0)
    upper = jnp.concatenate([scaled, edge], 0)
    field = state
    for step in range(STEPS):
        stacked = jnp.concatenate([field, wet[None]], 0)
        padded = padded_2(stacked, ((("grp", "tile"), 1),), 1)
        above = padded[:levels, :-2]
        below = padded[:levels, 2:]
        wet_above = padded[levels, :-2]
        wet_underneath = padded[levels, 2:]
        field = horizontal(
            field, horiz_coef, wet, above, below, wet_above, wet_underneath, keep_above, keep_below
        )
        field = field.at[0].add(forcing)
        field = vertical_solve(field, lower, upper)
    return (field, received)


def solution(mesh):
    in_specs = (
        P(None, ("grp", "tile"), None),
        P(None, ("grp", "tile"), None),
        P(("grp", "tile"), None),
        P("tile", None),
        P(None, ("grp", "tile"), None),
        P(None, ("grp", "tile"), None),
        P(("grp", "tile"), None, None, None),
        P(("grp", "tile"), None),
        P(("grp", "tile"), None),
        P(("grp", "tile"), None),
    )
    out_specs = (P(None, ("grp", "tile"), None), P(None, ("grp", "tile"), None))
    return jax.shard_map(local, mesh=mesh, in_specs=in_specs, out_specs=out_specs, check_vma=False)
```

profile of v0, /device:TPU:4, one launch (start us, length us, event | category | flops | bytes accessed | tf_op | source)
XLA Modules:
  0.0 119.7 jit_solution(11383672501700154401)
XLA Ops:
  0.7 1.4 %fusion.442 = (f32[8,512]{1,0:T(8,128)}, f32[8,512]{1,0:T(8,128)S(1)}) fusion(f32[8,512]{1,0:T(8,128)} %param.16, s32[8,512]{1,0:T(8,128)} %param.17, pred[]{:T(512)S(6)} %eq.61), kind=kLoop, calls=%fused_computation.1354 | loop fusion | flops 12288 | bytes 65537 | tf_op jit(solution)/shard_map/mul | solution.py:60
  2.1 1.8 %pad_maximum_fusion.7 = (f32[65,1,512]{2,1,0:T(1,128)S(1)}, f32[65,1,512]{2,1,0:T(1,128)S(1)}) fusion(f32[1,8,512]{2,1,0:T(8,128)S(1)} %bitcast.3014, f32[64,8,512]{2,1,0:T(8,128)} %param.14), kind=kLoop, calls=%fused_computation.226 | loop fusion | flops 66560 | bytes 1331200 | tf_op jit(solution)/shard_map/slice | solution.py:20
  4.0 2.1 %collective-permute-start = (f32[65,1,512]{2,1,0:T(1,128)S(1)}, f32[65,1,512]{2,1,0:T(1,128)S(1)}, u32[]{:S(2)}, u32[]{:S(2)}) collective-permute-start(f32[65,1,512]{2,1,0:T(1,128)S(1)} %get-tuple-element.431), channel_id=1, source_target_pairs={{0,1},{1,2},{2,3},{3,4},{4,5},{5,6},{6,7},{7,8},{8,9},{9,10},{10,1... | collective-permute-start | bytes 399368 | tf_op jit(solution)/shard_map/ppermute | solution.py:19
  6.0 7.2 %collective-permute-start.1 = (f32[65,1,512]{2,1,0:T(1,128)S(1)}, f32[65,1,512]{2,1,0:T(1,128)S(1)}, u32[]{:S(2)}, u32[]{:S(2)}) collective-permute-start(f32[65,1,512]{2,1,0:T(1,128)S(1)} %get-tuple-element.432), channel_id=1, source_target_pairs={{1,0},{2,1},{3,2},{4,3},{5,4},{6,5},{7,6},{8,7},{9,8},{10,9},{11,1... | collective-permute-start | bytes 399368 | tf_op jit(solution)/shard_map/ppermute | solution.py:22
  14.5 0.7 all_to_all.9
  15.2 2.5 %all-to-all-start = ((f32[32,1,32]{2,1,0:T(1,128)}), f32[32,1,32]{2,1,0:T(1,128)S(1)}, u32[]{:S(2)}, u32[]{:S(2)}) async-start(f32[32,1,32]{2,1,0:T(1,128)} %all_to_all.9), calls=%async_computation | async-start | bytes 32768 | tf_op jit(solution)/shard_map/all_to_all | solution.py:117
  18.6 2.8 %convolution_bitcast_fusion = f32[32,4,4,128]{3,2,1,0:T(4,128)S(1)} fusion(bf16[32,4,128,128]{3,2,1,0:T(8,128)(2,1)} %param.20, bf16[4,32,128]{2,1,0:T(8,128)(2,1)S(1)} %reshape.185), kind=kOutput, calls=%fused_computation | convolution fusion | flops 16777216 | bytes 4489216 | tf_op jit(solution)/shard_map/bfi,bkij->bkfj/dot_general | solution.py:101
  21.5 2.4 %fusion.16 = f32[32,32,512]{2,1,0:T(8,128)} fusion(f32[128,512,1]{1,0,2:T(8,128)S(1)} %reshape.193, s32[32,32]{1,0:T(8,128)S(1)} %multiply_add_fusion.63, s32[128]{0:T(128)S(1)} %multiply_add_fusion.65), kind=kOutput, calls=%fused_computation.25 | convolution fusion | flops 805437440 | bytes 2363904 | tf_op jit(solution)/shard_map/dot_general | solution.py:71
  23.9 5.9 %all-to-all-start.1 = ((f32[32,32,512]{2,1,0:T(8,128)}), f32[32,32,512]{2,1,0:T(8,128)}, u32[]{:S(2)}, u32[]{:S(2)}) async-start(f32[32,32,512]{2,1,0:T(8,128)} %fusion.16), calls=%async_computation.1 | async-start | bytes 4194304 | tf_op jit(solution)/shard_map/all_to_all | solution.py:110
  32.5 0.8 fusion.208
  33.3 1.7 %fusion.445 = (f32[64,8,511]{2,1,0:T(8,128)}, f32[64,8,511]{2,1,0:T(8,128)}) fusion(f32[64,8,512]{2,1,0:T(8,128)S(1)} %copy-done), kind=kLoop, calls=%fused_computation.1357 | loop fusion | bytes 4186112 | tf_op jit(solution)/shard_map/slice | solution.py:50
  36.2 2.4 %fusion.12 = f32[64,8,512]{2,1,0:T(8,128)S(1)} fusion(f32[64,8,512]{2,1,0:T(8,128)S(1)} %copy-done, f32[65,1,512]{2,1,0:T(1,128)S(1)} %collective-permute-done.1, f32[1,8,512]{2,1,0:T(8,128)S(1)} %bitcast.3016, f32[65,1,512]{2,1,0:T(1,128)S(1)} %collective-permute-done, f32[64,8,511]{2,1,0:T(8,128)} %get-tuple-element.437, ...), kind=kLoop, calls=%fused_computation.17 | loop fusion | flops 4456448 | bytes 4554752 | tf_op jit(solution)/shard_map/add | solution.py:60
  38.6 40.1 %all-to-all-done.1 = f32[32,32,512]{2,1,0:T(8,128)} async-done(((f32[32,32,512]{2,1,0:T(8,128)}), f32[32,32,512]{2,1,0:T(8,128)}, u32[]{:S(2)}, u32[]{:S(2)}) %all-to-all-start.1) | async-done | bytes 2097184 | tf_op jit(solution)/shard_map/all_to_all | solution.py:110
  78.8 3.0 %copy.19 = f32[512,1024]{1,0:T(8,128)} copy(f32[512,1024]{0,1:T(8,128)} %bitcast.11) | data formatting | bytes 4194304 | tf_op jit(solution)/shard_map/dot_general | solution.py:127
  82.0 3.4 %fusion.447 = (f32[32,128]{1,0:T(8,128)S(1)}, f32[4,32,128]{2,1,0:T(8,128)}) fusion(f32[4,128,1024]{2,1,0:T(8,128)} %bitcast.3013, f32[1024]{0:T(1024)S(1)} %eq.68, f32[32]{0:T(128)S(1)} %copy-done.209), kind=kOutput, calls=%fused_computation.1359 | convolution fusion | flops 201371648 | bytes 2183296 | tf_op jit(solution)/shard_map/dot_general | solution.py:127
  85.8 1.0 fusion.102
  87.2 1.1 constant_dynamic-update-slice_fusion.128
  88.7 1.0 add_divide_fusion.41
  90.1 1.2 constant_dynamic-update-slice_fusion.127
  92.5 1.0 copy-done.1
  93.5 0.9 fusion.443
  94.4 2.2 %collective-permute-start.2 = (f32[65,1,512]{2,1,0:T(1,128)}, f32[65,1,512]{2,1,0:T(1,128)S(1)}, u32[]{:S(2)}, u32[]{:S(2)}) collective-permute-start(f32[65,1,512]{2,1,0:T(1,128)} %get-tuple-element.427), channel_id=1, source_target_pairs={{0,1},{1,2},{2,3},{3,4},{4,5},{5,6},{6,7},{7,8},{8,9},{9,10},{10,1... | collective-permute-start | bytes 399368 | tf_op jit(solution)/shard_map/ppermute | solution.py:19
  96.6 7.1 %collective-permute-start.3 = (f32[65,1,512]{2,1,0:T(1,128)}, f32[65,1,512]{2,1,0:T(1,128)S(1)}, u32[]{:S(2)}, u32[]{:S(2)}) collective-permute-start(f32[65,1,512]{2,1,0:T(1,128)} %get-tuple-element.428), channel_id=1, source_target_pairs={{1,0},{2,1},{3,2},{4,3},{5,4},{6,5},{7,6},{8,7},{9,8},{10,9},{11,1... | collective-permute-start | bytes 399368 | tf_op jit(solution)/shard_map/ppermute | solution.py:22
  103.7 1.7 %fusion.444 = (f32[64,8,511]{2,1,0:T(8,128)}, f32[64,8,511]{2,1,0:T(8,128)}) fusion(f32[64,8,512]{2,1,0:T(8,128)S(1)} %get-tuple-element.439), kind=kLoop, calls=%fused_computation.1356 | loop fusion | bytes 4186112 | tf_op jit(solution)/shard_map/slice | solution.py:50
  105.4 1.5 %reshape.189 = f32[4,8,512]{2,1,0:T(8,128)} reshape(f32[4,32,128]{2,1,0:T(8,128)} %get-tuple-element.565) | data formatting | bytes 131072 | tf_op jit(solution)/shard_map/reshape | solution.py:128
  107.1 1.1 copy-done.3
  108.2 2.1 %fusion.4 = f32[64,8,512]{2,1,0:T(8,128)S(1)} fusion(f32[64,8,512]{2,1,0:T(8,128)S(1)} %get-tuple-element.439, f32[65,1,512]{2,1,0:T(1,128)S(1)} %collective-permute-done.3, f32[65,8,512]{2,1,0:T(8,128)S(1)} %copy-done.2, f32[65,1,512]{2,1,0:T(1,128)S(1)} %collective-permute-done.2, f32[64,8,511]{2,1,0:T(8,128)} %get-tuple-element.434, ...), kind=kLoop, calls=%fused_computation.7 | loop fusion | flops 3932160 | bytes 5603328 | tf_op jit(solution)/shard_map/add | solution.py:60
  110.7 1.5 %add_divide_fusion.1 = (f32[1,8,512]{2,1,0:T(8,128)S(1)}, f32[1,8,512]{2,1,0:T(8,128)S(1)}, f32[1,8,512]{2,1,0:T(8,128)S(1)}, f32[1,8,512]{2,1,0:T(8,128)S(1)}, ...) fusion(f32[1,8,512]{2,1,0:T(8,128)} %copy-done.100, ...), kind=kLoop, calls=%fused_computation.1048 | loop fusion | flops 532480 | bytes 2670592 | tf_op jit(solution)/shard_map/eval_jaxpr/div | solution.py:34
  112.6 1.4 %fusion.36 = (f32[8,512]{1,0:T(8,128)S(1)}, f32[8,512]{1,0:T(8,128)S(1)}, f32[8,512]{1,0:T(8,128)S(1)}, f32[8,512]{1,0:T(8,128)S(1)}, f32[8,512]{1,0:T(8,128)S(1...) fusion(f32[8,512]{1,0:T(8,128)S(1)} %copy-done.55, ...), kind=kLoop, calls=%fused_computation.253 | loop fusion | flops 757760 | bytes 3670016 | tf_op jit(solution)/shard_map/eval_jaxpr/div | solution.py:34
  114.5 1.4 %constant_dynamic-update-slice_fusion.192 = (f32[64,8,512]{2,1,0:T(8,128)S(1)}, f32[8,512]{1,0:T(8,128)S(1)}, f32[8,512]{1,0:T(8,128)S(1)}, f32[8,512]{1,0:T(8,1...) fusion(f32[8,512]{1,0:T(8,128)S(1)} %get-tuple-element.141, ...), kind=kLoop, calls=%fused_computation.221 | loop fusion | flops 1265663 | bytes 3162112
  116.2 1.3 %constant_dynamic-update-slice_fusion.191 = (f32[64,8,512]{2,1,0:T(8,128)S(1)}, f32[1,8,512]{2,1,0:T(8,128)S(1)}, f32[1,8,512]{2,1,0:T(8,128)S(1)}, f32[1,8,512]...) fusion(f32[64,8,512]{2,1,0:T(8,128)S(1)} %get-tuple-element.90,, ...), kind=kLoop, calls=%fused_computation.220 | loop fusion | flops 1495040 | bytes 2785280
  118.7 1.0 copy-done.210
  (582 shorter events, 7.8 us)
Async XLA Ops:
  0.6 17.2 %copy-start = (f32[64,8,512]{2,1,0:T(8,128)S(1)}, f32[64,8,512]{2,1,0:T(8,128)}, u32[]{:S(2)}) copy-start(f32[64,8,512]{2,1,0:T(8,128)} %param.14) | copy-start | bytes 3145732
  0.6 12.6 %copy-start.206 = (s32[32,4]{0,1:T(4,128)S(1)}, s32[32,4]{0,1:T(4,128)}, u32[]{:S(2)}) copy-start(s32[32,4]{0,1:T(4,128)} %param.21) | copy-start | bytes 1540
  0.7 12.6 %copy-start.207 = (s32[32,4]{0,1:T(4,128)S(1)}, s32[32,4]{0,1:T(4,128)}, u32[]{:S(2)}) copy-start(s32[32,4]{0,1:T(4,128)} %param.23) | copy-start | bytes 1540
  0.7 13.3 %copy-start.208 = (s32[32,4]{0,1:T(4,128)S(1)}, s32[32,4]{0,1:T(4,128)}, u32[]{:S(2)}) copy-start(s32[32,4]{0,1:T(4,128)} %param.22) | copy-start | bytes 1540
  3.9 14.6 %copy-start.202 = (f32[4,8,512]{2,1,0:T(8,128)S(1)}, f32[4,8,512]{2,1,0:T(8,128)}, u32[]{:S(2)}) copy-start(f32[4,8,512]{2,1,0:T(8,128)} %param.18) | copy-start | bytes 196612
  3.9 14.6 %copy-start.203 = (f32[4,8,512]{2,1,0:T(8,128)S(1)}, f32[4,8,512]{2,1,0:T(8,128)}, u32[]{:S(2)}) copy-start(f32[4,8,512]{2,1,0:T(8,128)} %param.19) | copy-start | bytes 196612
  4.0 13.8 %collective-permute-start = (f32[65,1,512]{2,1,0:T(1,128)S(1)}, f32[65,1,512]{2,1,0:T(1,128)S(1)}, u32[]{:S(2)}, u32[]{:S(2)}) collective-permute-start(f32[65,1,512]{2,1,0:T(1,128)S(1)} %get-tuple-element.431), channel_id=1, source_target_pairs={{0,1},{1,2},{2,3},{3,4},{4,5},{5,6},{6,7},{7,8},{8,9},{9,10},{10,1... | collective-permute-start | bytes 399368 | tf_op jit(solution)/shard_map/ppermute | solution.py:19
  6.0 11.8 %collective-permute-start.1 = (f32[65,1,512]{2,1,0:T(1,128)S(1)}, f32[65,1,512]{2,1,0:T(1,128)S(1)}, u32[]{:S(2)}, u32[]{:S(2)}) collective-permute-start(f32[65,1,512]{2,1,0:T(1,128)S(1)} %get-tuple-element.432), channel_id=1, source_target_pairs={{1,0},{2,1},{3,2},{4,3},{5,4},{6,5},{7,6},{8,7},{9,8},{10,9},{11,1... | collective-permute-start | bytes 399368 | tf_op jit(solution)/shard_map/ppermute | solution.py:22
  15.2 8.7 %all-to-all-start = ((f32[32,1,32]{2,1,0:T(1,128)}), f32[32,1,32]{2,1,0:T(1,128)S(1)}, u32[]{:S(2)}, u32[]{:S(2)}) async-start(f32[32,1,32]{2,1,0:T(1,128)} %all_to_all.9), calls=%async_computation | async-start | bytes 32768 | tf_op jit(solution)/shard_map/all_to_all | solution.py:117
  23.9 7.8 %copy-start.4 = (f32[63,8,512]{2,1,0:T(8,128)S(1)}, f32[63,8,512]{2,1,0:T(8,128)}, u32[]{:S(2)}) copy-start(f32[63,8,512]{2,1,0:T(8,128)} %param.15) | copy-start | bytes 3096580
  23.9 54.8 %all-to-all-start.1 = ((f32[32,32,512]{2,1,0:T(8,128)}), f32[32,32,512]{2,1,0:T(8,128)}, u32[]{:S(2)}, u32[]{:S(2)}) async-start(f32[32,32,512]{2,1,0:T(8,128)} %fusion.16), calls=%async_computation.1 | async-start | bytes 4194304 | tf_op jit(solution)/shard_map/all_to_all | solution.py:110
  33.3 54.0 %copy-start.5 = (f32[8,512]{1,0:T(8,128)}, f32[8,512]{1,0:T(8,128)S(1)}, u32[]{:S(2)}) copy-start(f32[8,512]{1,0:T(8,128)S(1)} %get-tuple-element.392) | copy-start | bytes 49156
  81.8 3.7 %copy-start.7 = (f32[8,512]{1,0:T(8,128)S(1)}, f32[8,512]{1,0:T(8,128)}, u32[]{:S(2)}) copy-start(f32[8,512]{1,0:T(8,128)} %get-tuple-element.393) | copy-start | bytes 49156
  81.8 3.7 %copy-start.9 = (f32[8,512]{1,0:T(8,128)S(1)}, f32[8,512]{1,0:T(8,128)}, u32[]{:S(2)}) copy-start(f32[8,512]{1,0:T(8,128)} %get-tuple-element.394) | copy-start | bytes 49156
  81.8 3.7 %copy-start.11 = (f32[8,512]{1,0:T(8,128)S(1)}, f32[8,512]{1,0:T(8,128)}, u32[]{:S(2)}) copy-start(f32[8,512]{1,0:T(8,128)} %get-tuple-element.395) | copy-start | bytes 49156
  81.8 3.7 %copy-start.13 = (f32[8,512]{1,0:T(8,128)S(1)}, f32[8,512]{1,0:T(8,128)}, u32[]{:S(2)}) copy-start(f32[8,512]{1,0:T(8,128)} %get-tuple-element.396) | copy-start | bytes 49156
  81.8 3.7 %copy-start.15 = (f32[8,512]{1,0:T(8,128)S(1)}, f32[8,512]{1,0:T(8,128)}, u32[]{:S(2)}) copy-start(f32[8,512]{1,0:T(8,128)} %get-tuple-element.397) | copy-start | bytes 49156
  81.8 3.7 %copy-start.17 = (f32[8,512]{1,0:T(8,128)S(1)}, f32[8,512]{1,0:T(8,128)}, u32[]{:S(2)}) copy-start(f32[8,512]{1,0:T(8,128)} %get-tuple-element.398) | copy-start | bytes 49156
  81.8 3.7 %copy-start.19 = (f32[8,512]{1,0:T(8,128)S(1)}, f32[8,512]{1,0:T(8,128)}, u32[]{:S(2)}) copy-start(f32[8,512]{1,0:T(8,128)} %get-tuple-element.399) | copy-start | bytes 49156
  81.9 3.7 %copy-start.21 = (f32[8,512]{1,0:T(8,128)S(1)}, f32[8,512]{1,0:T(8,128)}, u32[]{:S(2)}) copy-start(f32[8,512]{1,0:T(8,128)} %get-tuple-element.400) | copy-start | bytes 49156
  81.9 3.7 %copy-start.23 = (f32[8,512]{1,0:T(8,128)S(1)}, f32[8,512]{1,0:T(8,128)}, u32[]{:S(2)}) copy-start(f32[8,512]{1,0:T(8,128)} %get-tuple-element.401) | copy-start | bytes 49156
  81.9 3.7 %copy-start.25 = (f32[8,512]{1,0:T(8,128)S(1)}, f32[8,512]{1,0:T(8,128)}, u32[]{:S(2)}) copy-start(f32[8,512]{1,0:T(8,128)} %get-tuple-element.402) | copy-start | bytes 49156
  81.9 3.7 %copy-start.27 = (f32[8,512]{1,0:T(8,128)S(1)}, f32[8,512]{1,0:T(8,128)}, u32[]{:S(2)}) copy-start(f32[8,512]{1,0:T(8,128)} %get-tuple-element.403) | copy-start | bytes 49156
  81.9 3.7 %copy-start.29 = (f32[8,512]{1,0:T(8,128)S(1)}, f32[8,512]{1,0:T(8,128)}, u32[]{:S(2)}) copy-start(f32[8,512]{1,0:T(8,128)} %get-tuple-element.404) | copy-start | bytes 49156
  81.9 3.7 %copy-start.31 = (f32[8,512]{1,0:T(8,128)S(1)}, f32[8,512]{1,0:T(8,128)}, u32[]{:S(2)}) copy-start(f32[8,512]{1,0:T(8,128)} %get-tuple-element.405) | copy-start | bytes 49156
  81.9 3.7 %copy-start.33 = (f32[8,512]{1,0:T(8,128)S(1)}, f32[8,512]{1,0:T(8,128)}, u32[]{:S(2)}) copy-start(f32[8,512]{1,0:T(8,128)} %get-tuple-element.406) | copy-start | bytes 49156
  81.9 3.7 %copy-start.35 = (f32[8,512]{1,0:T(8,128)S(1)}, f32[8,512]{1,0:T(8,128)}, u32[]{:S(2)}) copy-start(f32[8,512]{1,0:T(8,128)} %get-tuple-element.407) | copy-start | bytes 49156
  81.9 3.7 %copy-start.37 = (f32[8,512]{1,0:T(8,128)S(1)}, f32[8,512]{1,0:T(8,128)}, u32[]{:S(2)}) copy-start(f32[8,512]{1,0:T(8,128)} %get-tuple-element.408) | copy-start | bytes 49156
  81.9 3.7 %copy-start.39 = (f32[8,512]{1,0:T(8,128)S(1)}, f32[8,512]{1,0:T(8,128)}, u32[]{:S(2)}) copy-start(f32[8,512]{1,0:T(8,128)} %get-tuple-element.409) | copy-start | bytes 49156
  82.0 3.7 %copy-start.41 = (f32[8,512]{1,0:T(8,128)S(1)}, f32[8,512]{1,0:T(8,128)}, u32[]{:S(2)}) copy-start(f32[8,512]{1,0:T(8,128)} %get-tuple-element.410) | copy-start | bytes 49156
  94.4 12.6 %collective-permute-start.2 = (f32[65,1,512]{2,1,0:T(1,128)}, f32[65,1,512]{2,1,0:T(1,128)S(1)}, u32[]{:S(2)}, u32[]{:S(2)}) collective-permute-start(f32[65,1,512]{2,1,0:T(1,128)} %get-tuple-element.427), channel_id=1, source_target_pairs={{0,1},{1,2},{2,3},{3,4},{4,5},{5,6},{6,7},{7,8},{8,9},{9,10},{10,1... | collective-permute-start | bytes 399368 | tf_op jit(solution)/shard_map/ppermute | solution.py:19
  96.6 10.4 %collective-permute-start.3 = (f32[65,1,512]{2,1,0:T(1,128)}, f32[65,1,512]{2,1,0:T(1,128)S(1)}, u32[]{:S(2)}, u32[]{:S(2)}) collective-permute-start(f32[65,1,512]{2,1,0:T(1,128)} %get-tuple-element.428), channel_id=1, source_target_pairs={{1,0},{2,1},{3,2},{4,3},{5,4},{6,5},{7,6},{8,7},{9,8},{10,9},{11,1... | collective-permute-start | bytes 399368 | tf_op jit(solution)/shard_map/ppermute | solution.py:22
  (185 other events, 308.9 us)
where the time goes:
time: 121 us; the launch traced here: 120 us
  waiting for transfers between devices  40.1 us (33%)
  starting transfers between devices  27 us (22%)
  other arithmetic  22.1 us (18%)
  local copies, waits for them, and re-layouts  16.5 us (14%)
  matrix products  9.03 us (7%)
  between operations  4.9 us (4%)
    all_to_all x1, waiting for transfers between devices, local(): lax.all_to_all(packed.reshape(groups * tiles, slots, F * 128), ('grp', 't...  40.1 us
    ppermute x2, starting transfers between devices, padded_2(): lax.ppermute(lax.slice_in_dim(block, 0, width, axis=dim), axis, backward)  14.3 us
    all_to_all x1, starting transfers between devices, local(): lax.all_to_all(packed.reshape(groups * tiles, slots, F * 128), ('grp', 't...  5.88 us
    unnamed x35, other arithmetic  5.19 us
    div x6, other arithmetic, forward(): r_now = (rhs + low * r_prev) / denom  5.18 us
    add x2, other arithmetic, horizontal(): return field + nu * wet * total  4.56 us
    unnamed x516, local copies, waits for them, and re-layouts  4.51 us
    ppermute x2, starting transfers between devices, padded_2(): lax.ppermute(lax.slice_in_dim(block, block.shape[dim] - width, None, axis...  4.27 us
  transfers between devices with their start and end apart: 6, of which 1 were waited for; matrix products, arithmetic and copies ran while one was open for 16% of the time, Pallas kernels for 0%

commit v1 on v0

v1 whole, which is shorter than its diff:
```python
import functools

import jax
import jax.numpy as jnp
from jax import lax
from jax.experimental import pallas as pl
from jax.experimental.pallas import tpu as pltpu
from jax.sharding import PartitionSpec as P

F = 4
K = 4
FORCING_GAIN = 0.25
VM = pl.BlockSpec(memory_space=pltpu.VMEM)
MIB = 1024 * 1024


def params(mib):
    return pltpu.CompilerParams(vmem_limit_bytes=mib * MIB)


def split(x):
    hi = x.astype(jnp.bfloat16)
    return hi, (x - hi.astype(jnp.float32)).astype(jnp.bfloat16)


def wet_of(ocean, mask):
    return jnp.where(ocean, mask.astype(jnp.float32), 1.0)


def iota(shape, dim):
    return lax.broadcasted_iota(jnp.int32, shape, dim)


def pack_kernel(
    tiles, slots, state, coupling, surface, mask, dtile, dblock, dgroup, w_hbm, out, w, terms, sem
):
    height, width = mask.shape
    cols = width // 128
    blocks = height * cols
    count = blocks * K
    copies = [
        pltpu.make_async_copy(w_hbm.at[:, c], w.at[c], sem.at[c]) for c in range(cols)
    ]
    for copy in copies:
        copy.start()
    ocean = lax.axis_index("grp") == 3
    me = lax.axis_index("tile")

    block = dblock[...]
    row = (block % cols) * height + block // cols
    code = dtile[...] * 128 + row + jnp.where(ocean, dgroup[...] * blocks, 0)
    lane = iota((blocks, count), 1)
    lane_k = (lane // height) % K
    spread = jnp.zeros((blocks, count), jnp.int32)
    for k in range(K):
        spread = jnp.where(lane_k == k, code[:, k : k + 1], spread)
    own = iota((blocks, count), 0) == (lane % height) * cols + lane // (height * K)
    code_row = jnp.sum(jnp.where(own, spread, 0), 0, keepdims=True)
    up, down = iota((count, count), 0), iota((count, count), 1)
    code_col = jnp.sum(jnp.where(up == down, code_row, 0), 1, keepdims=True)
    tile_row, tile_col, tag_col = code_row // 128, code_col // 128, code_col % 128
    same = tile_row == tile_col
    place_row = jnp.sum(jnp.where(same & (up < down), 1, 0), 0, keepdims=True)
    place_col = jnp.sum(jnp.where(same & (down < up), 1, 0), 1, keepdims=True)
    slot_row = tile_row * slots + place_row
    chooser = jnp.where(iota((tiles * slots, count), 0) == slot_row, 1.0, 0.0).astype(jnp.bfloat16)
    to_tile = jnp.where(iota((tiles, count), 0) == tile_row, 1.0, 0.0).astype(jnp.bfloat16)
    labels = jnp.where(
        iota((count, tiles * slots), 1) == me * slots + place_col,
        (tag_col + 1).astype(jnp.float32),
        0.0,
    ).astype(jnp.bfloat16)
    tags = jnp.dot(to_tile, labels, preferred_element_type=jnp.float32)
    out[:, F * slots :, :] = jnp.zeros((tiles, out.shape[1] - F * slots, 128), jnp.float32)
    for t in range(tiles):
        for part in range(tiles * slots // 128):
            out[t, F * slots + part : F * slots + part + 1, :] = tags[
                t : t + 1, part * 128 : (part + 1) * 128
            ]

    send = coupling[...] * (state[...] - surface[...]) * wet_of(ocean, mask[...])[None]
    row_of = iota((F * height, 128), 0) % height
    for c in range(cols):
        piece = send[:, :, c * 128 : (c + 1) * 128].reshape(F * height, 128)
        left = jnp.concatenate(
            [jnp.where(row_of == r, piece, 0.0).astype(jnp.bfloat16) for r in range(height)], 1
        )
        copies[c].wait()
        for k in range(K):
            right = w[c, :, k].reshape(height * 128, 128)
            made = jnp.dot(left, right, preferred_element_type=jnp.float32)
            at = (c * K + k) * height
            for f in range(F):
                terms[at : at + height, f * 128 : (f + 1) * 128] = made[
                    f * height : (f + 1) * height, :
                ]
    hi, lo = split(terms[...])
    packed = jnp.dot(
        jnp.concatenate([chooser, chooser], 1),
        jnp.concatenate([hi, lo], 0),
        preferred_element_type=jnp.float32,
    )
    for t in range(tiles):
        for f in range(F):
            out[t, f * slots : (f + 1) * slots, :] = packed[
                t * slots : (t + 1) * slots, f * 128 : (f + 1) * 128
            ]


def merge_kernel(tiles, slots, blocks, groups, got, *outs):
    ocean = lax.axis_index("grp") == groups - 1
    tags = got[0, F * slots :, :]
    for t in range(1, tiles):
        tags = tags + got[t, F * slots :, :]
    rows = (groups - 1) * blocks
    total = tiles * slots
    label = jnp.concatenate([tags[p : p + 1, :] for p in range(total // 128)], 1).astype(jnp.int32)
    ids = iota((rows, total), 0)
    ids = jnp.where(ocean, ids, ids % blocks) + 1
    chooser = jnp.where(ids == label, 1.0, 0.0).astype(jnp.bfloat16)
    for f in range(F):
        data = jnp.concatenate([got[t, f * slots : (f + 1) * slots, :] for t in range(tiles)], 0)
        hi, lo = split(data)
        merged = jnp.dot(chooser, hi, preferred_element_type=jnp.float32) + jnp.dot(
            chooser, lo, preferred_element_type=jnp.float32
        )
        for g in range(groups - 1):
            outs[g][f * blocks : (f + 1) * blocks, :] = merged[g * blocks : (g + 1) * blocks, :]


def edge_kernel(state, mask, top, bottom):
    levels, height, width = state.shape
    top[...] = jnp.zeros(top.shape, jnp.float32)
    bottom[...] = jnp.zeros(bottom.shape, jnp.float32)
    top[:levels, :] = state[:, 0, :]
    bottom[:levels, :] = state[:, height - 1, :]
    wet = wet_of(lax.axis_index("grp") == 3, mask[...])
    top[levels : levels + 1, :] = wet[:1]
    bottom[levels : levels + 1, :] = wet[height - 1 :]


def weights_of(tiles, groups, horiz, wet, wet_above, wet_below):
    height, width = wet.shape
    device = lax.axis_index("grp") * tiles + lax.axis_index("tile")
    rows = device * height + iota((height, width), 0)
    start = (groups - 1) * tiles * height
    last = groups * tiles * height - 1
    above = jnp.concatenate([wet_above, wet[:-1]], 0)
    below = jnp.concatenate([wet[1:], wet_below], 0)
    above = jnp.where((rows > 0) & (rows != start), above, 0.0)
    below = jnp.where((rows < last) & (rows + 1 != start), below, 0.0)
    column = iota((height, width), 1)
    left = jnp.where(column == 0, 0.0, pltpu.roll(wet, 1, 1))
    right = jnp.where(column == width - 1, 0.0, pltpu.roll(wet, width - 1, 1))
    scale = horiz * wet
    return scale * left, scale * right, scale * above, scale * below


def stencil(field, top, bottom, weights):
    left, right, above, below = weights
    height, width = field.shape
    return (
        field
        + left * (pltpu.roll(field, 1, 1) - field)
        + right * (pltpu.roll(field, width - 1, 1) - field)
        + above * (jnp.concatenate([top, field[:-1]], 0) - field)
        + below * (jnp.concatenate([field[1:], bottom], 0) - field)
    )


def base_kernel(
    tiles, groups, state, vert, horiz, mask, from_above, from_below, upper, gain, ratio, base, impulse, weights
):
    levels, height, width = state.shape
    wet = wet_of(lax.axis_index("grp") == groups - 1, mask[...])
    made = weights_of(
        tiles,
        groups,
        horiz[...],
        wet,
        from_above[levels : levels + 1, :],
        from_below[levels : levels + 1, :],
    )
    for i in range(4):
        weights[i] = made[i]
    zero = jnp.zeros((height, width), jnp.float32)

    def forward(level, carry, last=False, first=False):
        low, c, r, e = carry
        upp = zero if last else vert[level] * wet
        inverse = 1.0 / (1.0 + low + upp + low * c)
        c = -upp * inverse
        step = low * inverse
        field = stencil(
            state[level], from_above[pl.ds(level, 1), :], from_below[pl.ds(level, 1), :], made
        )
        r = field * inverse + step * r
        e = inverse if first else step * e
        upper[level] = c
        gain[level] = inverse
        ratio[level] = step
        base[level] = r
        impulse[level] = e
        return upp, c, r, e

    carry = forward(0, (zero, zero, zero, zero), first=True)
    carry = lax.fori_loop(1, levels - 1, forward, carry, unroll=2)
    _, _, r, e = forward(levels - 1, carry, last=True)

    def backward(i, carry):
        level = levels - 2 - i
        c = upper[level]
        x = base[level] - c * carry[0]
        y = impulse[level] - c * carry[1]
        base[level] = x
        impulse[level] = y
        return x, y

    lax.fori_loop(0, levels - 1, backward, (r, e), unroll=2)


def force_kernel(cols, base, impulse, mask, r0, r1, r2, field, received, force, top, bottom):
    levels, height, width = base.shape
    wet = wet_of(lax.axis_index("grp") == 3, mask[...])
    total = r0[...] + r1[...] + r2[...]
    for f in range(F):
        for c in range(cols):
            at = (f * cols + c) * height
            received[f, :, c * 128 : (c + 1) * 128] = total[at : at + height, :]
    forcing = FORCING_GAIN * wet * jnp.sum(received[...], 0)
    force[...] = forcing

    def one(level, _):
        x = base[level] + impulse[level] * forcing
        field[level] = x
        top[pl.ds(level, 1), :] = x[:1]
        bottom[pl.ds(level, 1), :] = x[height - 1 :]
        return 0

    lax.fori_loop(0, levels, one, 0, unroll=2)


def last_kernel(field, force, from_above, from_below, upper, gain, ratio, weights, out):
    levels, height, width = field.shape
    made = tuple(weights[i] for i in range(4))

    def forward(level, r, first=False):
        x = stencil(
            field[level], from_above[pl.ds(level, 1), :], from_below[pl.ds(level, 1), :], made
        )
        if first:
            x = x + force[...]
        r = x * gain[level] + ratio[level] * r
        out[level] = r
        return r

    r = forward(0, jnp.zeros((height, width), jnp.float32), first=True)
    r = lax.fori_loop(1, levels, forward, r, unroll=2)

    def backward(i, x):
        level = levels - 2 - i
        x = out[level] - upper[level] * x
        out[level] = x
        return x

    lax.fori_loop(0, levels - 1, backward, r, unroll=2)


def f32(*shape):
    return jax.ShapeDtypeStruct(shape, jnp.float32)


def local(
    state, vert_coef, horiz_coef, wet_mask, coupling, surface_in, remap_w, dest_tile, dest_block, dest_group
):
    levels, height, width = state.shape
    groups, tiles = lax.axis_size("grp"), lax.axis_size("tile")
    cols = width // 128
    blocks = height * cols
    slots = max(8, 2 * blocks * K // tiles)
    extra = -(-(tiles * slots // 128) // 8) * 8
    around = -(-(levels + 1) // 8) * 8
    devices = groups * tiles
    start = (groups - 1) * tiles
    pairs = [(i, i + 1) for i in range(devices - 1) if i + 1 != start]
    back = [(j, i) for i, j in pairs]
    axes = ("grp", "tile")

    top, bottom = pl.pallas_call(
        edge_kernel,
        out_shape=(f32(around, width), f32(around, width)),
        compiler_params=params(16),
    )(state, wet_mask)
    from_above = lax.ppermute(bottom, axes, pairs)
    from_below = lax.ppermute(top, axes, back)

    packed = pl.pallas_call(
        functools.partial(pack_kernel, tiles, slots),
        grid=(1,),
        out_shape=f32(tiles, F * slots + extra, 128),
        in_specs=[pl.BlockSpec((1, height, width), lambda i: (0, 0, 0))]
        + [VM] * 6
        + [pl.BlockSpec(memory_space=pl.ANY)],
        out_specs=VM,
        scratch_shapes=[
            pltpu.VMEM((cols, height, K, 128, 128), jnp.bfloat16),
            pltpu.VMEM((blocks * K, F * 128), jnp.float32),
            pltpu.SemaphoreType.DMA((cols,)),
        ],
        compiler_params=params(16),
    )(
        state,
        coupling,
        surface_in,
        wet_mask,
        dest_tile,
        dest_block,
        dest_group,
        remap_w.reshape(height, cols, K, 128, 128),
    )
    got = lax.all_to_all(packed, "tile", split_axis=0, concat_axis=0, tiled=True)

    full = f32(levels, height, width)
    upper, gain, ratio, base, impulse, weights = pl.pallas_call(
        functools.partial(base_kernel, tiles, groups),
        out_shape=(full, full, full, full, full, f32(4, height, width)),
        compiler_params=params(24),
        cost_estimate=pl.CostEstimate(flops=40 * state.size, bytes_accessed=28 * state.size, transcendentals=0),
    )(state, vert_coef, horiz_coef, wet_mask, from_above, from_below)

    merged = pl.pallas_call(
        functools.partial(merge_kernel, tiles, slots, blocks, groups),
        out_shape=(f32(F * blocks, 128),) * (groups - 1),
        compiler_params=params(8),
    )(got)
    arrived = [
        lax.ppermute(merged[g], "grp", [(g, groups - 1), (groups - 1, g)])
        for g in range(groups - 1)
    ]
    field, received, force, top, bottom = pl.pallas_call(
        functools.partial(force_kernel, cols),
        out_shape=(full, f32(F, height, width), f32(height, width), f32(levels, width), f32(levels, width)),
        compiler_params=params(16),
    )(base, impulse, wet_mask, *arrived)
    from_above = lax.ppermute(bottom, axes, pairs)
    from_below = lax.ppermute(top, axes, back)
    out = pl.pallas_call(
        last_kernel,
        out_shape=full,
        compiler_params=params(24),
    )(field, force, from_above, from_below, upper, gain, ratio, weights)
    return out, received


def solution(mesh):
    in_specs = (
        P(None, ("grp", "tile"), None),
        P(None, ("grp", "tile"), None),
        P(("grp", "tile"), None),
        P("tile", None),
        P(None, ("grp", "tile"), None),
        P(None, ("grp", "tile"), None),
        P(("grp", "tile"), None, None, None),
        P(("grp", "tile"), None),
        P(("grp", "tile"), None),
        P(("grp", "tile"), None),
    )
    out_specs = (P(None, ("grp", "tile"), None), P(None, ("grp", "tile"), None))
    return jax.shard_map(local, mesh=mesh, in_specs=in_specs, out_specs=out_specs, check_vma=False)
```

time: 121 us -> 64.9 us (0.54)
  the two profiles are of different devices: /device:TPU:4 before, /device:TPU:27 now
where the time goes in v1:
time: 64.9 us; the launch traced here: 64.3 us
  starting transfers between devices  25.2 us (39%)
  waiting for transfers between devices  18.1 us (28%)
  Pallas kernels  12 us (18%)
  local copies, waits for them, and re-layouts  8.12 us (13%)
  between operations  0.8 us (1%)
    ppermute x2, starting transfers between devices, local(): from_above = lax.ppermute(bottom, axes, pairs)  11.6 us
    all_to_all x1, waiting for transfers between devices, local(): lax.all_to_all(packed, 'tile', split_axis=0, concat_axis=0, tiled=True)  10.2 us
    unnamed x21, local copies, waits for them, and re-layouts  8.12 us
    ppermute x2, waiting for transfers between devices, local(): from_below = lax.ppermute(top, axes, back)  7.95 us
    all_to_all x1, starting transfers between devices, local(): lax.all_to_all(packed, 'tile', split_axis=0, concat_axis=0, tiled=True)  5.42 us
    ppermute x3, starting transfers between devices, local(): lax.ppermute(merged[g], 'grp', [(g, groups - 1), (groups - 1, g)])  4.34 us
    pallas_call x1, Pallas kernels, local(): pl.pallas_call(last_kernel, out_shape=full, compiler_params=params(24))  4.29 us
    ppermute x2, starting transfers between devices, local(): from_below = lax.ppermute(top, axes, back)  3.84 us
  transfers between devices with their start and end apart: 8, of which 2 were waited for; matrix products, arithmetic and copies ran while one was open for 0% of the time, Pallas kernels for 6%

profile of v1, /device:TPU:27, one launch (start us, length us, event | category | flops | bytes accessed | tf_op | source)
XLA Modules:
  0.0 64.3 jit_solution(12862800763829113925)
XLA Ops:
  0.6 0.0 copy-start.5
  0.6 0.8 %copy.12.dtile = s32[32,4]{1,0:T(8,128)S(1)} copy(s32[32,4]{0,1:T(4,128)} %param.17) | data formatting | bytes 1024 | tf_op args[7]
  1.4 0.8 %copy.13.dblock = s32[32,4]{1,0:T(8,128)S(1)} copy(s32[32,4]{0,1:T(4,128)} %param.18) | data formatting | bytes 1024 | tf_op args[8]
  2.2 0.8 %copy.14.dgroup = s32[32,4]{1,0:T(8,128)S(1)} copy(s32[32,4]{0,1:T(4,128)} %param.19) | data formatting | bytes 1024 | tf_op args[9]
  2.9 1.2 %copy-done = f32[64,8,512]{2,1,0:T(8,128)S(1)} copy-done((f32[64,8,512]{2,1,0:T(8,128)S(1)}, f32[64,8,512]{2,1,0:T(8,128)}, u32[]{:S(2)}) %copy-start) | copy-done | bytes 1048600
  4.2 2.2 %copy-done.2 = bf16[32,4,128,128]{3,2,1,0:T(8,128)(2,1)S(1)} copy-done((bf16[32,4,128,128]{3,2,1,0:T(8,128)(2,1)S(1)}, bf16[32,4,128,128]{3,2,1,0:T(8,128)(2,1)}, u32[]{:S(2)}) %copy-start.2) | copy-done | bytes 4194328
  6.3 0.7 %copy-done.4 = s32[8,512]{1,0:T(8,128)S(1)} copy-done((s32[8,512]{1,0:T(8,128)S(1)}, s32[8,512]{1,0:T(8,128)}, u32[]{:S(2)}) %copy-start.4) | copy-done | bytes 16408
  7.1 0.8 %copy-done.6 = f32[4,8,512]{2,1,0:T(8,128)S(1)} copy-done((f32[4,8,512]{2,1,0:T(8,128)S(1)}, f32[4,8,512]{2,1,0:T(8,128)}, u32[]{:S(2)}) %copy-start.6) | copy-done | bytes 65560
  7.9 0.8 %copy-done.7 = f32[4,8,512]{2,1,0:T(8,128)S(1)} copy-done((f32[4,8,512]{2,1,0:T(8,128)S(1)}, f32[4,8,512]{2,1,0:T(8,128)}, u32[]{:S(2)}) %copy-start.7) | copy-done | bytes 65560
  8.8 2.9 %shard_map.115 = f32[8,136,128]{2,1,0:T(8,128)} custom-call(f32[64,8,512]{2,1,0:T(8,128)S(1)} %copy-done, f32[4,8,512]{2,1,0:T(8,128)S(1)} %copy-done.6, f32[4,8,512]{2,1,0:T(8,128)S(1)} %copy-done.7, s32[8,512]{1,0:T(8,128)S(1)} %copy-done.4, s32[32,4]{1,0:T(8,128)S(1)} %copy.12.dtile, s32[32,4]{1,0:T(8,128)S(1)} %copy.13.dblock, s32[32,4]{1,0:T(8,128)S(1)} %copy.14.dgroup, ...), custom_call_target="tpu_custom_call" | custom-call | tf_op jit(solution)/shard_map/pallas_call | solution.py:297
  11.7 5.4 %all-to-all-start = ((f32[8,136,128]{2,1,0:T(8,128)}), f32[8,136,128]{2,1,0:T(8,128)S(1)}, u32[]{:S(2)}, u32[]{:S(2)}) async-start(f32[8,136,128]{2,1,0:T(8,128)} %shard_map.115), calls=%async_computation | async-start | bytes 1114112 | tf_op jit(solution)/shard_map/all_to_all | solution.py:321
  17.1 0.1 shard_map.113
  17.2 2.8 %collective-permute-start = (f32[72,512]{1,0:T(8,128)S(1)}, f32[72,512]{1,0:T(8,128)S(1)}, u32[]{:S(2)}, u32[]{:S(2)}) collective-permute-start(f32[72,512]{1,0:T(8,128)S(1)} %get-tuple-element.18), channel_id=1, source_target_pairs={{0,1},{1,2},{2,3},{3,4},{4,5},{5,6},{6,7},{7,8},{8,9},{9,10},{10,1... | collective-permute-start | bytes 442376 | tf_op jit(solution)/shard_map/ppermute | solution.py:294
  20.0 1.9 %collective-permute-start.1 = (f32[72,512]{1,0:T(8,128)S(1)}, f32[72,512]{1,0:T(8,128)S(1)}, u32[]{:S(2)}, u32[]{:S(2)}) collective-permute-start(f32[72,512]{1,0:T(8,128)S(1)} %get-tuple-element.19), channel_id=1, source_target_pairs={{1,0},{2,1},{3,2},{4,3},{5,4},{6,5},{7,6},{8,7},{9,8},{10,9},{11,1... | collective-permute-start | bytes 442376 | tf_op jit(solution)/shard_map/ppermute | solution.py:295
  21.9 10.2 %all-to-all-done.got = f32[8,136,128]{2,1,0:T(8,128)S(1)} async-done(((f32[8,136,128]{2,1,0:T(8,128)}), f32[8,136,128]{2,1,0:T(8,128)S(1)}, u32[]{:S(2)}, u32[]{:S(2)}) %all-to-all-start) | async-done | bytes 557088 | tf_op jit(solution)/shard_map/all_to_all | solution.py:321
  32.1 0.3 shard_map.116
  32.4 0.7 %collective-permute-start.2 = (f32[128,128]{1,0:T(8,128)S(1)}, f32[128,128]{1,0:T(8,128)S(1)}, u32[]{:S(2)}, u32[]{:S(2)}) collective-permute-start(f32[128,128]{1,0:T(8,128)S(1)} %get-tuple-element.22), channel_id=1, source_target_pairs={{0,24},{24,0},{1,25},{25,1},{2,26},{26,2},{3,27},{27,3},{4,28},{28... | collective-permute-start | bytes 196616 | tf_op jit(solution)/shard_map/ppermute | solution.py:337
  33.0 3.0 %collective-permute-start.3 = (f32[128,128]{1,0:T(8,128)S(1)}, f32[128,128]{1,0:T(8,128)S(1)}, u32[]{:S(2)}, u32[]{:S(2)}) collective-permute-start(f32[128,128]{1,0:T(8,128)S(1)} %get-tuple-element.23), channel_id=1, source_target_pairs={{8,24},{24,8},{9,25},{25,9},{10,26},{26,10},{11,27},{27,11},{12,28... | collective-permute-start | bytes 196616 | tf_op jit(solution)/shard_map/ppermute | solution.py:337
  36.1 0.7 %collective-permute-start.4 = (f32[128,128]{1,0:T(8,128)S(1)}, f32[128,128]{1,0:T(8,128)S(1)}, u32[]{:S(2)}, u32[]{:S(2)}) collective-permute-start(f32[128,128]{1,0:T(8,128)S(1)} %get-tuple-element.24), channel_id=1, source_target_pairs={{16,24},{24,16},{17,25},{25,17},{18,26},{26,18},{19,27},{27,19},{2... | collective-permute-start | bytes 196616 | tf_op jit(solution)/shard_map/ppermute | solution.py:337
  36.7 0.0 collective-permute-done.from_above
  36.7 0.0 collective-permute-done.1.from_below
  36.7 0.0 copy-done.3
  36.8 3.4 %shard_map.114 = (f32[64,8,512]{2,1,0:T(8,128)S(1)}, f32[64,8,512]{2,1,0:T(8,128)S(1)}, f32[64,8,512]{2,1,0:T(8,128)S(1)}, f32[64,8,512]{2,1,0:T(8,128)S(1)}, f3...) custom-call(f32[64,8,512]{2,1,0:T(8,128)S(1)} %copy-done.1, f32[63,8,512]{2,1,0:T(8,128)S(1)} %copy-done.3, ...), custom_call_target="tpu_custom_call" | custom-call | flops 10485760 | bytes 7340032 | tf_op jit(solution)/shard_map/pallas_call | solution.py:324
  40.2 0.0 collective-permute-done.2.r0
  40.2 0.0 collective-permute-done.3.r1
  40.2 0.0 collective-permute-done.4.r2
  40.2 1.1 %shard_map.117 = (f32[64,8,512]{2,1,0:T(8,128)S(1)}, f32[4,8,512]{2,1,0:T(8,128)}, f32[8,512]{1,0:T(8,128)S(1)}, f32[64,512]{1,0:T(8,128)S(1)}, f32[64,512]{1,0:T(8,128)S(1)}) custom-call(f32[64,8,512]{2,1,0:T(8,128)S(1)} %get-tuple-element.20.base, f32[64,8,512]{2,1,0:T(8,128)S(1)} %get-tuple-element.21.impulse, s32[8,512]{1,0:T(8,128)S(1)} %copy-done.5, ...), custom_call_target="tpu_custom_call" | custom-call | tf_op jit(solution)/shard_map/pallas_call | solution.py:340
  41.3 8.8 %collective-permute-start.5 = (f32[64,512]{1,0:T(8,128)S(1)}, f32[64,512]{1,0:T(8,128)S(1)}, u32[]{:S(2)}, u32[]{:S(2)}) collective-permute-start(f32[64,512]{1,0:T(8,128)S(1)} %get-tuple-element.27), channel_id=1, source_target_pairs={{0,1},{1,2},{2,3},{3,4},{4,5},{5,6},{6,7},{7,8},{8,9},{9,10},{10,1... | collective-permute-start | bytes 393224 | tf_op jit(solution)/shard_map/ppermute | solution.py:345
  50.1 1.9 %collective-permute-start.6 = (f32[64,512]{1,0:T(8,128)S(1)}, f32[64,512]{1,0:T(8,128)S(1)}, u32[]{:S(2)}, u32[]{:S(2)}) collective-permute-start(f32[64,512]{1,0:T(8,128)S(1)} %get-tuple-element.28), channel_id=1, source_target_pairs={{1,0},{2,1},{3,2},{4,3},{5,4},{6,5},{7,6},{8,7},{9,8},{10,9},{11,1... | collective-permute-start | bytes 393224 | tf_op jit(solution)/shard_map/ppermute | solution.py:346
  52.0 0.0 collective-permute-done.5.from_above
  52.0 7.9 %collective-permute-done.6.from_below = f32[64,512]{1,0:T(8,128)S(1)} collective-permute-done((f32[64,512]{1,0:T(8,128)S(1)}, f32[64,512]{1,0:T(8,128)S(1)}, u32[]{:S(2)}, u32[]{:S(2)}) %collective-permute-start.6) | collective-permute-done | bytes 131104 | tf_op jit(solution)/shard_map/ppermute | solution.py:346
  60.0 4.3 %shard_map.118 = f32[64,8,512]{2,1,0:T(8,128)} custom-call(f32[64,8,512]{2,1,0:T(8,128)S(1)} %get-tuple-element.25.field, f32[8,512]{1,0:T(8,128)S(1)} %get-tuple-element.26.force, f32[64,512]{1,0:T(8,128)S(1)} %collective-permute-done.5.from_above, f32[64,512]{1,0:T(8,128)S(1)} %collective-permute-done.6.from_below, ...), custom_call_target="tpu_custom_call" | custom-call | tf_op jit(solution)/shard_map/pallas_call | solution.py:347
  (11 shorter events, 0.0 us)
Async XLA Ops:
  0.6 16.5 %copy-start.5 = (s32[8,512]{1,0:T(8,128)S(1)}, s32[8,512]{1,0:T(8,128)}, u32[]{:S(2)}) copy-start(s32[8,512]{1,0:T(8,128)} %mask.7) | copy-start | bytes 49156
  2.9 1.2 %copy-start = (f32[64,8,512]{2,1,0:T(8,128)S(1)}, f32[64,8,512]{2,1,0:T(8,128)}, u32[]{:S(2)}) copy-start(f32[64,8,512]{2,1,0:T(8,128)} %state.5) | copy-start | bytes 3145732
  4.2 2.2 %copy-start.2 = (bf16[32,4,128,128]{3,2,1,0:T(8,128)(2,1)S(1)}, bf16[32,4,128,128]{3,2,1,0:T(8,128)(2,1)}, u32[]{:S(2)}) copy-start(bf16[32,4,128,128]{3,2,1,0:T(8,128)(2,1)} %param.16) | copy-start | bytes 12582916
  6.3 0.7 %copy-start.4 = (s32[8,512]{1,0:T(8,128)S(1)}, s32[8,512]{1,0:T(8,128)}, u32[]{:S(2)}) copy-start(s32[8,512]{1,0:T(8,128)} %mask.7) | copy-start | bytes 49156
  7.1 0.8 %copy-start.6 = (f32[4,8,512]{2,1,0:T(8,128)S(1)}, f32[4,8,512]{2,1,0:T(8,128)}, u32[]{:S(2)}) copy-start(f32[4,8,512]{2,1,0:T(8,128)} %coupling.1) | copy-start | bytes 196612
  7.9 0.8 %copy-start.7 = (f32[4,8,512]{2,1,0:T(8,128)S(1)}, f32[4,8,512]{2,1,0:T(8,128)}, u32[]{:S(2)}) copy-start(f32[4,8,512]{2,1,0:T(8,128)} %surface.1) | copy-start | bytes 196612
  8.7 8.4 %copy-start.1 = (f32[64,8,512]{2,1,0:T(8,128)S(1)}, f32[64,8,512]{2,1,0:T(8,128)}, u32[]{:S(2)}) copy-start(f32[64,8,512]{2,1,0:T(8,128)} %state.5) | copy-start | bytes 3145732
  8.7 28.0 %copy-start.3 = (f32[63,8,512]{2,1,0:T(8,128)S(1)}, f32[63,8,512]{2,1,0:T(8,128)}, u32[]{:S(2)}) copy-start(f32[63,8,512]{2,1,0:T(8,128)} %vert.1) | copy-start | bytes 3096580
  8.8 28.0 %copy-start.8 = (f32[8,512]{1,0:T(8,128)S(1)}, f32[8,512]{1,0:T(8,128)}, u32[]{:S(2)}) copy-start(f32[8,512]{1,0:T(8,128)} %horiz.1) | copy-start | bytes 49156
  11.7 20.4 %all-to-all-start = ((f32[8,136,128]{2,1,0:T(8,128)}), f32[8,136,128]{2,1,0:T(8,128)S(1)}, u32[]{:S(2)}, u32[]{:S(2)}) async-start(f32[8,136,128]{2,1,0:T(8,128)} %shard_map.115), calls=%async_computation | async-start | bytes 1114112 | tf_op jit(solution)/shard_map/all_to_all | solution.py:321
  17.2 19.6 %collective-permute-start = (f32[72,512]{1,0:T(8,128)S(1)}, f32[72,512]{1,0:T(8,128)S(1)}, u32[]{:S(2)}, u32[]{:S(2)}) collective-permute-start(f32[72,512]{1,0:T(8,128)S(1)} %get-tuple-element.18), channel_id=1, source_target_pairs={{0,1},{1,2},{2,3},{3,4},{4,5},{5,6},{6,7},{7,8},{8,9},{9,10},{10,1... | collective-permute-start | bytes 442376 | tf_op jit(solution)/shard_map/ppermute | solution.py:294
  20.0 16.7 %collective-permute-start.1 = (f32[72,512]{1,0:T(8,128)S(1)}, f32[72,512]{1,0:T(8,128)S(1)}, u32[]{:S(2)}, u32[]{:S(2)}) collective-permute-start(f32[72,512]{1,0:T(8,128)S(1)} %get-tuple-element.19), channel_id=1, source_target_pairs={{1,0},{2,1},{3,2},{4,3},{5,4},{6,5},{7,6},{8,7},{9,8},{10,9},{11,1... | collective-permute-start | bytes 442376 | tf_op jit(solution)/shard_map/ppermute | solution.py:295
  32.4 7.8 %collective-permute-start.2 = (f32[128,128]{1,0:T(8,128)S(1)}, f32[128,128]{1,0:T(8,128)S(1)}, u32[]{:S(2)}, u32[]{:S(2)}) collective-permute-start(f32[128,128]{1,0:T(8,128)S(1)} %get-tuple-element.22), channel_id=1, source_target_pairs={{0,24},{24,0},{1,25},{25,1},{2,26},{26,2},{3,27},{27,3},{4,28},{28... | collective-permute-start | bytes 196616 | tf_op jit(solution)/shard_map/ppermute | solution.py:337
  33.0 7.1 %collective-permute-start.3 = (f32[128,128]{1,0:T(8,128)S(1)}, f32[128,128]{1,0:T(8,128)S(1)}, u32[]{:S(2)}, u32[]{:S(2)}) collective-permute-start(f32[128,128]{1,0:T(8,128)S(1)} %get-tuple-element.23), channel_id=1, source_target_pairs={{8,24},{24,8},{9,25},{25,9},{10,26},{26,10},{11,27},{27,11},{12,28... | collective-permute-start | bytes 196616 | tf_op jit(solution)/shard_map/ppermute | solution.py:337
  36.1 4.1 %collective-permute-start.4 = (f32[128,128]{1,0:T(8,128)S(1)}, f32[128,128]{1,0:T(8,128)S(1)}, u32[]{:S(2)}, u32[]{:S(2)}) collective-permute-start(f32[128,128]{1,0:T(8,128)S(1)} %get-tuple-element.24), channel_id=1, source_target_pairs={{16,24},{24,16},{17,25},{25,17},{18,26},{26,18},{19,27},{27,19},{2... | collective-permute-start | bytes 196616 | tf_op jit(solution)/shard_map/ppermute | solution.py:337
  41.3 10.7 %collective-permute-start.5 = (f32[64,512]{1,0:T(8,128)S(1)}, f32[64,512]{1,0:T(8,128)S(1)}, u32[]{:S(2)}, u32[]{:S(2)}) collective-permute-start(f32[64,512]{1,0:T(8,128)S(1)} %get-tuple-element.27), channel_id=1, source_target_pairs={{0,1},{1,2},{2,3},{3,4},{4,5},{5,6},{6,7},{7,8},{8,9},{9,10},{10,1... | collective-permute-start | bytes 393224 | tf_op jit(solution)/shard_map/ppermute | solution.py:345
  50.1 9.9 %collective-permute-start.6 = (f32[64,512]{1,0:T(8,128)S(1)}, f32[64,512]{1,0:T(8,128)S(1)}, u32[]{:S(2)}, u32[]{:S(2)}) collective-permute-start(f32[64,512]{1,0:T(8,128)S(1)} %get-tuple-element.28), channel_id=1, source_target_pairs={{1,0},{2,1},{3,2},{4,3},{5,4},{6,5},{7,6},{8,7},{9,8},{10,9},{11,1... | collective-permute-start | bytes 393224 | tf_op jit(solution)/shard_map/ppermute | solution.py:346

commit v2 on v1

v2 whole, which is shorter than its diff:
```python
import functools

import jax
import jax.numpy as jnp
from jax import lax
from jax.experimental import pallas as pl
from jax.experimental.pallas import tpu as pltpu
from jax.sharding import PartitionSpec as P

F = 4
K = 4
FORCING_GAIN = 0.25
VM = pl.BlockSpec(memory_space=pltpu.VMEM)
HBM = pl.BlockSpec(memory_space=pltpu.HBM)
MIB = 1024 * 1024


def params(mib):
    return pltpu.CompilerParams(vmem_limit_bytes=mib * MIB)


def split(x):
    hi = x.astype(jnp.bfloat16)
    return hi, (x - hi.astype(jnp.float32)).astype(jnp.bfloat16)


def wet_of(ocean, mask):
    return jnp.where(ocean, mask.astype(jnp.float32), 1.0)


def iota(shape, dim):
    return lax.broadcasted_iota(jnp.int32, shape, dim)


def pack_kernel(
    tiles, slots, groups, state, coupling, surface, mask, dtile, dblock, dgroup, w_hbm, *rest
):
    outs = rest[:tiles]
    w, terms, first, gain, other, sem, sems = rest[tiles:]
    height, width = mask.shape
    cols = width // 128
    blocks = height * cols
    count = blocks * K
    copies = [pltpu.make_async_copy(w_hbm.at[:, c], w.at[c], sem.at[c]) for c in range(cols)]
    small = [
        pltpu.make_async_copy(state.at[0], first, sems.at[0]),
        pltpu.make_async_copy(coupling, gain, sems.at[1]),
        pltpu.make_async_copy(surface, other, sems.at[2]),
    ]
    for copy in small + copies:
        copy.start()
    ocean = lax.axis_index("grp") == groups - 1
    me = lax.axis_index("tile")

    block = dblock[...]
    line = block // cols
    col = block % cols
    group = jnp.where(ocean, dgroup[...], groups - 1)
    code = dtile[...] * 128 + col * height + line + jnp.where(ocean, dgroup[...] * blocks, 0)
    device = group * tiles + dtile[...]
    low = jnp.where(ocean, 0, (groups - 1) * tiles)
    high = jnp.where(ocean, (groups - 1) * tiles, groups * tiles)
    beside = jnp.where(line == height - 1, device + 1, device - 1)
    side = jnp.where(line == height - 1, 0, 1)
    reads = ((line == height - 1) | (line == 0)) & (beside >= low) & (beside < high)
    edge = (beside % tiles) * 32 + side * cols + col
    edge = edge + jnp.where(ocean, (beside // tiles) * (2 * cols), 0)
    edge = jnp.where(reads, edge, -1)

    item = iota((count, blocks), 0)
    item_k = (item // height) % K
    own = iota((count, blocks), 1) == (item % height) * cols + item // (height * K)
    up, down = iota((count, count), 0), iota((count, count), 1)

    def column(values):
        spread = jnp.broadcast_to(values[:1, :], (count, blocks))
        for k in range(1, K):
            spread = jnp.where(item_k == k, values[k : k + 1, :], spread)
        return jnp.sum(jnp.where(own, spread, 0), 1, keepdims=True)

    def turned(values):
        return jnp.sum(jnp.where(up == down, values, 0), 0, keepdims=True)

    code_col, edge_row = column(code), turned(column(edge))
    code_row = turned(code_col)
    tile_row, tile_col, tag_col = code_row // 128, code_col // 128, code_col % 128
    same = tile_row == tile_col
    place_row = jnp.sum(jnp.where(same & (up < down), 1, 0), 0, keepdims=True)
    place_col = jnp.sum(jnp.where(same & (down < up), 1, 0), 1, keepdims=True)
    slot_row = (tile_row ^ me) * slots + place_row
    chooser = jnp.where(iota((tiles * slots, count), 0) == slot_row, 1.0, 0.0).astype(jnp.bfloat16)
    to_tile = jnp.where((iota((tiles, count), 0) ^ me) == tile_row, 1.0, 0.0).astype(jnp.bfloat16)
    labels = jnp.where(
        iota((count, tiles * slots), 1) == (tile_col ^ me) * slots + place_col,
        (tag_col + 1).astype(jnp.float32),
        0.0,
    ).astype(jnp.bfloat16)
    tags = jnp.dot(to_tile, labels, preferred_element_type=jnp.float32)
    rim = 2 * cols * (groups - 1)
    rim_id = iota((tiles * rim, count), 0)
    rim_tile, rim_id = (rim_id // rim) ^ me, rim_id % rim
    rim_id = rim_tile * 32 + jnp.where(ocean, rim_id, rim_id % (2 * cols))
    rim_chooser = jnp.where(rim_id == edge_row, 1.0, 0.0).astype(jnp.bfloat16)
    base = F * slots + rim
    parts = tiles * slots // 128
    for t in range(tiles):
        outs[t][base:, :] = jnp.zeros((outs[t].shape[0] - base, 128), jnp.float32)
        for part in range(parts):
            outs[t][base + part : base + part + 1, :] = tags[
                t : t + 1, part * 128 : (part + 1) * 128
            ]

    for copy in small:
        copy.wait()
    send = gain[...] * (first[...][None] - other[...]) * wet_of(ocean, mask[...])[None]
    row_of = iota((F * height, 128), 0) % height
    for c in range(cols):
        piece = send[:, :, c * 128 : (c + 1) * 128].reshape(F * height, 128)
        left = jnp.concatenate(
            [jnp.where(row_of == r, piece, 0.0).astype(jnp.bfloat16) for r in range(height)], 1
        )
        copies[c].wait()
        for k in range(K):
            right = w[c, :, k].reshape(height * 128, 128)
            made = jnp.dot(left, right, preferred_element_type=jnp.float32)
            at = (c * K + k) * height
            for f in range(F):
                terms[at : at + height, f * 128 : (f + 1) * 128] = made[
                    f * height : (f + 1) * height, :
                ]
    total = terms[:, :128]
    for f in range(1, F):
        total = total + terms[:, f * 128 : (f + 1) * 128]
    hi, lo = split(terms[...])
    packed = jnp.dot(
        jnp.concatenate([chooser, chooser], 1),
        jnp.concatenate([hi, lo], 0),
        preferred_element_type=jnp.float32,
    )
    hi, lo = split(total)
    rims = jnp.dot(
        jnp.concatenate([rim_chooser, rim_chooser], 1),
        jnp.concatenate([hi, lo], 0),
        preferred_element_type=jnp.float32,
    )
    for t in range(tiles):
        for f in range(F):
            outs[t][f * slots : (f + 1) * slots, :] = packed[
                t * slots : (t + 1) * slots, f * 128 : (f + 1) * 128
            ]
        outs[t][F * slots : base, :] = rims[t * rim : (t + 1) * rim, :]


def merge_kernel(tiles, slots, blocks, groups, _, *refs):
    got, outs = refs[:tiles], refs[tiles:]
    ocean = lax.axis_index("grp") == groups - 1
    rim = outs[0].shape[0] - F * blocks
    base = F * slots + rim * (groups - 1)
    tail = got[0][F * slots :, :]
    for t in range(1, tiles):
        tail = tail + got[t][F * slots :, :]
    tags = tail[base - F * slots :, :]
    rows = (groups - 1) * blocks
    total = tiles * slots
    label = jnp.concatenate([tags[p : p + 1, :] for p in range(total // 128)], 1).astype(jnp.int32)
    ids = iota((rows, total), 0)
    ids = jnp.where(ocean, ids, ids % blocks) + 1
    chooser = jnp.where(ids == label, 1.0, 0.0).astype(jnp.bfloat16)
    for f in range(F):
        data = jnp.concatenate([got[t][f * slots : (f + 1) * slots, :] for t in range(tiles)], 0)
        hi, lo = split(data)
        merged = jnp.dot(chooser, hi, preferred_element_type=jnp.float32) + jnp.dot(
            chooser, lo, preferred_element_type=jnp.float32
        )
        for g in range(groups - 1):
            outs[g][f * blocks : (f + 1) * blocks, :] = merged[g * blocks : (g + 1) * blocks, :]
    for g in range(groups - 1):
        outs[g][F * blocks :, :] = tail[g * rim : (g + 1) * rim, :]


def edge_kernel(groups, state_hbm, vert_hbm, horiz, mask, down, up, state, vert, sem):
    levels, height, width = state.shape
    half = levels // 2
    copies = [
        pltpu.make_async_copy(state_hbm, state, sem.at[0]),
        pltpu.make_async_copy(vert_hbm, vert, sem.at[1]),
    ]
    for copy in copies:
        copy.start()
    wet = wet_of(lax.axis_index("grp") == groups - 1, mask[...])
    cols = width // 128
    last = height - 1
    for c in range(cols):
        at = slice(c * 128, (c + 1) * 128)
        down[levels + half, c : c + 1, :] = wet[last:, at]
        down[levels + half, cols + c : cols + c + 1, :] = wet[last - 1 : last, at]
        up[levels + half, c : c + 1, :] = wet[1:2, at]
        up[levels + half, cols + c : cols + c + 1, :] = wet[:1, at]
        for out, row in ((down, last), (up, 0)):
            out[levels + half + 1, c : c + 1, :] = horiz[row : row + 1, at]
            out[levels + half + 1, cols + c : cols + c + 1, :] = horiz[row : row + 1, at]
    copies[0].wait()
    for c in range(cols):
        at = slice(c * 128, (c + 1) * 128)
        down[:levels, c, :] = state[:, last, at]
        down[:levels, cols + c, :] = state[:, last - 1, at]
        up[:levels, c, :] = state[:, 1, at]
        up[:levels, cols + c, :] = state[:, 0, at]
    copies[1].wait()
    for c in range(cols):
        at = slice(c * 128, (c + 1) * 128)
        for out, row in ((down, last), (up, 0)):
            out[levels : levels + half, c, :] = vert[:half, row, at]
            out[levels : levels + half - 1, cols + c, :] = vert[half:, row, at]
            out[levels + half - 1, cols + c : cols + c + 1, :] = jnp.zeros((1, 128), jnp.float32)


def weights_of(tiles, groups, horiz, wet, wet_above, wet_below):
    height, width = wet.shape
    device = lax.axis_index("grp") * tiles + lax.axis_index("tile")
    rows = device * height + iota((height, width), 0)
    start = (groups - 1) * tiles * height
    last = groups * tiles * height - 1
    above = jnp.concatenate([wet_above, wet[:-1]], 0)
    below = jnp.concatenate([wet[1:], wet_below], 0)
    above = jnp.where((rows > 0) & (rows != start), above, 0.0)
    below = jnp.where((rows < last) & (rows + 1 != start), below, 0.0)
    column = iota((height, width), 1)
    left = jnp.where(column == 0, 0.0, pltpu.roll(wet, 1, 1))
    right = jnp.where(column == width - 1, 0.0, pltpu.roll(wet, width - 1, 1))
    scale = horiz * wet
    return scale * left, scale * right, scale * above, scale * below


def line_of(halo, first, cols):
    return jnp.concatenate([halo[first + c : first + c + 1, :] for c in range(cols)], 1)


def stencil(field, halo, weights):
    left, right, above, below = weights
    height, width = field.shape
    cols = width // 128
    top, bottom = line_of(halo, 0, cols), line_of(halo, cols, cols)
    return (
        field
        + left * (pltpu.roll(field, 1, 1) - field)
        + right * (pltpu.roll(field, width - 1, 1) - field)
        + above * (jnp.concatenate([top, field[:-1]], 0) - field)
        + below * (jnp.concatenate([field[1:], bottom], 0) - field)
    )


def shifted(halo, lane):
    rows = halo.shape[0]
    to_right, to_left = pltpu.roll(halo, 1, 1), pltpu.roll(halo, 127, 1)
    return (
        jnp.where(lane == 0, pltpu.roll(to_right, 1, 0), to_right),
        jnp.where(lane == 127, pltpu.roll(to_left, rows - 1, 0), to_left),
    )


def base_kernel(
    tiles, groups, state, vert, horiz, mask, down, up, above, below,
    upper, gain, ratio, base, impulse, weights, halo_base, halo_impulse, halo_wet, halo_vert, halo_upper,
):
    levels, height, width = state.shape
    cols = width // 128
    half = levels // 2
    shape = (2 * cols, 128)
    low_half = iota(shape, 0) < cols
    lane = iota(shape, 1)

    def turn(x):
        return pltpu.roll(x, cols, 0)

    def beside(i):
        return jnp.where(low_half, above[i], below[i])

    def behind(i):
        return turn(jnp.where(low_half, below[i], above[i]))

    def inside(i):
        return turn(jnp.where(low_half, down[i], up[i]))

    wet = wet_of(lax.axis_index("grp") == groups - 1, mask[...])
    wet_halo = beside(levels + half)
    halo_wet[...] = wet_halo
    made = weights_of(
        tiles, groups, horiz[...], wet, line_of(wet_halo, 0, cols), line_of(wet_halo, cols, cols)
    )
    for i in range(4):
        weights[i] = made[i]
    scale = beside(levels + half + 1) * wet_halo
    wet_left, wet_right = shifted(wet_halo, lane)
    place = iota(shape, 0) % cols
    weight_left = scale * jnp.where((place == 0) & (lane == 0), 0.0, wet_left)
    weight_right = scale * jnp.where((place == cols - 1) & (lane == 127), 0.0, wet_right)
    weight_behind = scale * behind(levels + half)
    weight_inside = scale * inside(levels + half)

    def spread(i, _):
        a, b = above[levels + i], below[levels + i]
        halo_vert[i] = jnp.where(low_half, a, turn(b)) * wet_halo
        halo_vert[half + i] = jnp.where(low_half, turn(a), b) * wet_halo
        return 0

    lax.fori_loop(0, half, spread, 0, unroll=4)
    zero = jnp.zeros((height, width), jnp.float32)
    zero_halo = jnp.zeros(shape, jnp.float32)

    def forward(level, carry, last=False, first=False):
        low, c, r, e, low_h, c_h, r_h, e_h = carry
        upp = zero if last else vert[level] * wet
        inverse = 1.0 / (1.0 + low + upp + low * c)
        c = -upp * inverse
        step = low * inverse
        halo = beside(level)
        r = stencil(state[level], halo, made) * inverse + step * r
        e = inverse if first else step * e
        upper[level] = c
        gain[level] = inverse
        ratio[level] = step
        base[level] = r
        impulse[level] = e
        upp_h = zero_halo if last else halo_vert[level]
        inverse = 1.0 / (1.0 + low_h + upp_h + low_h * c_h)
        c_h = -upp_h * inverse
        step = low_h * inverse
        left, right = shifted(halo, lane)
        field = (
            halo
            + weight_left * (left - halo)
            + weight_right * (right - halo)
            + weight_behind * (behind(level) - halo)
            + weight_inside * (inside(level) - halo)
        )
        r_h = field * inverse + step * r_h
        e_h = inverse if first else step * e_h
        halo_upper[level] = c_h
        halo_base[level] = r_h
        halo_impulse[level] = e_h
        return upp, c, r, e, upp_h, c_h, r_h, e_h

    carry = forward(0, (zero,) * 4 + (zero_halo,) * 4, first=True)
    carry = lax.fori_loop(1, levels - 1, forward, carry, unroll=2)
    carry = forward(levels - 1, carry, last=True)

    def backward(i, carry):
        level = levels - 2 - i
        c, c_h = upper[level], halo_upper[level]
        x = base[level] - c * carry[0]
        y = impulse[level] - c * carry[1]
        x_h = halo_base[level] - c_h * carry[2]
        y_h = halo_impulse[level] - c_h * carry[3]
        base[level] = x
        impulse[level] = y
        halo_base[level] = x_h
        halo_impulse[level] = y_h
        return x, y, x_h, y_h

    lax.fori_loop(0, levels - 1, backward, (carry[2], carry[3], carry[6], carry[7]), unroll=2)


def last_kernel(
    cols, groups, mask, base, impulse, upper, gain, ratio, weights, halo_base, halo_impulse, halo_wet, *refs
):
    arrived = refs[: groups - 1]
    out, received, field, sem = refs[groups - 1 :]
    levels, height, width = base.shape
    total = arrived[0][...]
    for other in arrived[1:]:
        total = total + other[...]
    for f in range(F):
        for c in range(cols):
            at = (f * cols + c) * height
            received[f, :, c * 128 : (c + 1) * 128] = total[at : at + height, :]
    wet = wet_of(lax.axis_index("grp") == groups - 1, mask[...])
    force = FORCING_GAIN * wet * jnp.sum(received[...], 0)
    force_halo = FORCING_GAIN * halo_wet[...] * total[F * cols * height :, :]
    made = tuple(weights[i] for i in range(4))

    def forward(level, r, first=False):
        halo = halo_base[level] + halo_impulse[level] * force_halo
        x = stencil(base[level] + impulse[level] * force, halo, made)
        if first:
            x = x + force
        r = x * gain[level] + ratio[level] * r
        field[level] = r
        return r

    r = forward(0, jnp.zeros((height, width), jnp.float32), first=True)
    x = lax.fori_loop(1, levels, forward, r, unroll=2)

    def backward(i, x):
        level = levels - 2 - i
        x = field[level] - upper[level] * x
        field[level] = x
        return x

    chunks = 4
    size = levels // chunks
    copies = []
    for i in range(chunks):
        x = lax.fori_loop(max(0, i * size - 1), (i + 1) * size - 1, backward, x, unroll=3 if i == 0 else 2)
        at = pl.ds(levels - (i + 1) * size, size)
        copies.append(pltpu.make_async_copy(field.at[at], out.at[at], sem.at[i]))
        copies[-1].start()
    for copy in copies:
        copy.wait()


def f32(*shape):
    return jax.ShapeDtypeStruct(shape, jnp.float32)


def local(
    state, vert_coef, horiz_coef, wet_mask, coupling, surface_in, remap_w, dest_tile, dest_block, dest_group
):
    levels, height, width = state.shape
    groups, tiles = lax.axis_size("grp"), lax.axis_size("tile")
    cols = width // 128
    blocks = height * cols
    slots = max(8, 2 * blocks * K // tiles)
    rim = 2 * cols
    tags = -(-(tiles * slots // 128) // 8) * 8
    devices = groups * tiles
    start = (groups - 1) * tiles
    pairs = [(i, i + 1) for i in range(devices - 1) if i + 1 != start]
    back = [(j, i) for i, j in pairs]
    axes = ("grp", "tile")

    edges = levels + levels // 2 + 2
    down, up = pl.pallas_call(
        functools.partial(edge_kernel, groups),
        out_shape=(f32(edges, rim, 128),) * 2,
        in_specs=[HBM, HBM, VM, VM],
        scratch_shapes=[
            pltpu.VMEM((levels, height, width), jnp.float32),
            pltpu.VMEM((levels - 1, height, width), jnp.float32),
            pltpu.SemaphoreType.DMA((2,)),
        ],
        compiler_params=params(8),
    )(state, vert_coef, horiz_coef, wet_mask)
    above = lax.ppermute(down, axes, pairs)
    below = lax.ppermute(up, axes, back)

    packed = pl.pallas_call(
        functools.partial(pack_kernel, tiles, slots, groups),
        out_shape=(f32(F * slots + rim * (groups - 1) + tags, 128),) * tiles,
        in_specs=[HBM] * 3 + [VM] * 4 + [HBM],
        scratch_shapes=[
            pltpu.VMEM((cols, height, K, 128, 128), jnp.bfloat16),
            pltpu.VMEM((blocks * K, F * 128), jnp.float32),
            pltpu.VMEM((height, width), jnp.float32),
            pltpu.VMEM((F, height, width), jnp.float32),
            pltpu.VMEM((F, height, width), jnp.float32),
            pltpu.SemaphoreType.DMA((cols,)),
            pltpu.SemaphoreType.DMA((3,)),
        ],
        compiler_params=params(12),
    )(
        state,
        coupling,
        surface_in,
        wet_mask,
        dest_tile.T,
        dest_block.T,
        dest_group.T,
        remap_w.reshape(height, cols, K, 128, 128),
    )
    got = [packed[0]] + [
        lax.ppermute(packed[k], "tile", [(i, i ^ k) for i in range(tiles)])
        for k in range(tiles - 1, 0, -1)
    ][::-1]

    full, halo = f32(levels, height, width), f32(levels, rim, 128)
    solved = pl.pallas_call(
        functools.partial(base_kernel, tiles, groups),
        out_shape=(full,) * 5 + (f32(4, height, width), halo, halo, f32(rim, 128)),
        scratch_shapes=[pltpu.VMEM((levels, rim, 128), jnp.float32)] * 2,
        compiler_params=params(16),
        cost_estimate=pl.CostEstimate(flops=60 * state.size, bytes_accessed=28 * state.size, transcendentals=0),
    )(state, vert_coef, horiz_coef, wet_mask, down, up, above, below)
    upper, gain, ratio, base, impulse, weights, halo_base, halo_impulse, halo_wet = solved

    merged = pl.pallas_call(
        functools.partial(merge_kernel, tiles, slots, blocks, groups),
        out_shape=(f32(F * blocks + rim, 128),) * (groups - 1),
        compiler_params=params(8),
    )(halo_wet, *got)
    arrived = [
        lax.ppermute(merged[g], "grp", [(g, groups - 1), (groups - 1, g)])
        for g in range(groups - 1)
    ]
    return pl.pallas_call(
        functools.partial(last_kernel, cols, groups),
        out_shape=(full, f32(F, height, width)),
        out_specs=(HBM, VM),
        scratch_shapes=[
            pltpu.VMEM((levels, height, width), jnp.float32),
            pltpu.SemaphoreType.DMA((4,)),
        ],
        compiler_params=params(16),
    )(
        wet_mask, base, impulse, upper, gain, ratio, weights, halo_base, halo_impulse, halo_wet, *arrived
    )


def solution(mesh):
    in_specs = (
        P(None, ("grp", "tile"), None),
        P(None, ("grp", "tile"), None),
        P(("grp", "tile"), None),
        P("tile", None),
        P(None, ("grp", "tile"), None),
        P(None, ("grp", "tile"), None),
        P(("grp", "tile"), None, None, None),
        P(("grp", "tile"), None),
        P(("grp", "tile"), None),
        P(("grp", "tile"), None),
    )
    out_specs = (P(None, ("grp", "tile"), None), P(None, ("grp", "tile"), None))
    return jax.shard_map(local, mesh=mesh, in_specs=in_specs, out_specs=out_specs, check_vma=False)
```

time: 64.9 us -> 59.8 us (0.921)
  the two profiles are of different devices: /device:TPU:27 before, /device:TPU:14 now
where the time goes in v2:
time: 59.8 us; the launch traced here: 59.1 us
  starting transfers between devices  21.9 us (37%)
  waiting for transfers between devices  12.4 us (21%)
  Pallas kernels  12.3 us (21%)
  local copies, waits for them, and re-layouts  11.7 us (20%)
  between operations  0.77 us (1%)
    unnamed x32, local copies, waits for them, and re-layouts  11.7 us
    ppermute x7, starting transfers between devices, local(): lax.ppermute(packed[k], 'tile', [(i, i ^ k) for i in range(tiles)])  8.58 us
    ppermute x3, starting transfers between devices, local(): lax.ppermute(merged[g], 'grp', [(g, groups - 1), (groups - 1, g)])  7.8 us
    ppermute x7, waiting for transfers between devices, local(): lax.ppermute(packed[k], 'tile', [(i, i ^ k) for i in range(tiles)])  7.2 us
    ppermute x3, waiting for transfers between devices, local(): lax.ppermute(merged[g], 'grp', [(g, groups - 1), (groups - 1, g)])  5.17 us
    pallas_call x1, Pallas kernels, local(): pl.pallas_call(functools.partial(last_kernel, cols, groups), out_shape=(f...  4.85 us
    pallas_call x1, Pallas kernels, local(): pl.pallas_call(functools.partial(base_kernel, tiles, groups), out_shape=(...  3.79 us
    ppermute x1, starting transfers between devices, local(): below = lax.ppermute(up, axes, back)  3.64 us
  transfers between devices with their start and end apart: 12, of which 7 were waited for; matrix products, arithmetic and copies ran while one was open for 0% of the time, Pallas kernels for 10%

profile of v2, /device:TPU:14, one launch (start us, length us, event | category | flops | bytes accessed | tf_op | source)
XLA Modules:
  0.0 59.1 jit_solution(10477625353308112652)
XLA Ops:
  0.6 1.2 %copy-done = f32[64,8,512]{2,1,0:T(8,128)S(1)} copy-done((f32[64,8,512]{2,1,0:T(8,128)S(1)}, f32[64,8,512]{2,1,0:T(8,128)}, u32[]{:S(2)}) %copy-start) | copy-done | bytes 1048600
  1.9 1.2 %copy-done.4 = f32[63,8,512]{2,1,0:T(8,128)S(1)} copy-done((f32[63,8,512]{2,1,0:T(8,128)S(1)}, f32[63,8,512]{2,1,0:T(8,128)}, u32[]{:S(2)}) %copy-start.4) | copy-done | bytes 1032216
  3.1 0.7 %copy-done.6 = s32[8,512]{1,0:T(8,128)S(1)} copy-done((s32[8,512]{1,0:T(8,128)S(1)}, s32[8,512]{1,0:T(8,128)}, u32[]{:S(2)}) %copy-start.6) | copy-done | bytes 16408
  3.8 0.7 %copy-done.11 = f32[8,512]{1,0:T(8,128)S(1)} copy-done((f32[8,512]{1,0:T(8,128)S(1)}, f32[8,512]{1,0:T(8,128)}, u32[]{:S(2)}) %copy-start.11) | copy-done | bytes 16408
  4.5 1.0 %shard_map.113 = (f32[98,8,128]{2,1,0:T(8,128)S(1)}, f32[98,8,128]{2,1,0:T(8,128)S(1)}) custom-call(f32[64,8,512]{2,1,0:T(8,128)S(1)} %copy-done, f32[63,8,512]{2,1,0:T(8,128)S(1)} %copy-done.4, f32[8,512]{1,0:T(8,128)S(1)} %copy-done.11, s32[8,512]{1,0:T(8,128)S(1)} %copy-done.6), custom_call_target="tpu_custom_call" | custom-call | tf_op jit(solution)/shard_map/pallas_call | solution.py:433
  5.6 1.9 %collective-permute-start = (f32[98,8,128]{2,1,0:T(8,128)S(1)}, f32[98,8,128]{2,1,0:T(8,128)S(1)}, u32[]{:S(2)}, u32[]{:S(2)}) collective-permute-start(f32[98,8,128]{2,1,0:T(8,128)S(1)} %get-tuple-element.24.down), channel_id=1, source_target_pairs={{0,1},{1,2},{2,3},{3,4},{4,5},{5,6},{6,7},{7,8},{8,9},{9,10},{10,1... | collective-permute-start | bytes 1204232 | tf_op jit(solution)/shard_map/ppermute | solution.py:444
  7.5 3.6 %collective-permute-start.1 = (f32[98,8,128]{2,1,0:T(8,128)S(1)}, f32[98,8,128]{2,1,0:T(8,128)S(1)}, u32[]{:S(2)}, u32[]{:S(2)}) collective-permute-start(f32[98,8,128]{2,1,0:T(8,128)S(1)} %get-tuple-element.25.up), channel_id=1, source_target_pairs={{1,0},{2,1},{3,2},{4,3},{5,4},{6,5},{7,6},{8,7},{9,8},{10,9},{11,1... | collective-permute-start | bytes 1204232 | tf_op jit(solution)/shard_map/ppermute | solution.py:445
  11.2 1.2 %copy-done.1 = f32[64,8,512]{2,1,0:T(8,128)S(1)} copy-done((f32[64,8,512]{2,1,0:T(8,128)S(1)}, f32[64,8,512]{2,1,0:T(8,128)}, u32[]{:S(2)}) %copy-start.1) | copy-done | bytes 1048600
  12.4 2.2 %copy-done.3 = bf16[32,4,128,128]{3,2,1,0:T(8,128)(2,1)S(1)} copy-done((bf16[32,4,128,128]{3,2,1,0:T(8,128)(2,1)S(1)}, bf16[32,4,128,128]{3,2,1,0:T(8,128)(2,1)}, u32[]{:S(2)}) %copy-start.3) | copy-done | bytes 4194328
  14.6 0.7 %copy-done.7 = s32[8,512]{1,0:T(8,128)S(1)} copy-done((s32[8,512]{1,0:T(8,128)S(1)}, s32[8,512]{1,0:T(8,128)}, u32[]{:S(2)}) %copy-start.7) | copy-done | bytes 16408
  15.3 0.8 %copy-done.9 = f32[4,8,512]{2,1,0:T(8,128)S(1)} copy-done((f32[4,8,512]{2,1,0:T(8,128)S(1)}, f32[4,8,512]{2,1,0:T(8,128)}, u32[]{:S(2)}) %copy-start.9) | copy-done | bytes 65560
  16.1 0.8 %copy-done.10 = f32[4,8,512]{2,1,0:T(8,128)S(1)} copy-done((f32[4,8,512]{2,1,0:T(8,128)S(1)}, f32[4,8,512]{2,1,0:T(8,128)}, u32[]{:S(2)}) %copy-start.10) | copy-done | bytes 65560
  17.0 0.7 %copy-done.13 = s32[32,4]{0,1:T(4,128)S(1)} copy-done((s32[32,4]{0,1:T(4,128)S(1)}, s32[32,4]{0,1:T(4,128)}, u32[]{:S(2)}) %copy-start.13) | copy-done | bytes 536
  17.6 0.7 %copy-done.14 = s32[32,4]{0,1:T(4,128)S(1)} copy-done((s32[32,4]{0,1:T(4,128)S(1)}, s32[32,4]{0,1:T(4,128)}, u32[]{:S(2)}) %copy-start.14) | copy-done | bytes 536
  18.3 0.7 %copy-done.15 = s32[32,4]{0,1:T(4,128)S(1)} copy-done((s32[32,4]{0,1:T(4,128)S(1)}, s32[32,4]{0,1:T(4,128)}, u32[]{:S(2)}) %copy-start.15) | copy-done | bytes 536
  19.0 2.3 %shard_map.115 = (f32[160,128]{1,0:T(8,128)S(1)}, f32[160,128]{1,0:T(8,128)S(1)}, f32[160,128]{1,0:T(8,128)S(1)}, f32[160,128]{1,0:T(8,128)S(1)}, f32[160,128]{1...) custom-call(f32[64,8,512]{2,1,0:T(8,128)S(1)} %copy-done.1, ...), custom_call_target="tpu_custom_call" | custom-call | tf_op jit(solution)/shard_map/pallas_call | solution.py:447
  21.8 1.5 %collective-permute-start.4 = (f32[160,128]{1,0:T(8,128)S(1)}, f32[160,128]{1,0:T(8,128)S(1)}, u32[]{:S(2)}, u32[]{:S(2)}) collective-permute-start(f32[160,128]{1,0:T(8,128)S(1)} %get-tuple-element.38), channel_id=1, source_target_pairs={{0,3},{1,2},{2,1},{3,0},{4,7},{5,6},{6,5},{7,4},{8,11},{9,10},{10,... | collective-permute-start | bytes 245768 | tf_op jit(solution)/shard_map/ppermute | solution.py:472
  23.3 2.6 %collective-permute-start.5 = (f32[160,128]{1,0:T(8,128)S(1)}, f32[160,128]{1,0:T(8,128)S(1)}, u32[]{:S(2)}, u32[]{:S(2)}) collective-permute-start(f32[160,128]{1,0:T(8,128)S(1)} %get-tuple-element.39), channel_id=1, source_target_pairs={{0,4},{1,5},{2,6},{3,7},{4,0},{5,1},{6,2},{7,3},{8,12},{9,13},{10,... | collective-permute-start | bytes 245768 | tf_op jit(solution)/shard_map/ppermute | solution.py:472
  25.9 0.9 %collective-permute-done.3.refs_2_ = f32[160,128]{1,0:T(8,128)S(1)} collective-permute-done((f32[160,128]{1,0:T(8,128)S(1)}, f32[160,128]{1,0:T(8,128)S(1)}, u32[]{:S(2)}, u32[]{:S(2)}) %collective-permute-start.3) | collective-permute-done | bytes 81952 | tf_op jit(solution)/shard_map/ppermute | solution.py:472
  26.7 1.4 %collective-permute-start.6 = (f32[160,128]{1,0:T(8,128)S(1)}, f32[160,128]{1,0:T(8,128)S(1)}, u32[]{:S(2)}, u32[]{:S(2)}) collective-permute-start(f32[160,128]{1,0:T(8,128)S(1)} %get-tuple-element.40), channel_id=1, source_target_pairs={{0,5},{1,4},{2,7},{3,6},{4,1},{5,0},{6,3},{7,2},{8,13},{9,12},{10,... | collective-permute-start | bytes 245768 | tf_op jit(solution)/shard_map/ppermute | solution.py:472
  28.2 2.6 %collective-permute-start.8 = (f32[160,128]{1,0:T(8,128)S(1)}, f32[160,128]{1,0:T(8,128)S(1)}, u32[]{:S(2)}, u32[]{:S(2)}) collective-permute-start(f32[160,128]{1,0:T(8,128)S(1)} %get-tuple-element.42), channel_id=1, source_target_pairs={{0,7},{1,6},{2,5},{3,4},{4,3},{5,2},{6,1},{7,0},{8,15},{9,14},{10,... | collective-permute-start | bytes 245768 | tf_op jit(solution)/shard_map/ppermute | solution.py:472
  30.8 3.8 %shard_map.114 = (f32[64,8,512]{2,1,0:T(8,128)S(1)}, f32[64,8,512]{2,1,0:T(8,128)S(1)}, f32[64,8,512]{2,1,0:T(8,128)S(1)}, f32[64,8,512]{2,1,0:T(8,128)S(1)}, f3...) custom-call(f32[64,8,512]{2,1,0:T(8,128)S(1)} %copy-done.2, ...), custom_call_target="tpu_custom_call" | custom-call | flops 15728640 | bytes 7340032 | tf_op jit(solution)/shard_map/pallas_call | solution.py:477
  34.6 0.9 %collective-permute-done.5.refs_4_ = f32[160,128]{1,0:T(8,128)S(1)} collective-permute-done((f32[160,128]{1,0:T(8,128)S(1)}, f32[160,128]{1,0:T(8,128)S(1)}, u32[]{:S(2)}, u32[]{:S(2)}) %collective-permute-start.5) | collective-permute-done | bytes 81952 | tf_op jit(solution)/shard_map/ppermute | solution.py:472
  35.5 1.8 %collective-permute-done.6.refs_5_ = f32[160,128]{1,0:T(8,128)S(1)} collective-permute-done((f32[160,128]{1,0:T(8,128)S(1)}, f32[160,128]{1,0:T(8,128)S(1)}, u32[]{:S(2)}, u32[]{:S(2)}) %collective-permute-start.6) | collective-permute-done | bytes 81952 | tf_op jit(solution)/shard_map/ppermute | solution.py:472
  37.2 2.4 %collective-permute-done.7.refs_6_ = f32[160,128]{1,0:T(8,128)S(1)} collective-permute-done((f32[160,128]{1,0:T(8,128)S(1)}, f32[160,128]{1,0:T(8,128)S(1)}, u32[]{:S(2)}, u32[]{:S(2)}) %collective-permute-start.7) | collective-permute-done | bytes 81952 | tf_op jit(solution)/shard_map/ppermute | solution.py:472
  39.7 1.3 %collective-permute-done.8.refs_7_ = f32[160,128]{1,0:T(8,128)S(1)} collective-permute-done((f32[160,128]{1,0:T(8,128)S(1)}, f32[160,128]{1,0:T(8,128)S(1)}, u32[]{:S(2)}, u32[]{:S(2)}) %collective-permute-start.8) | collective-permute-done | bytes 81952 | tf_op jit(solution)/shard_map/ppermute | solution.py:472
  41.3 4.0 %collective-permute-start.10 = (f32[136,128]{1,0:T(8,128)S(1)}, f32[136,128]{1,0:T(8,128)S(1)}, u32[]{:S(2)}, u32[]{:S(2)}) collective-permute-start(f32[136,128]{1,0:T(8,128)S(1)} %get-tuple-element.44), channel_id=1, source_target_pairs={{8,24},{24,8},{9,25},{25,9},{10,26},{26,10},{11,27},{27,11},{12,28... | collective-permute-start | bytes 208904 | tf_op jit(solution)/shard_map/ppermute | solution.py:492
  45.2 1.9 %collective-permute-start.11 = (f32[136,128]{1,0:T(8,128)S(1)}, f32[136,128]{1,0:T(8,128)S(1)}, u32[]{:S(2)}, u32[]{:S(2)}) collective-permute-start(f32[136,128]{1,0:T(8,128)S(1)} %get-tuple-element.45), channel_id=1, source_target_pairs={{16,24},{24,16},{17,25},{25,17},{18,26},{26,18},{19,27},{27,19},{2... | collective-permute-start | bytes 208904 | tf_op jit(solution)/shard_map/ppermute | solution.py:492
  47.1 1.9 %collective-permute-start.9 = (f32[136,128]{1,0:T(8,128)S(1)}, f32[136,128]{1,0:T(8,128)S(1)}, u32[]{:S(2)}, u32[]{:S(2)}) collective-permute-start(f32[136,128]{1,0:T(8,128)S(1)} %get-tuple-element.43), channel_id=1, source_target_pairs={{0,24},{24,0},{1,25},{25,1},{2,26},{26,2},{3,27},{27,3},{4,28},{28... | collective-permute-start | bytes 208904 | tf_op jit(solution)/shard_map/ppermute | solution.py:492
  49.1 2.3 %collective-permute-done.11.refs_2_ = f32[136,128]{1,0:T(8,128)S(1)} collective-permute-done((f32[136,128]{1,0:T(8,128)S(1)}, f32[136,128]{1,0:T(8,128)S(1)}, u32[]{:S(2)}, u32[]{:S(2)}) %collective-permute-start.11) | collective-permute-done | bytes 69664 | tf_op jit(solution)/shard_map/ppermute | solution.py:492
  51.4 2.8 %collective-permute-done.9.refs_0_ = f32[136,128]{1,0:T(8,128)S(1)} collective-permute-done((f32[136,128]{1,0:T(8,128)S(1)}, f32[136,128]{1,0:T(8,128)S(1)}, u32[]{:S(2)}, u32[]{:S(2)}) %collective-permute-start.9) | collective-permute-done | bytes 69664 | tf_op jit(solution)/shard_map/ppermute | solution.py:492
  54.2 4.8 %shard_map.117 = (f32[64,8,512]{2,1,0:T(8,128)}, f32[4,8,512]{2,1,0:T(8,128)}) custom-call(s32[8,512]{1,0:T(8,128)S(1)} %copy-done.8, f32[64,8,512]{2,1,0:T(8,128)S(1)} %get-tuple-element.26.base, f32[64,8,512]{2,1,0:T(8,128)S(1)} %get-tuple-element.27.impulse, f32[64,8,512]{2,1,0:T(8,128)S(1)} %get-tuple-element.28.upper, ...), custom_call_target="tpu_custom_call" | custom-call | tf_op jit(solution)/shard_map/pallas_call | solution.py:495
  (29 shorter events, 0.8 us)
Async XLA Ops:
  0.6 1.2 %copy-start = (f32[64,8,512]{2,1,0:T(8,128)S(1)}, f32[64,8,512]{2,1,0:T(8,128)}, u32[]{:S(2)}) copy-start(f32[64,8,512]{2,1,0:T(8,128)} %state.3) | copy-start | bytes 3145732
  1.9 1.2 %copy-start.4 = (f32[63,8,512]{2,1,0:T(8,128)S(1)}, f32[63,8,512]{2,1,0:T(8,128)}, u32[]{:S(2)}) copy-start(f32[63,8,512]{2,1,0:T(8,128)} %vert.1) | copy-start | bytes 3096580
  3.1 0.7 %copy-start.6 = (s32[8,512]{1,0:T(8,128)S(1)}, s32[8,512]{1,0:T(8,128)}, u32[]{:S(2)}) copy-start(s32[8,512]{1,0:T(8,128)} %mask.7) | copy-start | bytes 49156
  3.8 0.7 %copy-start.11 = (f32[8,512]{1,0:T(8,128)S(1)}, f32[8,512]{1,0:T(8,128)}, u32[]{:S(2)}) copy-start(f32[8,512]{1,0:T(8,128)} %horiz.3) | copy-start | bytes 49156
  4.5 26.3 %copy-start.2 = (f32[64,8,512]{2,1,0:T(8,128)S(1)}, f32[64,8,512]{2,1,0:T(8,128)}, u32[]{:S(2)}) copy-start(f32[64,8,512]{2,1,0:T(8,128)} %state.3) | copy-start | bytes 3145732
  4.5 26.3 %copy-start.5 = (f32[63,8,512]{2,1,0:T(8,128)S(1)}, f32[63,8,512]{2,1,0:T(8,128)}, u32[]{:S(2)}) copy-start(f32[63,8,512]{2,1,0:T(8,128)} %vert.1) | copy-start | bytes 3096580
  4.5 26.3 %copy-start.8 = (s32[8,512]{1,0:T(8,128)S(1)}, s32[8,512]{1,0:T(8,128)}, u32[]{:S(2)}) copy-start(s32[8,512]{1,0:T(8,128)} %mask.7) | copy-start | bytes 49156
  4.5 26.3 %copy-start.12 = (f32[8,512]{1,0:T(8,128)S(1)}, f32[8,512]{1,0:T(8,128)}, u32[]{:S(2)}) copy-start(f32[8,512]{1,0:T(8,128)} %horiz.3) | copy-start | bytes 49156
  5.6 22.6 %collective-permute-start = (f32[98,8,128]{2,1,0:T(8,128)S(1)}, f32[98,8,128]{2,1,0:T(8,128)S(1)}, u32[]{:S(2)}, u32[]{:S(2)}) collective-permute-start(f32[98,8,128]{2,1,0:T(8,128)S(1)} %get-tuple-element.24.down), channel_id=1, source_target_pairs={{0,1},{1,2},{2,3},{3,4},{4,5},{5,6},{6,7},{7,8},{8,9},{9,10},{10,1... | collective-permute-start | bytes 1204232 | tf_op jit(solution)/shard_map/ppermute | solution.py:444
  7.5 20.7 %collective-permute-start.1 = (f32[98,8,128]{2,1,0:T(8,128)S(1)}, f32[98,8,128]{2,1,0:T(8,128)S(1)}, u32[]{:S(2)}, u32[]{:S(2)}) collective-permute-start(f32[98,8,128]{2,1,0:T(8,128)S(1)} %get-tuple-element.25.up), channel_id=1, source_target_pairs={{1,0},{2,1},{3,2},{4,3},{5,4},{6,5},{7,6},{8,7},{9,8},{10,9},{11,1... | collective-permute-start | bytes 1204232 | tf_op jit(solution)/shard_map/ppermute | solution.py:445
  11.1 1.2 %copy-start.1 = (f32[64,8,512]{2,1,0:T(8,128)S(1)}, f32[64,8,512]{2,1,0:T(8,128)}, u32[]{:S(2)}) copy-start(f32[64,8,512]{2,1,0:T(8,128)} %state.3) | copy-start | bytes 3145732
  12.4 2.2 %copy-start.3 = (bf16[32,4,128,128]{3,2,1,0:T(8,128)(2,1)S(1)}, bf16[32,4,128,128]{3,2,1,0:T(8,128)(2,1)}, u32[]{:S(2)}) copy-start(bf16[32,4,128,128]{3,2,1,0:T(8,128)(2,1)} %param.16) | copy-start | bytes 12582916
  14.6 0.7 %copy-start.7 = (s32[8,512]{1,0:T(8,128)S(1)}, s32[8,512]{1,0:T(8,128)}, u32[]{:S(2)}) copy-start(s32[8,512]{1,0:T(8,128)} %mask.7) | copy-start | bytes 49156
  15.3 0.8 %copy-start.9 = (f32[4,8,512]{2,1,0:T(8,128)S(1)}, f32[4,8,512]{2,1,0:T(8,128)}, u32[]{:S(2)}) copy-start(f32[4,8,512]{2,1,0:T(8,128)} %coupling.1) | copy-start | bytes 196612
  16.1 0.8 %copy-start.10 = (f32[4,8,512]{2,1,0:T(8,128)S(1)}, f32[4,8,512]{2,1,0:T(8,128)}, u32[]{:S(2)}) copy-start(f32[4,8,512]{2,1,0:T(8,128)} %surface.1) | copy-start | bytes 196612
  17.0 0.7 %copy-start.13 = (s32[32,4]{0,1:T(4,128)S(1)}, s32[32,4]{0,1:T(4,128)}, u32[]{:S(2)}) copy-start(s32[32,4]{0,1:T(4,128)} %param.17) | copy-start | bytes 1540
  17.6 0.7 %copy-start.14 = (s32[32,4]{0,1:T(4,128)S(1)}, s32[32,4]{0,1:T(4,128)}, u32[]{:S(2)}) copy-start(s32[32,4]{0,1:T(4,128)} %param.18) | copy-start | bytes 1540
  18.3 0.7 %copy-start.15 = (s32[32,4]{0,1:T(4,128)S(1)}, s32[32,4]{0,1:T(4,128)}, u32[]{:S(2)}) copy-start(s32[32,4]{0,1:T(4,128)} %param.19) | copy-start | bytes 1540
  21.4 1.9 %collective-permute-start.2 = (f32[160,128]{1,0:T(8,128)S(1)}, f32[160,128]{1,0:T(8,128)S(1)}, u32[]{:S(2)}, u32[]{:S(2)}) collective-permute-start(f32[160,128]{1,0:T(8,128)S(1)} %get-tuple-element.36), channel_id=1, source_target_pairs={{0,1},{1,0},{2,3},{3,2},{4,5},{5,4},{6,7},{7,6},{8,9},{9,8},{10,11... | collective-permute-start | bytes 245768 | tf_op jit(solution)/shard_map/ppermute | solution.py:472
  21.4 5.3 %collective-permute-start.3 = (f32[160,128]{1,0:T(8,128)S(1)}, f32[160,128]{1,0:T(8,128)S(1)}, u32[]{:S(2)}, u32[]{:S(2)}) collective-permute-start(f32[160,128]{1,0:T(8,128)S(1)} %get-tuple-element.37), channel_id=1, source_target_pairs={{0,2},{1,3},{2,0},{3,1},{4,6},{5,7},{6,4},{7,5},{8,10},{9,11},{10,... | collective-permute-start | bytes 245768 | tf_op jit(solution)/shard_map/ppermute | solution.py:472
  21.8 12.8 %collective-permute-start.4 = (f32[160,128]{1,0:T(8,128)S(1)}, f32[160,128]{1,0:T(8,128)S(1)}, u32[]{:S(2)}, u32[]{:S(2)}) collective-permute-start(f32[160,128]{1,0:T(8,128)S(1)} %get-tuple-element.38), channel_id=1, source_target_pairs={{0,3},{1,2},{2,1},{3,0},{4,7},{5,6},{6,5},{7,4},{8,11},{9,10},{10,... | collective-permute-start | bytes 245768 | tf_op jit(solution)/shard_map/ppermute | solution.py:472
  23.3 12.2 %collective-permute-start.5 = (f32[160,128]{1,0:T(8,128)S(1)}, f32[160,128]{1,0:T(8,128)S(1)}, u32[]{:S(2)}, u32[]{:S(2)}) collective-permute-start(f32[160,128]{1,0:T(8,128)S(1)} %get-tuple-element.39), channel_id=1, source_target_pairs={{0,4},{1,5},{2,6},{3,7},{4,0},{5,1},{6,2},{7,3},{8,12},{9,13},{10,... | collective-permute-start | bytes 245768 | tf_op jit(solution)/shard_map/ppermute | solution.py:472
  26.7 10.5 %collective-permute-start.6 = (f32[160,128]{1,0:T(8,128)S(1)}, f32[160,128]{1,0:T(8,128)S(1)}, u32[]{:S(2)}, u32[]{:S(2)}) collective-permute-start(f32[160,128]{1,0:T(8,128)S(1)} %get-tuple-element.40), channel_id=1, source_target_pairs={{0,5},{1,4},{2,7},{3,6},{4,1},{5,0},{6,3},{7,2},{8,13},{9,12},{10,... | collective-permute-start | bytes 245768 | tf_op jit(solution)/shard_map/ppermute | solution.py:472
  28.1 11.5 %collective-permute-start.7 = (f32[160,128]{1,0:T(8,128)S(1)}, f32[160,128]{1,0:T(8,128)S(1)}, u32[]{:S(2)}, u32[]{:S(2)}) collective-permute-start(f32[160,128]{1,0:T(8,128)S(1)} %get-tuple-element.41), channel_id=1, source_target_pairs={{0,6},{1,7},{2,4},{3,5},{4,2},{5,3},{6,0},{7,1},{8,14},{9,15},{10,... | collective-permute-start | bytes 245768 | tf_op jit(solution)/shard_map/ppermute | solution.py:472
  28.2 12.8 %collective-permute-start.8 = (f32[160,128]{1,0:T(8,128)S(1)}, f32[160,128]{1,0:T(8,128)S(1)}, u32[]{:S(2)}, u32[]{:S(2)}) collective-permute-start(f32[160,128]{1,0:T(8,128)S(1)} %get-tuple-element.42), channel_id=1, source_target_pairs={{0,7},{1,6},{2,5},{3,4},{4,3},{5,2},{6,1},{7,0},{8,15},{9,14},{10,... | collective-permute-start | bytes 245768 | tf_op jit(solution)/shard_map/ppermute | solution.py:472
  41.3 7.8 %collective-permute-start.10 = (f32[136,128]{1,0:T(8,128)S(1)}, f32[136,128]{1,0:T(8,128)S(1)}, u32[]{:S(2)}, u32[]{:S(2)}) collective-permute-start(f32[136,128]{1,0:T(8,128)S(1)} %get-tuple-element.44), channel_id=1, source_target_pairs={{8,24},{24,8},{9,25},{25,9},{10,26},{26,10},{11,27},{27,11},{12,28... | collective-permute-start | bytes 208904 | tf_op jit(solution)/shard_map/ppermute | solution.py:492
  45.2 6.2 %collective-permute-start.11 = (f32[136,128]{1,0:T(8,128)S(1)}, f32[136,128]{1,0:T(8,128)S(1)}, u32[]{:S(2)}, u32[]{:S(2)}) collective-permute-start(f32[136,128]{1,0:T(8,128)S(1)} %get-tuple-element.45), channel_id=1, source_target_pairs={{16,24},{24,16},{17,25},{25,17},{18,26},{26,18},{19,27},{27,19},{2... | collective-permute-start | bytes 208904 | tf_op jit(solution)/shard_map/ppermute | solution.py:492
  47.1 7.1 %collective-permute-start.9 = (f32[136,128]{1,0:T(8,128)S(1)}, f32[136,128]{1,0:T(8,128)S(1)}, u32[]{:S(2)}, u32[]{:S(2)}) collective-permute-start(f32[136,128]{1,0:T(8,128)S(1)} %get-tuple-element.43), channel_id=1, source_target_pairs={{0,24},{24,0},{1,25},{25,1},{2,26},{26,2},{3,27},{27,3},{4,28},{28... | collective-permute-start | bytes 208904 | tf_op jit(solution)/shard_map/ppermute | solution.py:492

commit v3 on v2

--- a/solution.py
+++ b/solution.py
@@ -439,7 +439,7 @@
             pltpu.VMEM((levels - 1, height, width), jnp.float32),
             pltpu.SemaphoreType.DMA((2,)),
         ],
-        compiler_params=params(8),
+        compiler_params=params(60),
     )(state, vert_coef, horiz_coef, wet_mask)
     above = lax.ppermute(down, axes, pairs)
     below = lax.ppermute(up, axes, back)
@@ -457,7 +457,7 @@
             pltpu.SemaphoreType.DMA((cols,)),
             pltpu.SemaphoreType.DMA((3,)),
         ],
-        compiler_params=params(12),
+        compiler_params=params(60),
     )(
         state,
         coupling,

time: 59.8 us -> 53.9 us (0.901)
  local copies, waits for them, and re-layouts: 11.7 us -> 0.92 us
  Pallas kernels: 12.3 us -> 17.3 us
    unnamed x32 -> x14, local copies, waits for them, and re-layouts: 11.7 us -> 0.92 us
    pallas_call x1, Pallas kernels: 2.33 us -> 4.86 us  [local(): pl.pallas_call(functools.partial(pack_kernel, tiles, slots, groups), out_...]
    pallas_call x1, Pallas kernels: 1.04 us -> 3.54 us  [local(): pl.pallas_call(functools.partial(edge_kernel, groups), out_shape=(f32(edg...]
  transfers between devices with their start and end apart: 12 -> 12, of which waited for: 7 -> 7; matrix products, arithmetic and copies ran while one was open for 0% -> 0% of each run, Pallas kernels for 10% -> 16%
where the time goes in v3:
time: 53.9 us; the launch traced here: 53.6 us
  starting transfers between devices  21.8 us (40%)
  Pallas kernels  17.3 us (32%)
  waiting for transfers between devices  12.8 us (24%)
  local copies, waits for them, and re-layouts  0.92 us (2%)
  between operations  0.8 us (1%)
    ppermute x7, starting transfers between devices, local(): lax.ppermute(packed[k], 'tile', [(i, i ^ k) for i in range(tiles)])  8.58 us
    ppermute x7, waiting for transfers between devices, local(): lax.ppermute(packed[k], 'tile', [(i, i ^ k) for i in range(tiles)])  7.61 us
    ppermute x3, starting transfers between devices, local(): lax.ppermute(merged[g], 'grp', [(g, groups - 1), (groups - 1, g)])  7.51 us
    ppermute x3, waiting for transfers between devices, local(): lax.ppermute(merged[g], 'grp', [(g, groups - 1), (groups - 1, g)])  5.17 us
    pallas_call x1, Pallas kernels, local(): pl.pallas_call(functools.partial(pack_kernel, tiles, slots, groups), out_...  4.86 us
    pallas_call x1, Pallas kernels, local(): pl.pallas_call(functools.partial(last_kernel, cols, groups), out_shape=(f...  4.85 us
    pallas_call x1, Pallas kernels, local(): pl.pallas_call(functools.partial(base_kernel, tiles, groups), out_shape=(...  3.78 us
    ppermute x1, starting transfers between devices, local(): below = lax.ppermute(up, axes, back)  3.64 us
  transfers between devices with their start and end apart: 12, of which 7 were waited for; matrix products, arithmetic and copies ran while one was open for 0% of the time, Pallas kernels for 16%

profile of v3, /device:TPU:14, one launch (start us, length us, event | category | flops | bytes accessed | tf_op | source)
XLA Modules:
  0.0 53.6 jit_solution(1113276460778749998)
XLA Ops:
  0.6 0.0 copy-start
  0.7 0.0 copy-start.4
  0.7 3.5 %shard_map.113 = (f32[98,8,128]{2,1,0:T(8,128)}, f32[98,8,128]{2,1,0:T(8,128)}) custom-call(f32[64,8,512]{2,1,0:T(8,128)} %state.3, f32[63,8,512]{2,1,0:T(8,128)} %vert.1, f32[8,512]{1,0:T(8,128)} %horiz.3, s32[8,512]{1,0:T(8,128)} %mask.7), custom_call_target="tpu_custom_call" | custom-call | tf_op jit(solution)/shard_map/pallas_call | solution.py:433
  4.2 0.0 copy-start.2
  4.2 2.1 %collective-permute-start = (f32[98,8,128]{2,1,0:T(8,128)}, f32[98,8,128]{2,1,0:T(8,128)S(1)}, u32[]{:S(2)}, u32[]{:S(2)}) collective-permute-start(f32[98,8,128]{2,1,0:T(8,128)} %get-tuple-element.24.down), channel_id=1, source_target_pairs={{0,1},{1,2},{2,3},{3,4},{4,5},{5,6},{6,7},{7,8},{8,9},{9,10},{10,1... | collective-permute-start | bytes 1204232 | tf_op jit(solution)/shard_map/ppermute | solution.py:444
  6.3 3.6 %collective-permute-start.1 = (f32[98,8,128]{2,1,0:T(8,128)}, f32[98,8,128]{2,1,0:T(8,128)S(1)}, u32[]{:S(2)}, u32[]{:S(2)}) collective-permute-start(f32[98,8,128]{2,1,0:T(8,128)} %get-tuple-element.25.up), channel_id=1, source_target_pairs={{1,0},{2,1},{3,2},{4,3},{5,4},{6,5},{7,6},{8,7},{9,8},{10,9},{11,1... | collective-permute-start | bytes 1204232 | tf_op jit(solution)/shard_map/ppermute | solution.py:445
  9.9 4.9 %shard_map.115 = (f32[160,128]{1,0:T(8,128)}, f32[160,128]{1,0:T(8,128)}, f32[160,128]{1,0:T(8,128)}, f32[160,128]{1,0:T(8,128)}, f32[160,128]{1,0:T(8,128)}, /*...) custom-call(f32[64,8,512]{2,1,0:T(8,128)} %state.3, f32[4,8,512]{2,1,0:T(8,128)} %coupling.1, ...), custom_call_target="tpu_custom_call" | custom-call | tf_op jit(solution)/shard_map/pallas_call | solution.py:447
  14.8 0.1 collective-permute-start.2
  14.9 0.4 collective-permute-start.3
  15.3 1.5 %collective-permute-start.4 = (f32[160,128]{1,0:T(8,128)}, f32[160,128]{1,0:T(8,128)S(1)}, u32[]{:S(2)}, u32[]{:S(2)}) collective-permute-start(f32[160,128]{1,0:T(8,128)} %get-tuple-element.38), channel_id=1, source_target_pairs={{0,3},{1,2},{2,1},{3,0},{4,7},{5,6},{6,5},{7,4},{8,11},{9,10},{10,... | collective-permute-start | bytes 245768 | tf_op jit(solution)/shard_map/ppermute | solution.py:472
  16.8 0.0 collective-permute-done.2.refs_1_
  16.8 2.6 %collective-permute-start.5 = (f32[160,128]{1,0:T(8,128)}, f32[160,128]{1,0:T(8,128)S(1)}, u32[]{:S(2)}, u32[]{:S(2)}) collective-permute-start(f32[160,128]{1,0:T(8,128)} %get-tuple-element.39), channel_id=1, source_target_pairs={{0,4},{1,5},{2,6},{3,7},{4,0},{5,1},{6,2},{7,3},{8,12},{9,13},{10,... | collective-permute-start | bytes 245768 | tf_op jit(solution)/shard_map/ppermute | solution.py:472
  19.4 1.1 %collective-permute-done.3.refs_2_ = f32[160,128]{1,0:T(8,128)S(1)} collective-permute-done((f32[160,128]{1,0:T(8,128)}, f32[160,128]{1,0:T(8,128)S(1)}, u32[]{:S(2)}, u32[]{:S(2)}) %collective-permute-start.3) | collective-permute-done | bytes 81952 | tf_op jit(solution)/shard_map/ppermute | solution.py:472
  20.4 1.4 %collective-permute-start.6 = (f32[160,128]{1,0:T(8,128)}, f32[160,128]{1,0:T(8,128)S(1)}, u32[]{:S(2)}, u32[]{:S(2)}) collective-permute-start(f32[160,128]{1,0:T(8,128)} %get-tuple-element.40), channel_id=1, source_target_pairs={{0,5},{1,4},{2,7},{3,6},{4,1},{5,0},{6,3},{7,2},{8,13},{9,12},{10,... | collective-permute-start | bytes 245768 | tf_op jit(solution)/shard_map/ppermute | solution.py:472
  21.8 0.0 collective-permute-done.above
  21.8 0.0 collective-permute-start.7
  21.8 0.0 collective-permute-done.1.below
  21.8 2.6 %collective-permute-start.8 = (f32[160,128]{1,0:T(8,128)}, f32[160,128]{1,0:T(8,128)S(1)}, u32[]{:S(2)}, u32[]{:S(2)}) collective-permute-start(f32[160,128]{1,0:T(8,128)} %get-tuple-element.42), channel_id=1, source_target_pairs={{0,7},{1,6},{2,5},{3,4},{4,3},{5,2},{6,1},{7,0},{8,15},{9,14},{10,... | collective-permute-start | bytes 245768 | tf_op jit(solution)/shard_map/ppermute | solution.py:472
  24.5 3.8 %shard_map.114 = (f32[64,8,512]{2,1,0:T(8,128)S(1)}, f32[64,8,512]{2,1,0:T(8,128)S(1)}, f32[64,8,512]{2,1,0:T(8,128)S(1)}, f32[64,8,512]{2,1,0:T(8,128)S(1)}, f3...) custom-call(f32[64,8,512]{2,1,0:T(8,128)S(1)} %copy-done, ...), custom_call_target="tpu_custom_call" | custom-call | flops 15728640 | bytes 7340032 | tf_op jit(solution)/shard_map/pallas_call | solution.py:477
  28.3 0.0 collective-permute-done.4.refs_3_
  28.3 1.0 %collective-permute-done.5.refs_4_ = f32[160,128]{1,0:T(8,128)S(1)} collective-permute-done((f32[160,128]{1,0:T(8,128)}, f32[160,128]{1,0:T(8,128)S(1)}, u32[]{:S(2)}, u32[]{:S(2)}) %collective-permute-start.5) | collective-permute-done | bytes 81952 | tf_op jit(solution)/shard_map/ppermute | solution.py:472
  29.3 1.8 %collective-permute-done.6.refs_5_ = f32[160,128]{1,0:T(8,128)S(1)} collective-permute-done((f32[160,128]{1,0:T(8,128)}, f32[160,128]{1,0:T(8,128)S(1)}, u32[]{:S(2)}, u32[]{:S(2)}) %collective-permute-start.6) | collective-permute-done | bytes 81952 | tf_op jit(solution)/shard_map/ppermute | solution.py:472
  31.0 2.3 %collective-permute-done.7.refs_6_ = f32[160,128]{1,0:T(8,128)S(1)} collective-permute-done((f32[160,128]{1,0:T(8,128)}, f32[160,128]{1,0:T(8,128)S(1)}, u32[]{:S(2)}, u32[]{:S(2)}) %collective-permute-start.7) | collective-permute-done | bytes 81952 | tf_op jit(solution)/shard_map/ppermute | solution.py:472
  33.4 1.5 %collective-permute-done.8.refs_7_ = f32[160,128]{1,0:T(8,128)S(1)} collective-permute-done((f32[160,128]{1,0:T(8,128)}, f32[160,128]{1,0:T(8,128)S(1)}, u32[]{:S(2)}, u32[]{:S(2)}) %collective-permute-start.8) | collective-permute-done | bytes 81952 | tf_op jit(solution)/shard_map/ppermute | solution.py:472
  34.9 0.9 %copy-done.5 = f32[160,128]{1,0:T(8,128)S(1)} copy-done((f32[160,128]{1,0:T(8,128)S(1)}, f32[160,128]{1,0:T(8,128)}, u32[]{:S(2)}) %copy-start.5) | copy-done | bytes 81944
  35.7 0.3 shard_map.116
  36.0 3.7 %collective-permute-start.10 = (f32[136,128]{1,0:T(8,128)S(1)}, f32[136,128]{1,0:T(8,128)S(1)}, u32[]{:S(2)}, u32[]{:S(2)}) collective-permute-start(f32[136,128]{1,0:T(8,128)S(1)} %get-tuple-element.44), channel_id=1, source_target_pairs={{8,24},{24,8},{9,25},{25,9},{10,26},{26,10},{11,27},{27,11},{12,28... | collective-permute-start | bytes 208904 | tf_op jit(solution)/shard_map/ppermute | solution.py:492
  39.7 1.9 %collective-permute-start.11 = (f32[136,128]{1,0:T(8,128)S(1)}, f32[136,128]{1,0:T(8,128)S(1)}, u32[]{:S(2)}, u32[]{:S(2)}) collective-permute-start(f32[136,128]{1,0:T(8,128)S(1)} %get-tuple-element.45), channel_id=1, source_target_pairs={{16,24},{24,16},{17,25},{25,17},{18,26},{26,18},{19,27},{27,19},{2... | collective-permute-start | bytes 208904 | tf_op jit(solution)/shard_map/ppermute | solution.py:492
  41.6 1.9 %collective-permute-start.9 = (f32[136,128]{1,0:T(8,128)S(1)}, f32[136,128]{1,0:T(8,128)S(1)}, u32[]{:S(2)}, u32[]{:S(2)}) collective-permute-start(f32[136,128]{1,0:T(8,128)S(1)} %get-tuple-element.43), channel_id=1, source_target_pairs={{0,24},{24,0},{1,25},{25,1},{2,26},{26,2},{3,27},{27,3},{4,28},{28... | collective-permute-start | bytes 208904 | tf_op jit(solution)/shard_map/ppermute | solution.py:492
  43.6 2.3 %collective-permute-done.11.refs_2_ = f32[136,128]{1,0:T(8,128)S(1)} collective-permute-done((f32[136,128]{1,0:T(8,128)S(1)}, f32[136,128]{1,0:T(8,128)S(1)}, u32[]{:S(2)}, u32[]{:S(2)}) %collective-permute-start.11) | collective-permute-done | bytes 69664 | tf_op jit(solution)/shard_map/ppermute | solution.py:492
  45.9 2.8 %collective-permute-done.9.refs_0_ = f32[136,128]{1,0:T(8,128)S(1)} collective-permute-done((f32[136,128]{1,0:T(8,128)S(1)}, f32[136,128]{1,0:T(8,128)S(1)}, u32[]{:S(2)}, u32[]{:S(2)}) %collective-permute-start.9) | collective-permute-done | bytes 69664 | tf_op jit(solution)/shard_map/ppermute | solution.py:492
  48.7 4.8 %shard_map.117 = (f32[64,8,512]{2,1,0:T(8,128)}, f32[4,8,512]{2,1,0:T(8,128)}) custom-call(s32[8,512]{1,0:T(8,128)S(1)} %copy-done.4, f32[64,8,512]{2,1,0:T(8,128)S(1)} %get-tuple-element.26.base, f32[64,8,512]{2,1,0:T(8,128)S(1)} %get-tuple-element.27.impulse, f32[64,8,512]{2,1,0:T(8,128)S(1)} %get-tuple-element.28.upper, ...), custom_call_target="tpu_custom_call" | custom-call | tf_op jit(solution)/shard_map/pallas_call | solution.py:495
  (11 shorter events, 0.0 us)
Async XLA Ops:
  0.6 23.9 %copy-start = (f32[64,8,512]{2,1,0:T(8,128)S(1)}, f32[64,8,512]{2,1,0:T(8,128)}, u32[]{:S(2)}) copy-start(f32[64,8,512]{2,1,0:T(8,128)} %state.3) | copy-start | bytes 3145732
  0.6 23.8 %copy-start.1 = (f32[63,8,512]{2,1,0:T(8,128)S(1)}, f32[63,8,512]{2,1,0:T(8,128)}, u32[]{:S(2)}) copy-start(f32[63,8,512]{2,1,0:T(8,128)} %vert.1) | copy-start | bytes 3096580
  0.7 23.8 %copy-start.6 = (f32[8,512]{1,0:T(8,128)S(1)}, f32[8,512]{1,0:T(8,128)}, u32[]{:S(2)}) copy-start(f32[8,512]{1,0:T(8,128)} %horiz.3) | copy-start | bytes 49156
  0.7 23.8 %copy-start.4 = (s32[8,512]{1,0:T(8,128)S(1)}, s32[8,512]{1,0:T(8,128)}, u32[]{:S(2)}) copy-start(s32[8,512]{1,0:T(8,128)} %mask.7) | copy-start | bytes 49156
  4.2 20.3 %copy-start.2 = (f32[98,8,128]{2,1,0:T(8,128)S(1)}, f32[98,8,128]{2,1,0:T(8,128)}, u32[]{:S(2)}) copy-start(f32[98,8,128]{2,1,0:T(8,128)} %get-tuple-element.24.down) | copy-start | bytes 1204228
  4.2 20.3 %copy-start.3 = (f32[98,8,128]{2,1,0:T(8,128)S(1)}, f32[98,8,128]{2,1,0:T(8,128)}, u32[]{:S(2)}) copy-start(f32[98,8,128]{2,1,0:T(8,128)} %get-tuple-element.25.up) | copy-start | bytes 1204228
  4.2 17.6 %collective-permute-start = (f32[98,8,128]{2,1,0:T(8,128)}, f32[98,8,128]{2,1,0:T(8,128)S(1)}, u32[]{:S(2)}, u32[]{:S(2)}) collective-permute-start(f32[98,8,128]{2,1,0:T(8,128)} %get-tuple-element.24.down), channel_id=1, source_target_pairs={{0,1},{1,2},{2,3},{3,4},{4,5},{5,6},{6,7},{7,8},{8,9},{9,10},{10,1... | collective-permute-start | bytes 1204232 | tf_op jit(solution)/shard_map/ppermute | solution.py:444
  6.3 15.5 %collective-permute-start.1 = (f32[98,8,128]{2,1,0:T(8,128)}, f32[98,8,128]{2,1,0:T(8,128)S(1)}, u32[]{:S(2)}, u32[]{:S(2)}) collective-permute-start(f32[98,8,128]{2,1,0:T(8,128)} %get-tuple-element.25.up), channel_id=1, source_target_pairs={{1,0},{2,1},{3,2},{4,3},{5,4},{6,5},{7,6},{8,7},{9,8},{10,9},{11,1... | collective-permute-start | bytes 1204232 | tf_op jit(solution)/shard_map/ppermute | solution.py:445
  14.8 1.9 %collective-permute-start.2 = (f32[160,128]{1,0:T(8,128)}, f32[160,128]{1,0:T(8,128)S(1)}, u32[]{:S(2)}, u32[]{:S(2)}) collective-permute-start(f32[160,128]{1,0:T(8,128)} %get-tuple-element.36), channel_id=1, source_target_pairs={{0,1},{1,0},{2,3},{3,2},{4,5},{5,4},{6,7},{7,6},{8,9},{9,8},{10,11... | collective-permute-start | bytes 245768 | tf_op jit(solution)/shard_map/ppermute | solution.py:472
  14.9 5.5 %collective-permute-start.3 = (f32[160,128]{1,0:T(8,128)}, f32[160,128]{1,0:T(8,128)S(1)}, u32[]{:S(2)}, u32[]{:S(2)}) collective-permute-start(f32[160,128]{1,0:T(8,128)} %get-tuple-element.37), channel_id=1, source_target_pairs={{0,2},{1,3},{2,0},{3,1},{4,6},{5,7},{6,4},{7,5},{8,10},{9,11},{10,... | collective-permute-start | bytes 245768 | tf_op jit(solution)/shard_map/ppermute | solution.py:472
  15.3 13.0 %collective-permute-start.4 = (f32[160,128]{1,0:T(8,128)}, f32[160,128]{1,0:T(8,128)S(1)}, u32[]{:S(2)}, u32[]{:S(2)}) collective-permute-start(f32[160,128]{1,0:T(8,128)} %get-tuple-element.38), channel_id=1, source_target_pairs={{0,3},{1,2},{2,1},{3,0},{4,7},{5,6},{6,5},{7,4},{8,11},{9,10},{10,... | collective-permute-start | bytes 245768 | tf_op jit(solution)/shard_map/ppermute | solution.py:472
  16.8 12.5 %collective-permute-start.5 = (f32[160,128]{1,0:T(8,128)}, f32[160,128]{1,0:T(8,128)S(1)}, u32[]{:S(2)}, u32[]{:S(2)}) collective-permute-start(f32[160,128]{1,0:T(8,128)} %get-tuple-element.39), channel_id=1, source_target_pairs={{0,4},{1,5},{2,6},{3,7},{4,0},{5,1},{6,2},{7,3},{8,12},{9,13},{10,... | collective-permute-start | bytes 245768 | tf_op jit(solution)/shard_map/ppermute | solution.py:472
  20.4 10.6 %collective-permute-start.6 = (f32[160,128]{1,0:T(8,128)}, f32[160,128]{1,0:T(8,128)S(1)}, u32[]{:S(2)}, u32[]{:S(2)}) collective-permute-start(f32[160,128]{1,0:T(8,128)} %get-tuple-element.40), channel_id=1, source_target_pairs={{0,5},{1,4},{2,7},{3,6},{4,1},{5,0},{6,3},{7,2},{8,13},{9,12},{10,... | collective-permute-start | bytes 245768 | tf_op jit(solution)/shard_map/ppermute | solution.py:472
  21.8 11.5 %collective-permute-start.7 = (f32[160,128]{1,0:T(8,128)}, f32[160,128]{1,0:T(8,128)S(1)}, u32[]{:S(2)}, u32[]{:S(2)}) collective-permute-start(f32[160,128]{1,0:T(8,128)} %get-tuple-element.41), channel_id=1, source_target_pairs={{0,6},{1,7},{2,4},{3,5},{4,2},{5,3},{6,0},{7,1},{8,14},{9,15},{10,... | collective-permute-start | bytes 245768 | tf_op jit(solution)/shard_map/ppermute | solution.py:472
  21.8 13.0 %collective-permute-start.8 = (f32[160,128]{1,0:T(8,128)}, f32[160,128]{1,0:T(8,128)S(1)}, u32[]{:S(2)}, u32[]{:S(2)}) collective-permute-start(f32[160,128]{1,0:T(8,128)} %get-tuple-element.42), channel_id=1, source_target_pairs={{0,7},{1,6},{2,5},{3,4},{4,3},{5,2},{6,1},{7,0},{8,15},{9,14},{10,... | collective-permute-start | bytes 245768 | tf_op jit(solution)/shard_map/ppermute | solution.py:472
  34.9 0.9 %copy-start.5 = (f32[160,128]{1,0:T(8,128)S(1)}, f32[160,128]{1,0:T(8,128)}, u32[]{:S(2)}) copy-start(f32[160,128]{1,0:T(8,128)} %get-tuple-element.35.refs_0_) | copy-start | bytes 245764
  36.0 7.5 %collective-permute-start.10 = (f32[136,128]{1,0:T(8,128)S(1)}, f32[136,128]{1,0:T(8,128)S(1)}, u32[]{:S(2)}, u32[]{:S(2)}) collective-permute-start(f32[136,128]{1,0:T(8,128)S(1)} %get-tuple-element.44), channel_id=1, source_target_pairs={{8,24},{24,8},{9,25},{25,9},{10,26},{26,10},{11,27},{27,11},{12,28... | collective-permute-start | bytes 208904 | tf_op jit(solution)/shard_map/ppermute | solution.py:492
  39.7 6.2 %collective-permute-start.11 = (f32[136,128]{1,0:T(8,128)S(1)}, f32[136,128]{1,0:T(8,128)S(1)}, u32[]{:S(2)}, u32[]{:S(2)}) collective-permute-start(f32[136,128]{1,0:T(8,128)S(1)} %get-tuple-element.45), channel_id=1, source_target_pairs={{16,24},{24,16},{17,25},{25,17},{18,26},{26,18},{19,27},{27,19},{2... | collective-permute-start | bytes 208904 | tf_op jit(solution)/shard_map/ppermute | solution.py:492
  41.6 7.1 %collective-permute-start.9 = (f32[136,128]{1,0:T(8,128)S(1)}, f32[136,128]{1,0:T(8,128)S(1)}, u32[]{:S(2)}, u32[]{:S(2)}) collective-permute-start(f32[136,128]{1,0:T(8,128)S(1)} %get-tuple-element.43), channel_id=1, source_target_pairs={{0,24},{24,0},{1,25},{25,1},{2,26},{26,2},{3,27},{27,3},{4,28},{28... | collective-permute-start | bytes 208904 | tf_op jit(solution)/shard_map/ppermute | solution.py:492

commit v4 on v3

v4 whole, which is shorter than its diff:
```python
import functools

import jax
import jax.numpy as jnp
from jax import lax
from jax.experimental import pallas as pl
from jax.experimental.pallas import tpu as pltpu
from jax.sharding import PartitionSpec as P

F = 4
K = 4
FORCING_GAIN = 0.25
VM = pl.BlockSpec(memory_space=pltpu.VMEM)
HBM = pl.BlockSpec(memory_space=pltpu.HBM)
MIB = 1024 * 1024


def params(mib):
    return pltpu.CompilerParams(vmem_limit_bytes=mib * MIB)


def split(x):
    hi = x.astype(jnp.bfloat16)
    return hi, (x - hi.astype(jnp.float32)).astype(jnp.bfloat16)


def wet_of(ocean, mask):
    return jnp.where(ocean, mask.astype(jnp.float32), 1.0)


def iota(shape, dim):
    return lax.broadcasted_iota(jnp.int32, shape, dim)


def pack_kernel(
    tiles, slots, groups, state, coupling, surface, mask, dtile, dblock, dgroup, w, *refs
):
    outs = refs[: tiles // 2]
    terms, w_here, *here, w_sem, sem = refs[tiles // 2 :]
    height, width = mask.shape
    cols = width // 128
    given = (dtile, dblock, dgroup, state.at[0], coupling, surface, mask)
    small = [pltpu.make_async_copy(a, b, sem.at[i]) for i, (a, b) in enumerate(zip(given, here))]
    large = [pltpu.make_async_copy(w.at[:, c], w_here.at[c], w_sem.at[c]) for c in range(cols)]
    for copy in small + large:
        copy.start()
    dtile, dblock, dgroup, state, coupling, surface, mask = here
    for copy in small[:3]:
        copy.wait()
    blocks = height * cols
    count = blocks * K
    ocean = lax.axis_index("grp") == groups - 1
    me = lax.axis_index("tile")

    block = dblock[...]
    line = block // cols
    col = block % cols
    group = jnp.where(ocean, dgroup[...], groups - 1)
    code = dtile[...] * 128 + col * height + line + jnp.where(ocean, dgroup[...] * blocks, 0)
    device = group * tiles + dtile[...]
    low = jnp.where(ocean, 0, (groups - 1) * tiles)
    high = jnp.where(ocean, (groups - 1) * tiles, groups * tiles)
    odd = device % 2 == 1
    beside = jnp.where(odd, device + 1, device - 1)
    reads = (line == jnp.where(odd, height - 1, 0)) & (beside >= low) & (beside < high)
    edge = (beside % tiles) * 16 + col + jnp.where(ocean, (beside // tiles) * cols, 0)
    edge = jnp.where(reads, edge, -1)

    item = iota((count, blocks), 0)
    item_k = (item // height) % K
    own = iota((count, blocks), 1) == (item % height) * cols + item // (height * K)
    up, down = iota((count, count), 0), iota((count, count), 1)

    def column(values):
        spread = jnp.broadcast_to(values[:1, :], (count, blocks))
        for k in range(1, K):
            spread = jnp.where(item_k == k, values[k : k + 1, :], spread)
        return jnp.sum(jnp.where(own, spread, 0), 1, keepdims=True)

    def turned(values):
        return jnp.sum(jnp.where(up == down, values, 0), 0, keepdims=True)

    def place_of(tile):
        return ((tile // 2) ^ (me // 2)) * 2 + tile % 2

    code_col, edge_row = column(code), turned(column(edge))
    code_row = turned(code_col)
    tile_row, tile_col, tag_col = code_row // 128, code_col // 128, code_col % 128
    same = tile_row == tile_col
    slot_row = jnp.sum(jnp.where(same & (up < down), 1, 0), 0, keepdims=True)
    slot_col = jnp.sum(jnp.where(same & (down < up), 1, 0), 1, keepdims=True)
    place_row, place_col = place_of(tile_row), place_of(tile_col)
    chooser = jnp.where(
        iota((tiles * slots, count), 0) == place_row * slots + slot_row, 1.0, 0.0
    ).astype(jnp.bfloat16)
    to_tile = jnp.where(iota((tiles, count), 0) == place_row, 1.0, 0.0).astype(jnp.bfloat16)
    labels = jnp.where(
        iota((count, 128), 1) == (place_col // 2) * slots + slot_col,
        (tag_col + 1).astype(jnp.float32),
        0.0,
    ).astype(jnp.bfloat16)
    tags = jnp.dot(to_tile, labels, preferred_element_type=jnp.float32)
    rim = cols * (groups - 1)
    rim_id = iota((tiles * 16, count), 0)
    rim_place, rim_id = rim_id // 16, rim_id % 16
    rim_tile = ((rim_place // 2) ^ (me // 2)) * 2 + rim_place % 2
    rim_id = jnp.where(
        rim_id < rim, rim_tile * 16 + jnp.where(ocean, rim_id, rim_id % cols), -2
    )
    rim_chooser = jnp.where(rim_id == edge_row, 1.0, 0.0).astype(jnp.bfloat16)

    for copy in small[3:]:
        copy.wait()
    send = coupling[...] * (state[...][None] - surface[...]) * wet_of(ocean, mask[...])[None]
    row_of = iota((F * height, 128), 0) % height
    for c in range(cols):
        piece = send[:, :, c * 128 : (c + 1) * 128].reshape(F * height, 128)
        left = jnp.concatenate(
            [jnp.where(row_of == r, piece, 0.0).astype(jnp.bfloat16) for r in range(height)], 1
        )
        large[c].wait()
        for k in range(K):
            right = w_here[c, :, k].reshape(height * 128, 128)
            made = jnp.dot(left, right, preferred_element_type=jnp.float32)
            at = (c * K + k) * height
            for f in range(F):
                terms[at : at + height, f * 128 : (f + 1) * 128] = made[
                    f * height : (f + 1) * height, :
                ]
    total = terms[:, :128]
    for f in range(1, F):
        total = total + terms[:, f * 128 : (f + 1) * 128]
    hi, lo = split(terms[...])
    packed = jnp.dot(
        jnp.concatenate([chooser, chooser], 1),
        jnp.concatenate([hi, lo], 0),
        preferred_element_type=jnp.float32,
    )
    hi, lo = split(total)
    rims = jnp.dot(
        jnp.concatenate([rim_chooser, rim_chooser], 1),
        jnp.concatenate([hi, lo], 0),
        preferred_element_type=jnp.float32,
    )
    size = F * slots + 16
    for t in range(tiles):
        out, at = outs[t // 2], (t % 2) * size
        for f in range(F):
            out[at + f * slots : at + (f + 1) * slots, :] = packed[
                t * slots : (t + 1) * slots, f * 128 : (f + 1) * 128
            ]
        at = at + F * slots
        out[at : at + 16, :] = rims[t * 16 : (t + 1) * 16, :]
        out[at + rim : at + rim + 1, :] = tags[t : t + 1, :]


def merge_kernel(slots, height, cols, groups, _, *refs):
    got, (mine, theirs) = refs[:-2], refs[-2:]
    blocks = height * cols
    size = F * slots + 16
    rim = cols * (groups - 1)
    rows = (groups - 1) * blocks
    ocean = lax.axis_index("grp") == groups - 1
    core = lax.axis_index("tile") % 2
    ids = iota((rows, 128), 0)
    ids = jnp.where(ocean, ids, ids % blocks) + 1

    def merged(which, out):
        first = which * size
        tail = got[0][pl.ds(first + F * slots, 16), :]
        for chunk in got[1:]:
            tail = tail + chunk[pl.ds(first + F * slots, 16), :]
        label = tail[rim : rim + 1, :].astype(jnp.int32)
        chooser = jnp.where(ids == label, 1.0, 0.0).astype(jnp.bfloat16)
        chooser = jnp.concatenate([chooser, chooser], 1)
        total = jnp.zeros((rows, 128), jnp.float32)
        for f in range(F):
            data = jnp.concatenate([chunk[pl.ds(first + f * slots, slots), :] for chunk in got], 0)
            hi, lo = split(data)
            part = jnp.dot(chooser, jnp.concatenate([hi, lo], 0), preferred_element_type=jnp.float32)
            total = total + part
            for g in range(groups - 1):
                at = (g * F + f) * blocks
                out[at : at + blocks, :] = part[g * blocks : (g + 1) * blocks, :]
        out[rows * F : rows * F + rim, :] = tail[:rim, :]
        return total.reshape(rim, height, 128)

    own = merged(core, mine)
    sibling = merged(1 - core, theirs)
    even = core == 0
    at = rows * F + rim
    theirs[at : at + rim, :] = jnp.where(even, own[:, height - 1, :], own[:, 0, :])
    mine[at : at + rim, :] = jnp.where(even, sibling[:, 0, :], sibling[:, height - 1, :])


def add_kernel(cols, mine, theirs, *outs):
    even = lax.axis_index("tile") % 2 == 0
    rows = outs[0].shape[0] - 2 * cols
    groups = len(outs)
    tail = groups * rows
    rims = mine[tail:, :] + theirs[tail:, :]
    for g, out in enumerate(outs):
        out[:rows, :] = mine[g * rows : (g + 1) * rows, :] + theirs[g * rows : (g + 1) * rows, :]
        far = rims[g * cols : (g + 1) * cols, :]
        near = rims[(groups + g) * cols : (groups + g + 1) * cols, :]
        out[rows : rows + cols, :] = jnp.where(even, far, near)
        out[rows + cols :, :] = jnp.where(even, near, far)


def edge_kernel(groups, state, vert, horiz, mask, down, up, wet, sem):
    levels, height, width = state.shape
    half = levels // 2
    cols = width // 128
    last = height - 1
    copies = [pltpu.make_async_copy(mask, wet, sem.at[0])]

    def move(src, dst):
        copies.append(pltpu.make_async_copy(src, dst, sem.at[len(copies)]))

    for c in range(cols):
        at, one, two = pl.ds(c * 128, 128), pl.ds(c, 1), pl.ds(cols + c, 1)
        all_levels = pl.ds(0, levels)
        move(state.at[:, pl.ds(last, 1), at], down.at[all_levels, one])
        move(state.at[:, pl.ds(last - 1, 1), at], down.at[all_levels, two])
        move(state.at[:, pl.ds(1, 1), at], up.at[all_levels, one])
        move(state.at[:, pl.ds(0, 1), at], up.at[all_levels, two])
        for out, row in ((down, pl.ds(last, 1)), (up, pl.ds(0, 1))):
            move(vert.at[pl.ds(0, half), row, at], out.at[pl.ds(levels, half), one])
            move(vert.at[pl.ds(half, half - 1), row, at], out.at[pl.ds(levels, half - 1), two])
            move(horiz.at[row, at], out.at[levels + half + 1, one])
            move(horiz.at[row, at], out.at[levels + half + 1, two])
    for copy in copies:
        copy.start()
    copies[0].wait()
    wet = wet_of(lax.axis_index("grp") == groups - 1, wet[...])
    for c in range(cols):
        at = slice(c * 128, (c + 1) * 128)
        one, two = slice(c, c + 1), slice(cols + c, cols + c + 1)
        down[levels + half, one, :] = wet[last:, at]
        down[levels + half, two, :] = wet[last - 1 : last, at]
        up[levels + half, one, :] = wet[1:2, at]
        up[levels + half, two, :] = wet[:1, at]
        for out in (down, up):
            out[levels + half - 1, two, :] = jnp.zeros((1, 128), jnp.float32)
    for copy in copies[1:]:
        copy.wait()


def weights_of(tiles, groups, horiz, wet, wet_above, wet_below):
    height, width = wet.shape
    device = lax.axis_index("grp") * tiles + lax.axis_index("tile")
    rows = device * height + iota((height, width), 0)
    start = (groups - 1) * tiles * height
    last = groups * tiles * height - 1
    above = jnp.concatenate([wet_above, wet[:-1]], 0)
    below = jnp.concatenate([wet[1:], wet_below], 0)
    above = jnp.where((rows > 0) & (rows != start), above, 0.0)
    below = jnp.where((rows < last) & (rows + 1 != start), below, 0.0)
    column = iota((height, width), 1)
    left = jnp.where(column == 0, 0.0, pltpu.roll(wet, 1, 1))
    right = jnp.where(column == width - 1, 0.0, pltpu.roll(wet, width - 1, 1))
    scale = horiz * wet
    return scale * left, scale * right, scale * above, scale * below


def line_of(halo, first, cols):
    return jnp.concatenate([halo[first + c : first + c + 1, :] for c in range(cols)], 1)


def around(field, halo):
    height, width = field.shape
    cols = width // 128
    return (
        pltpu.roll(field, 1, 1),
        pltpu.roll(field, width - 1, 1),
        jnp.concatenate([line_of(halo, 0, cols), field[:-1]], 0),
        jnp.concatenate([field[1:], line_of(halo, cols, cols)], 0),
    )


def stencil(field, halo, weights):
    total = field
    for other, weight in zip(around(field, halo), weights):
        total = total + weight * (other - field)
    return total


def shifted(halo, lane):
    rows = halo.shape[0]
    to_right, to_left = pltpu.roll(halo, 1, 1), pltpu.roll(halo, 127, 1)
    return (
        jnp.where(lane == 0, pltpu.roll(to_right, 1, 0), to_right),
        jnp.where(lane == 127, pltpu.roll(to_left, rows - 1, 0), to_left),
    )


def solve_kernel(
    tiles, groups, state, vert, horiz, mask, down, up, above, below, parts, halo_wet,
    upper, gain, ratio, base, impulse, halo_base, halo_impulse, halo_vert, halo_upper,
):
    levels, height, width = state.shape
    cols = width // 128
    half = levels // 2
    shape = (2 * cols, 128)
    low_half = iota(shape, 0) < cols
    lane = iota(shape, 1)

    def turn(x):
        return pltpu.roll(x, cols, 0)

    def beside(i):
        return jnp.where(low_half, above[i], below[i])

    def behind(i):
        return turn(jnp.where(low_half, below[i], above[i]))

    def inside(i):
        return turn(jnp.where(low_half, down[i], up[i]))

    wet = wet_of(lax.axis_index("grp") == groups - 1, mask[...])
    wet_halo = beside(levels + half)
    halo_wet[...] = wet_halo
    weights = weights_of(
        tiles, groups, horiz[...], wet, line_of(wet_halo, 0, cols), line_of(wet_halo, cols, cols)
    )
    scale = beside(levels + half + 1) * wet_halo
    wet_left, wet_right = shifted(wet_halo, lane)
    place = iota(shape, 0) % cols
    weight_left = scale * jnp.where((place == 0) & (lane == 0), 0.0, wet_left)
    weight_right = scale * jnp.where((place == cols - 1) & (lane == 127), 0.0, wet_right)
    weight_behind = scale * behind(levels + half)
    weight_inside = scale * inside(levels + half)

    def spread(i, _):
        a, b = above[levels + i], below[levels + i]
        halo_vert[i] = jnp.where(low_half, a, turn(b)) * wet_halo
        halo_vert[half + i] = jnp.where(low_half, turn(a), b) * wet_halo
        return 0

    lax.fori_loop(0, half, spread, 0, unroll=4)
    zero = jnp.zeros((height, width), jnp.float32)
    zero_halo = jnp.zeros(shape, jnp.float32)

    def forward(level, carry, last=False, first=False):
        low, c, r, e, low_h, c_h, r_h, e_h = carry
        upp = zero if last else vert[level] * wet
        inverse = 1.0 / (1.0 + low + upp + low * c)
        c = -upp * inverse
        step = low * inverse
        halo = beside(level)
        r = stencil(state[level], halo, weights) * inverse + step * r
        e = inverse if first else step * e
        upper[level] = c
        gain[level] = inverse
        ratio[level] = step
        base[level] = r
        impulse[level] = e
        upp_h = zero_halo if last else halo_vert[level]
        inverse = 1.0 / (1.0 + low_h + upp_h + low_h * c_h)
        c_h = -upp_h * inverse
        step = low_h * inverse
        left, right = shifted(halo, lane)
        field = (
            halo
            + weight_left * (left - halo)
            + weight_right * (right - halo)
            + weight_behind * (behind(level) - halo)
            + weight_inside * (inside(level) - halo)
        )
        r_h = field * inverse + step * r_h
        e_h = inverse if first else step * e_h
        halo_upper[level] = c_h
        halo_base[level] = r_h
        halo_impulse[level] = e_h
        return upp, c, r, e, upp_h, c_h, r_h, e_h

    carry = forward(0, (zero,) * 4 + (zero_halo,) * 4, first=True)
    carry = lax.fori_loop(1, levels - 1, forward, carry, unroll=2)
    carry = forward(levels - 1, carry, last=True)

    def backward(i, carry):
        level = levels - 2 - i
        c, c_h = upper[level], halo_upper[level]
        x = base[level] - c * carry[0]
        y = impulse[level] - c * carry[1]
        x_h = halo_base[level] - c_h * carry[2]
        y_h = halo_impulse[level] - c_h * carry[3]
        base[level] = x
        impulse[level] = y
        halo_base[level] = x_h
        halo_impulse[level] = y_h
        return x, y, x_h, y_h

    lax.fori_loop(0, levels - 1, backward, (carry[2], carry[3], carry[6], carry[7]), unroll=2)

    rest = 1.0 - weights[0] - weights[1] - weights[2] - weights[3]

    def forward_parts(level, carry, first=False):
        g = impulse[level]
        rhs = [stencil(base[level], halo_base[level], weights), rest * g + (1.0 if first else 0.0)]
        rhs += [w * x for w, x in zip(weights, around(g, halo_impulse[level]))]
        inverse, step = gain[level], ratio[level]
        made = tuple(x * inverse + step * r for x, r in zip(rhs, carry))
        for i in range(6):
            parts[i, level] = made[i]
        return made

    carry = forward_parts(0, (zero,) * 6, first=True)
    carry = lax.fori_loop(1, levels, forward_parts, carry)

    def backward_parts(i, carry):
        level = levels - 2 - i
        c = upper[level]
        made = tuple(parts[j, level] - c * carry[j] for j in range(6))
        for j in range(6):
            parts[j, level] = made[j]
        return made

    lax.fori_loop(0, levels - 1, backward_parts, carry, unroll=2)


def last_kernel(cols, groups, mask, parts, halo_wet, *refs):
    arrived = refs[: groups - 1]
    out, received, field, sem = refs[groups - 1 :]
    _, levels, height, width = parts.shape
    total = arrived[0][...]
    for other in arrived[1:]:
        total = total + other[...]
    for f in range(F):
        for c in range(cols):
            at = (f * cols + c) * height
            received[f, :, c * 128 : (c + 1) * 128] = total[at : at + height, :]
    wet = wet_of(lax.axis_index("grp") == groups - 1, mask[...])
    force = FORCING_GAIN * wet * jnp.sum(received[...], 0)
    force_halo = FORCING_GAIN * halo_wet[...] * total[F * cols * height :, :]
    factors = (force,) + around(force, force_halo)

    def level_of(level, _):
        x = parts[0, level]
        for i in range(5):
            x = x + parts[i + 1, level] * factors[i]
        field[level] = x
        return 0

    chunks = 4
    size = levels // chunks
    copies = []
    for i in range(chunks):
        lax.fori_loop(i * size, (i + 1) * size, level_of, 0, unroll=4)
        at = pl.ds(i * size, size)
        copies.append(pltpu.make_async_copy(field.at[at], out.at[at], sem.at[i]))
        copies[-1].start()
    for copy in copies:
        copy.wait()


def f32(*shape):
    return jax.ShapeDtypeStruct(shape, jnp.float32)


def cost(us):
    return pl.CostEstimate(flops=0, bytes_accessed=int(us * 3e6), transcendentals=0)


def local(
    state, vert_coef, horiz_coef, wet_mask, coupling, surface_in, remap_w, dest_tile, dest_block, dest_group
):
    levels, height, width = state.shape
    groups, tiles = lax.axis_size("grp"), lax.axis_size("tile")
    cols = width // 128
    blocks = height * cols
    slots = max(8, 2 * blocks * K // tiles)
    rim = 2 * cols
    devices = groups * tiles
    start = (groups - 1) * tiles
    pairs = [(i, i + 1) for i in range(devices - 1) if i + 1 != start]
    back = [(j, i) for i, j in pairs]
    axes = ("grp", "tile")

    edges = levels + levels // 2 + 2
    down, up = pl.pallas_call(
        functools.partial(edge_kernel, groups),
        out_shape=(f32(edges, rim, 128),) * 2,
        in_specs=[HBM] * 4,
        scratch_shapes=[
            pltpu.VMEM((height, width), jnp.int32),
            pltpu.SemaphoreType.DMA((1 + 12 * cols,)),
        ],
        compiler_params=params(60),
        cost_estimate=cost(10),
    )(state, vert_coef, horiz_coef, wet_mask)
    above = lax.ppermute(down, axes, pairs)
    below = lax.ppermute(up, axes, back)

    packed = pl.pallas_call(
        functools.partial(pack_kernel, tiles, slots, groups),
        out_shape=(f32(2 * (F * slots + 16), 128),) * (tiles // 2),
        in_specs=[HBM] * 8,
        scratch_shapes=[
            pltpu.VMEM((blocks * K, F * 128), jnp.float32),
            pltpu.VMEM((cols, height, K, 128, 128), jnp.bfloat16),
        ]
        + [pltpu.VMEM((K, blocks), jnp.int32)] * 3
        + [pltpu.VMEM((height, width), jnp.float32)]
        + [pltpu.VMEM((F, height, width), jnp.float32)] * 2
        + [
            pltpu.VMEM((height, width), jnp.int32),
            pltpu.SemaphoreType.DMA((cols,)),
            pltpu.SemaphoreType.DMA((7,)),
        ],
        compiler_params=params(60),
        cost_estimate=cost(3),
    )(
        state,
        coupling,
        surface_in,
        wet_mask,
        dest_tile.T,
        dest_block.T,
        dest_group.T,
        remap_w.reshape(height, cols, K, 128, 128),
    )
    got = [packed[0]] + [
        lax.ppermute(packed[k], "tile", [(i, ((i // 2) ^ k) * 2 + i % 2) for i in range(tiles)])
        for k in range(1, tiles // 2)
    ]

    full, halo = f32(levels, height, width), f32(levels, rim, 128)
    scratch = [pltpu.VMEM(s.shape, jnp.float32) for s in [full] * 5 + [halo] * 4]
    parts, halo_wet = pl.pallas_call(
        functools.partial(solve_kernel, tiles, groups),
        out_shape=(f32(6, levels, height, width), f32(rim, 128)),
        scratch_shapes=scratch,
        compiler_params=params(24),
        cost_estimate=cost(8),
    )(state, vert_coef, horiz_coef, wet_mask, down, up, above, below)

    rows = (groups - 1) * (F * blocks + rim)
    mine, theirs = pl.pallas_call(
        functools.partial(merge_kernel, slots, height, cols, groups),
        out_shape=(f32(rows, 128),) * 2,
        compiler_params=params(8),
        cost_estimate=cost(1),
    )(halo_wet, *got)
    theirs = lax.ppermute(theirs, "tile", [(i, i ^ 1) for i in range(tiles)])
    merged = pl.pallas_call(
        functools.partial(add_kernel, cols),
        out_shape=(f32(F * blocks + rim, 128),) * (groups - 1),
        compiler_params=params(8),
        cost_estimate=cost(1),
    )(mine, theirs)
    arrived = [
        lax.ppermute(merged[g], "grp", [(g, groups - 1), (groups - 1, g)])
        for g in range(groups - 1)
    ]
    return pl.pallas_call(
        functools.partial(last_kernel, cols, groups),
        out_shape=(full, f32(F, height, width)),
        out_specs=(HBM, VM),
        scratch_shapes=[
            pltpu.VMEM((levels, height, width), jnp.float32),
            pltpu.SemaphoreType.DMA((4,)),
        ],
        compiler_params=params(16),
    )(wet_mask, parts, halo_wet, *arrived)


def solution(mesh):
    in_specs = (
        P(None, ("grp", "tile"), None),
        P(None, ("grp", "tile"), None),
        P(("grp", "tile"), None),
        P("tile", None),
        P(None, ("grp", "tile"), None),
        P(None, ("grp", "tile"), None),
        P(("grp", "tile"), None, None, None),
        P(("grp", "tile"), None),
        P(("grp", "tile"), None),
        P(("grp", "tile"), None),
    )
    out_specs = (P(None, ("grp", "tile"), None), P(None, ("grp", "tile"), None))
    return jax.shard_map(local, mesh=mesh, in_specs=in_specs, out_specs=out_specs, check_vma=False)
```

time: 53.9 us -> 50.8 us (0.942)
  the two profiles are of different devices: /device:TPU:14 before, /device:TPU:4 now
where the time goes in v4:
time: 50.8 us; the launch traced here: 50.1 us
  starting transfers between devices  23 us (45%)
  Pallas kernels  19.1 us (38%)
  waiting for transfers between devices  4.22 us (8%)
  local copies, waits for them, and re-layouts  2.92 us (6%)
  between operations  0.81 us (2%)
    pallas_call x1, Pallas kernels, local(): pl.pallas_call(functools.partial(solve_kernel, tiles, groups), out_shape=...  10.2 us
    ppermute x3, starting transfers between devices, local(): lax.ppermute(merged[g], 'grp', [(g, groups - 1), (groups - 1, g)])  9.35 us
    ppermute x1, starting transfers between devices, local(): below = lax.ppermute(up, axes, back)  7.24 us
    ppermute x3, starting transfers between devices, local(): lax.ppermute(packed[k], 'tile', [(i, (i // 2 ^ k) * 2 + i % 2) for i in r...  4.44 us
    pallas_call x1, Pallas kernels, local(): pl.pallas_call(functools.partial(pack_kernel, tiles, slots, groups), out_...  4.05 us
    unnamed x14, local copies, waits for them, and re-layouts  2.92 us
    pallas_call x1, Pallas kernels, local(): pl.pallas_call(functools.partial(edge_kernel, groups), out_shape=(f32(edg...  2.63 us
    ppermute x3, waiting for transfers between devices, local(): lax.ppermute(merged[g], 'grp', [(g, groups - 1), (groups - 1, g)])  2.39 us
  transfers between devices with their start and end apart: 9, of which 3 were waited for; matrix products, arithmetic and copies ran while one was open for 0% of the time, Pallas kernels for 28%

profile of v4, /device:TPU:4, one launch (start us, length us, event | category | flops | bytes accessed | tf_op | source)
XLA Modules:
  0.0 50.1 jit_solution(573902074649293767)
XLA Ops:
  0.6 0.0 copy-start
  0.7 0.0 copy-start.4
  0.7 2.6 %shard_map.113 = (f32[98,8,128]{2,1,0:T(8,128)}, f32[98,8,128]{2,1,0:T(8,128)}) custom-call(f32[64,8,512]{2,1,0:T(8,128)} %state.5, f32[63,8,512]{2,1,0:T(8,128)} %vert.3, f32[8,512]{1,0:T(8,128)} %horiz.3, s32[8,512]{1,0:T(8,128)} %mask.7), custom_call_target="tpu_custom_call" | custom-call | bytes 30000000 | tf_op jit(solution)/shard_map/pallas_call | solution.py:481
  3.3 1.9 %collective-permute-start = (f32[98,8,128]{2,1,0:T(8,128)}, f32[98,8,128]{2,1,0:T(8,128)S(1)}, u32[]{:S(2)}, u32[]{:S(2)}) collective-permute-start(f32[98,8,128]{2,1,0:T(8,128)} %get-tuple-element.15.down), channel_id=1, source_target_pairs={{0,1},{1,2},{2,3},{3,4},{4,5},{5,6},{6,7},{7,8},{8,9},{9,10},{10,1... | collective-permute-start | bytes 1204232 | tf_op jit(solution)/shard_map/ppermute | solution.py:492
  5.2 7.2 %collective-permute-start.1 = (f32[98,8,128]{2,1,0:T(8,128)}, f32[98,8,128]{2,1,0:T(8,128)S(1)}, u32[]{:S(2)}, u32[]{:S(2)}) collective-permute-start(f32[98,8,128]{2,1,0:T(8,128)} %get-tuple-element.16.up), channel_id=1, source_target_pairs={{1,0},{2,1},{3,2},{4,3},{5,4},{6,5},{7,6},{8,7},{9,8},{10,9},{11,1... | collective-permute-start | bytes 1204232 | tf_op jit(solution)/shard_map/ppermute | solution.py:493
  12.5 4.1 %shard_map.115 = (f32[288,128]{1,0:T(8,128)}, f32[288,128]{1,0:T(8,128)}, f32[288,128]{1,0:T(8,128)}, f32[288,128]{1,0:T(8,128)}) custom-call(f32[64,8,512]{2,1,0:T(8,128)} %state.5, f32[4,8,512]{2,1,0:T(8,128)} %coupling.1, f32[4,8,512]{2,1,0:T(8,128)} %surface.1, s32[8,512]{1,0:T(8,128)} %mask.7, s32[4,32]{1,0:T(4,128)} %bitcast.5, s32[4,32]{1,0:T(4,128)} %bitcast.6, ...), custom_call_target="tpu_custom_call" | custom-call | bytes 9000000 | tf_op jit(solution)/shard_map/pallas_call | solution.py:495
  16.5 0.1 collective-permute-start.2
  16.6 0.6 %collective-permute-start.3 = (f32[288,128]{1,0:T(8,128)}, f32[288,128]{1,0:T(8,128)S(1)}, u32[]{:S(2)}, u32[]{:S(2)}) collective-permute-start(f32[288,128]{1,0:T(8,128)} %get-tuple-element.21), channel_id=1, source_target_pairs={{0,4},{1,5},{2,6},{3,7},{4,0},{5,1},{6,2},{7,3},{8,12},{9,13},{10,... | collective-permute-start | bytes 442376 | tf_op jit(solution)/shard_map/ppermute | solution.py:524
  17.2 3.8 %collective-permute-start.4 = (f32[288,128]{1,0:T(8,128)}, f32[288,128]{1,0:T(8,128)S(1)}, u32[]{:S(2)}, u32[]{:S(2)}) collective-permute-start(f32[288,128]{1,0:T(8,128)} %get-tuple-element.22), channel_id=1, source_target_pairs={{0,6},{1,7},{2,4},{3,5},{4,2},{5,3},{6,0},{7,1},{8,14},{9,15},{10,... | collective-permute-start | bytes 442376 | tf_op jit(solution)/shard_map/ppermute | solution.py:524
  21.0 0.0 collective-permute-done.above
  21.0 0.4 collective-permute-done.1.below
  21.4 0.0 copy-done.1
  21.4 0.0 copy-done.4
  21.4 0.0 copy-start.2
  21.4 1.0 %copy-done.2 = f32[98,8,128]{2,1,0:T(8,128)S(1)} copy-done((f32[98,8,128]{2,1,0:T(8,128)S(1)}, f32[98,8,128]{2,1,0:T(8,128)}, u32[]{:S(2)}) %copy-start.2) | copy-done | bytes 401432
  22.4 1.0 %copy-done.3 = f32[98,8,128]{2,1,0:T(8,128)S(1)} copy-done((f32[98,8,128]{2,1,0:T(8,128)S(1)}, f32[98,8,128]{2,1,0:T(8,128)}, u32[]{:S(2)}) %copy-start.3) | copy-done | bytes 401432
  23.4 10.2 %shard_map.114 = (f32[6,64,8,512]{3,2,1,0:T(8,128)S(1)}, f32[8,128]{1,0:T(8,128)S(1)}) custom-call(f32[64,8,512]{2,1,0:T(8,128)S(1)} %copy-done, f32[63,8,512]{2,1,0:T(8,128)S(1)} %copy-done.1, f32[8,512]{1,0:T(8,128)S(1)} %copy-done.6, s32[8,512]{1,0:T(8,128)S(1)} %copy-done.4, f32[98,8,128]{2,1,0:T(8,128)S(1)} %copy-done.2, f32[98,8,128]{2,1,0:T(8,128)S(1)} %copy-done.3, ...), custom_call_target="tpu_custom_call" | custom-call | bytes 24000000 | tf_op jit(solution)/shard_map/pallas_call | solution.py:530
  33.6 0.0 collective-permute-done.2.refs_1_
  33.6 0.0 collective-permute-done.3.refs_2_
  33.6 0.0 collective-permute-done.4.refs_3_
  33.6 0.0 copy-start.5
  33.6 0.9 %copy-done.5 = f32[288,128]{1,0:T(8,128)S(1)} copy-done((f32[288,128]{1,0:T(8,128)S(1)}, f32[288,128]{1,0:T(8,128)}, u32[]{:S(2)}) %copy-start.5) | copy-done | bytes 147480
  34.5 0.3 shard_map.116
  34.8 0.1 collective-permute-start.5
  34.9 1.4 %collective-permute-done.5.theirs = f32[408,128]{1,0:T(8,128)S(1)} collective-permute-done((f32[408,128]{1,0:T(8,128)S(1)}, f32[408,128]{1,0:T(8,128)S(1)}, u32[]{:S(2)}, u32[]{:S(2)}) %collective-permute-start.5) | collective-permute-done | bytes 208928 | tf_op jit(solution)/shard_map/ppermute | solution.py:545
  36.4 0.7 %collective-permute-start.6 = (f32[136,128]{1,0:T(8,128)S(1)}, f32[136,128]{1,0:T(8,128)S(1)}, u32[]{:S(2)}, u32[]{:S(2)}) collective-permute-start(f32[136,128]{1,0:T(8,128)S(1)} %get-tuple-element.25), channel_id=1, source_target_pairs={{0,24},{24,0},{1,25},{25,1},{2,26},{26,2},{3,27},{27,3},{4,28},{28... | collective-permute-start | bytes 208904 | tf_op jit(solution)/shard_map/ppermute | solution.py:553
  37.0 0.7 %collective-permute-start.7 = (f32[136,128]{1,0:T(8,128)S(1)}, f32[136,128]{1,0:T(8,128)S(1)}, u32[]{:S(2)}, u32[]{:S(2)}) collective-permute-start(f32[136,128]{1,0:T(8,128)S(1)} %get-tuple-element.26), channel_id=1, source_target_pairs={{8,24},{24,8},{9,25},{25,9},{10,26},{26,10},{11,27},{27,11},{12,28... | collective-permute-start | bytes 208904 | tf_op jit(solution)/shard_map/ppermute | solution.py:553
  37.7 8.0 %collective-permute-start.8 = (f32[136,128]{1,0:T(8,128)S(1)}, f32[136,128]{1,0:T(8,128)S(1)}, u32[]{:S(2)}, u32[]{:S(2)}) collective-permute-start(f32[136,128]{1,0:T(8,128)S(1)} %get-tuple-element.27), channel_id=1, source_target_pairs={{16,24},{24,16},{17,25},{25,17},{18,26},{26,18},{19,27},{27,19},{2... | collective-permute-start | bytes 208904 | tf_op jit(solution)/shard_map/ppermute | solution.py:553
  45.7 0.0 collective-permute-done.6.refs_0_
  45.8 0.0 collective-permute-done.7.refs_1_
  45.8 2.4 %collective-permute-done.8.refs_2_ = f32[136,128]{1,0:T(8,128)S(1)} collective-permute-done((f32[136,128]{1,0:T(8,128)S(1)}, f32[136,128]{1,0:T(8,128)S(1)}, u32[]{:S(2)}, u32[]{:S(2)}) %collective-permute-start.8) | collective-permute-done | bytes 69664 | tf_op jit(solution)/shard_map/ppermute | solution.py:553
  48.2 1.9 %shard_map.118 = (f32[64,8,512]{2,1,0:T(8,128)}, f32[4,8,512]{2,1,0:T(8,128)}) custom-call(s32[8,512]{1,0:T(8,128)S(1)} %copy-done.4, f32[6,64,8,512]{3,2,1,0:T(8,128)S(1)} %get-tuple-element.17.parts, f32[8,128]{1,0:T(8,128)S(1)} %get-tuple-element.18._.halo_wet, f32[136,128]{1,0:T(8,128)S(1)} %collective-permute-done.6.refs_0_, ...), custom_call_target="tpu_custom_call" | custom-call | tf_op jit(solution)/shard_map/pallas_call | solution.py:556
  (6 shorter events, 0.0 us)
Async XLA Ops:
  0.6 20.7 %copy-start = (f32[64,8,512]{2,1,0:T(8,128)S(1)}, f32[64,8,512]{2,1,0:T(8,128)}, u32[]{:S(2)}) copy-start(f32[64,8,512]{2,1,0:T(8,128)} %state.5) | copy-start | bytes 3145732
  0.6 20.7 %copy-start.1 = (f32[63,8,512]{2,1,0:T(8,128)S(1)}, f32[63,8,512]{2,1,0:T(8,128)}, u32[]{:S(2)}) copy-start(f32[63,8,512]{2,1,0:T(8,128)} %vert.3) | copy-start | bytes 3096580
  0.7 20.7 %copy-start.6 = (f32[8,512]{1,0:T(8,128)S(1)}, f32[8,512]{1,0:T(8,128)}, u32[]{:S(2)}) copy-start(f32[8,512]{1,0:T(8,128)} %horiz.3) | copy-start | bytes 49156
  0.7 20.7 %copy-start.4 = (s32[8,512]{1,0:T(8,128)S(1)}, s32[8,512]{1,0:T(8,128)}, u32[]{:S(2)}) copy-start(s32[8,512]{1,0:T(8,128)} %mask.7) | copy-start | bytes 49156
  3.3 17.7 %collective-permute-start = (f32[98,8,128]{2,1,0:T(8,128)}, f32[98,8,128]{2,1,0:T(8,128)S(1)}, u32[]{:S(2)}, u32[]{:S(2)}) collective-permute-start(f32[98,8,128]{2,1,0:T(8,128)} %get-tuple-element.15.down), channel_id=1, source_target_pairs={{0,1},{1,2},{2,3},{3,4},{4,5},{5,6},{6,7},{7,8},{8,9},{9,10},{10,1... | collective-permute-start | bytes 1204232 | tf_op jit(solution)/shard_map/ppermute | solution.py:492
  5.2 16.1 %collective-permute-start.1 = (f32[98,8,128]{2,1,0:T(8,128)}, f32[98,8,128]{2,1,0:T(8,128)S(1)}, u32[]{:S(2)}, u32[]{:S(2)}) collective-permute-start(f32[98,8,128]{2,1,0:T(8,128)} %get-tuple-element.16.up), channel_id=1, source_target_pairs={{1,0},{2,1},{3,2},{4,3},{5,4},{6,5},{7,6},{8,7},{9,8},{10,9},{11,1... | collective-permute-start | bytes 1204232 | tf_op jit(solution)/shard_map/ppermute | solution.py:493
  16.5 17.1 %collective-permute-start.2 = (f32[288,128]{1,0:T(8,128)}, f32[288,128]{1,0:T(8,128)S(1)}, u32[]{:S(2)}, u32[]{:S(2)}) collective-permute-start(f32[288,128]{1,0:T(8,128)} %get-tuple-element.20), channel_id=1, source_target_pairs={{0,2},{1,3},{2,0},{3,1},{4,6},{5,7},{6,4},{7,5},{8,10},{9,11},{10,... | collective-permute-start | bytes 442376 | tf_op jit(solution)/shard_map/ppermute | solution.py:524
  16.6 17.0 %collective-permute-start.3 = (f32[288,128]{1,0:T(8,128)}, f32[288,128]{1,0:T(8,128)S(1)}, u32[]{:S(2)}, u32[]{:S(2)}) collective-permute-start(f32[288,128]{1,0:T(8,128)} %get-tuple-element.21), channel_id=1, source_target_pairs={{0,4},{1,5},{2,6},{3,7},{4,0},{5,1},{6,2},{7,3},{8,12},{9,13},{10,... | collective-permute-start | bytes 442376 | tf_op jit(solution)/shard_map/ppermute | solution.py:524
  17.2 16.4 %collective-permute-start.4 = (f32[288,128]{1,0:T(8,128)}, f32[288,128]{1,0:T(8,128)S(1)}, u32[]{:S(2)}, u32[]{:S(2)}) collective-permute-start(f32[288,128]{1,0:T(8,128)} %get-tuple-element.22), channel_id=1, source_target_pairs={{0,6},{1,7},{2,4},{3,5},{4,2},{5,3},{6,0},{7,1},{8,14},{9,15},{10,... | collective-permute-start | bytes 442376 | tf_op jit(solution)/shard_map/ppermute | solution.py:524
  21.4 1.0 %copy-start.2 = (f32[98,8,128]{2,1,0:T(8,128)S(1)}, f32[98,8,128]{2,1,0:T(8,128)}, u32[]{:S(2)}) copy-start(f32[98,8,128]{2,1,0:T(8,128)} %get-tuple-element.15.down) | copy-start | bytes 1204228
  22.4 1.0 %copy-start.3 = (f32[98,8,128]{2,1,0:T(8,128)S(1)}, f32[98,8,128]{2,1,0:T(8,128)}, u32[]{:S(2)}) copy-start(f32[98,8,128]{2,1,0:T(8,128)} %get-tuple-element.16.up) | copy-start | bytes 1204228
  33.6 0.9 %copy-start.5 = (f32[288,128]{1,0:T(8,128)S(1)}, f32[288,128]{1,0:T(8,128)}, u32[]{:S(2)}) copy-start(f32[288,128]{1,0:T(8,128)} %get-tuple-element.19.refs_0_) | copy-start | bytes 442372
  34.8 1.5 %collective-permute-start.5 = (f32[408,128]{1,0:T(8,128)S(1)}, f32[408,128]{1,0:T(8,128)S(1)}, u32[]{:S(2)}, u32[]{:S(2)}) collective-permute-start(f32[408,128]{1,0:T(8,128)S(1)} %get-tuple-element.24), channel_id=1, source_target_pairs={{0,1},{1,0},{2,3},{3,2},{4,5},{5,4},{6,7},{7,6},{8,9},{9,8},{10,11... | collective-permute-start | bytes 626696 | tf_op jit(solution)/shard_map/ppermute | solution.py:545
  36.4 9.4 %collective-permute-start.6 = (f32[136,128]{1,0:T(8,128)S(1)}, f32[136,128]{1,0:T(8,128)S(1)}, u32[]{:S(2)}, u32[]{:S(2)}) collective-permute-start(f32[136,128]{1,0:T(8,128)S(1)} %get-tuple-element.25), channel_id=1, source_target_pairs={{0,24},{24,0},{1,25},{25,1},{2,26},{26,2},{3,27},{27,3},{4,28},{28... | collective-permute-start | bytes 208904 | tf_op jit(solution)/shard_map/ppermute | solution.py:553
  37.0 8.7 %collective-permute-start.7 = (f32[136,128]{1,0:T(8,128)S(1)}, f32[136,128]{1,0:T(8,128)S(1)}, u32[]{:S(2)}, u32[]{:S(2)}) collective-permute-start(f32[136,128]{1,0:T(8,128)S(1)} %get-tuple-element.26), channel_id=1, source_target_pairs={{8,24},{24,8},{9,25},{25,9},{10,26},{26,10},{11,27},{27,11},{12,28... | collective-permute-start | bytes 208904 | tf_op jit(solution)/shard_map/ppermute | solution.py:553
  37.7 10.4 %collective-permute-start.8 = (f32[136,128]{1,0:T(8,128)S(1)}, f32[136,128]{1,0:T(8,128)S(1)}, u32[]{:S(2)}, u32[]{:S(2)}) collective-permute-start(f32[136,128]{1,0:T(8,128)S(1)} %get-tuple-element.27), channel_id=1, source_target_pairs={{16,24},{24,16},{17,25},{25,17},{18,26},{26,18},{19,27},{27,19},{2... | collective-permute-start | bytes 208904 | tf_op jit(solution)/shard_map/ppermute | solution.py:553

commit v5 on v4

--- a/solution.py
+++ b/solution.py
@@ -154,7 +154,7 @@
         out[at + rim : at + rim + 1, :] = tags[t : t + 1, :]
 
 
-def merge_kernel(slots, height, cols, groups, _, *refs):
+def merge_kernel(slots, height, cols, groups, *refs):
     got, (mine, theirs) = refs[:-2], refs[-2:]
     blocks = height * cols
     size = F * slots + 16
@@ -294,9 +294,14 @@
     )
 
 
+def inverse_of(x):
+    y = pl.reciprocal(x, approx=True)
+    return y * (2.0 - x * y)
+
+
 def solve_kernel(
-    tiles, groups, state, vert, horiz, mask, down, up, above, below, parts, halo_wet,
-    upper, gain, ratio, base, impulse, halo_base, halo_impulse, halo_vert, halo_upper,
+    tiles, groups, state, vert, horiz, mask, above, below, chunk, parts, halo_wet, chunk_out,
+    upper, gain, ratio, base, impulse, halo_base, halo_impulse, halo_vert, halo_upper, rim, sem,
 ):
     levels, height, width = state.shape
     cols = width // 128
@@ -314,9 +319,11 @@
     def behind(i):
         return turn(jnp.where(low_half, below[i], above[i]))
 
-    def inside(i):
-        return turn(jnp.where(low_half, down[i], up[i]))
-
+    copy = pltpu.make_async_copy(chunk, chunk_out, sem)
+    copy.start()
+    for c in range(cols):
+        rim[:, c, :] = state[:, 0, c * 128 : (c + 1) * 128]
+        rim[:, cols + c, :] = state[:, height - 1, c * 128 : (c + 1) * 128]
     wet = wet_of(lax.axis_index("grp") == groups - 1, mask[...])
     wet_halo = beside(levels + half)
     halo_wet[...] = wet_halo
@@ -329,7 +336,8 @@
     weight_left = scale * jnp.where((place == 0) & (lane == 0), 0.0, wet_left)
     weight_right = scale * jnp.where((place == cols - 1) & (lane == 127), 0.0, wet_right)
     weight_behind = scale * behind(levels + half)
-    weight_inside = scale * inside(levels + half)
+    wet_inside = [wet[r : r + 1, c * 128 : (c + 1) * 128] for r in (0, height - 1) for c in range(cols)]
+    weight_inside = scale * jnp.concatenate(wet_inside, 0)
 
     def spread(i, _):
         a, b = above[levels + i], below[levels + i]
@@ -344,7 +352,7 @@
     def forward(level, carry, last=False, first=False):
         low, c, r, e, low_h, c_h, r_h, e_h = carry
         upp = zero if last else vert[level] * wet
-        inverse = 1.0 / (1.0 + low + upp + low * c)
+        inverse = inverse_of(1.0 + low + upp + low * c)
         c = -upp * inverse
         step = low * inverse
         halo = beside(level)
@@ -356,7 +364,7 @@
         base[level] = r
         impulse[level] = e
         upp_h = zero_halo if last else halo_vert[level]
-        inverse = 1.0 / (1.0 + low_h + upp_h + low_h * c_h)
+        inverse = inverse_of(1.0 + low_h + upp_h + low_h * c_h)
         c_h = -upp_h * inverse
         step = low_h * inverse
         left, right = shifted(halo, lane)
@@ -365,7 +373,7 @@
             + weight_left * (left - halo)
             + weight_right * (right - halo)
             + weight_behind * (behind(level) - halo)
-            + weight_inside * (inside(level) - halo)
+            + weight_inside * (rim[level] - halo)
         )
         r_h = field * inverse + step * r_h
         e_h = inverse if first else step * e_h
@@ -375,7 +383,7 @@
         return upp, c, r, e, upp_h, c_h, r_h, e_h
 
     carry = forward(0, (zero,) * 4 + (zero_halo,) * 4, first=True)
-    carry = lax.fori_loop(1, levels - 1, forward, carry, unroll=2)
+    carry = lax.fori_loop(1, levels - 1, forward, carry, unroll=31)
     carry = forward(levels - 1, carry, last=True)
 
     def backward(i, carry):
@@ -391,7 +399,7 @@
         halo_impulse[level] = y_h
         return x, y, x_h, y_h
 
-    lax.fori_loop(0, levels - 1, backward, (carry[2], carry[3], carry[6], carry[7]), unroll=2)
+    lax.fori_loop(0, levels - 1, backward, (carry[2], carry[3], carry[6], carry[7]), unroll=9)
 
     rest = 1.0 - weights[0] - weights[1] - weights[2] - weights[3]
 
@@ -406,7 +414,7 @@
         return made
 
     carry = forward_parts(0, (zero,) * 6, first=True)
-    carry = lax.fori_loop(1, levels, forward_parts, carry)
+    carry = lax.fori_loop(1, levels, forward_parts, carry, unroll=7)
 
     def backward_parts(i, carry):
         level = levels - 2 - i
@@ -416,7 +424,8 @@
             parts[j, level] = made[j]
         return made
 
-    lax.fori_loop(0, levels - 1, backward_parts, carry, unroll=2)
+    lax.fori_loop(0, levels - 1, backward_parts, carry, unroll=9)
+    copy.wait()
 
 
 def last_kernel(cols, groups, mask, parts, halo_wet, *refs):
@@ -462,25 +471,12 @@
     return pl.CostEstimate(flops=0, bytes_accessed=int(us * 3e6), transcendentals=0)
 
 
-def local(
-    state, vert_coef, horiz_coef, wet_mask, coupling, surface_in, remap_w, dest_tile, dest_block, dest_group
-):
+def edges_of(groups, state, vert_coef, horiz_coef, wet_mask):
     levels, height, width = state.shape
-    groups, tiles = lax.axis_size("grp"), lax.axis_size("tile")
     cols = width // 128
-    blocks = height * cols
-    slots = max(8, 2 * blocks * K // tiles)
-    rim = 2 * cols
-    devices = groups * tiles
-    start = (groups - 1) * tiles
-    pairs = [(i, i + 1) for i in range(devices - 1) if i + 1 != start]
-    back = [(j, i) for i, j in pairs]
-    axes = ("grp", "tile")
-
-    edges = levels + levels // 2 + 2
-    down, up = pl.pallas_call(
+    return pl.pallas_call(
         functools.partial(edge_kernel, groups),
-        out_shape=(f32(edges, rim, 128),) * 2,
+        out_shape=(f32(levels + levels // 2 + 2, 2 * cols, 128),) * 2,
         in_specs=[HBM] * 4,
         scratch_shapes=[
             pltpu.VMEM((height, width), jnp.int32),
@@ -489,10 +485,13 @@
         compiler_params=params(60),
         cost_estimate=cost(10),
     )(state, vert_coef, horiz_coef, wet_mask)
-    above = lax.ppermute(down, axes, pairs)
-    below = lax.ppermute(up, axes, back)
-
-    packed = pl.pallas_call(
+
+
+def pack(groups, tiles, slots, state, coupling, surface, mask, dtile, dblock, dgroup, w):
+    height, width = mask.shape
+    cols = width // 128
+    blocks = height * cols
+    return pl.pallas_call(
         functools.partial(pack_kernel, tiles, slots, groups),
         out_shape=(f32(2 * (F * slots + 16), 128),) * (tiles // 2),
         in_specs=[HBM] * 8,
@@ -510,38 +509,72 @@
         ],
         compiler_params=params(60),
         cost_estimate=cost(3),
-    )(
-        state,
-        coupling,
-        surface_in,
-        wet_mask,
-        dest_tile.T,
-        dest_block.T,
-        dest_group.T,
-        remap_w.reshape(height, cols, K, 128, 128),
-    )
-    got = [packed[0]] + [
+    )(state, coupling, surface, mask, dtile.T, dblock.T, dgroup.T, w.reshape(height, cols, K, 128, 128))
+
+
+def solve(groups, tiles, state, vert_coef, horiz_coef, wet_mask, above, below, chunk):
+    levels, height, width = state.shape
+    full, halo = f32(levels, height, width), f32(levels, width // 64, 128)
+    scratch = [pltpu.VMEM(s.shape, jnp.float32) for s in [full] * 5 + [halo] * 5]
+    return pl.pallas_call(
+        functools.partial(solve_kernel, tiles, groups),
+        out_shape=(f32(6, levels, height, width), f32(width // 64, 128), f32(*chunk.shape)),
+        in_specs=[VM] * 6 + [HBM],
+        scratch_shapes=scratch + [pltpu.SemaphoreType.DMA],
+        compiler_params=params(24),
+        cost_estimate=cost(8),
+    )(state, vert_coef, horiz_coef, wet_mask, above, below, chunk)
+
+
+def finish(groups, wet_mask, parts, halo_wet, arrived):
+    _, levels, height, width = parts.shape
+    return pl.pallas_call(
+        functools.partial(last_kernel, width // 128, groups),
+        out_shape=(f32(levels, height, width), f32(F, height, width)),
+        out_specs=(HBM, VM),
+        scratch_shapes=[
+            pltpu.VMEM((levels, height, width), jnp.float32),
+            pltpu.SemaphoreType.DMA((4,)),
+        ],
+        compiler_params=params(16),
+    )(wet_mask, parts, halo_wet, *arrived)
+
+
+def local(
+    state, vert_coef, horiz_coef, wet_mask, coupling, surface_in, remap_w, dest_tile, dest_block, dest_group
+):
+    levels, height, width = state.shape
+    groups, tiles = lax.axis_size("grp"), lax.axis_size("tile")
+    cols = width // 128
+    blocks = height * cols
+    slots = max(8, 2 * blocks * K // tiles)
+    rim = 2 * cols
+    devices = groups * tiles
+    start = (groups - 1) * tiles
+    pairs = [(i, i + 1) for i in range(devices - 1) if i + 1 != start]
+    back = [(j, i) for i, j in pairs]
+    axes = ("grp", "tile")
+
+    down, up = edges_of(groups, state, vert_coef, horiz_coef, wet_mask)
+    above = lax.ppermute(down, axes, pairs)
+    below = lax.ppermute(up, axes, back)
+    packed = pack(
+        groups, tiles, slots, state, coupling, surface_in, wet_mask, dest_tile, dest_block, dest_group, remap_w
+    )
+    got = [
         lax.ppermute(packed[k], "tile", [(i, ((i // 2) ^ k) * 2 + i % 2) for i in range(tiles)])
         for k in range(1, tiles // 2)
     ]
-
-    full, halo = f32(levels, height, width), f32(levels, rim, 128)
-    scratch = [pltpu.VMEM(s.shape, jnp.float32) for s in [full] * 5 + [halo] * 4]
-    parts, halo_wet = pl.pallas_call(
-        functools.partial(solve_kernel, tiles, groups),
-        out_shape=(f32(6, levels, height, width), f32(rim, 128)),
-        scratch_shapes=scratch,
-        compiler_params=params(24),
-        cost_estimate=cost(8),
-    )(state, vert_coef, horiz_coef, wet_mask, down, up, above, below)
-
+    parts, halo_wet, chunk = solve(
+        groups, tiles, state, vert_coef, horiz_coef, wet_mask, above, below, packed[0]
+    )
     rows = (groups - 1) * (F * blocks + rim)
     mine, theirs = pl.pallas_call(
         functools.partial(merge_kernel, slots, height, cols, groups),
         out_shape=(f32(rows, 128),) * 2,
         compiler_params=params(8),
         cost_estimate=cost(1),
-    )(halo_wet, *got)
+    )(chunk, *got)
     theirs = lax.ppermute(theirs, "tile", [(i, i ^ 1) for i in range(tiles)])
     merged = pl.pallas_call(
         functools.partial(add_kernel, cols),
@@ -553,16 +586,7 @@
         lax.ppermute(merged[g], "grp", [(g, groups - 1), (groups - 1, g)])
         for g in range(groups - 1)
     ]
-    return pl.pallas_call(
-        functools.partial(last_kernel, cols, groups),
-        out_shape=(full, f32(F, height, width)),
-        out_specs=(HBM, VM),
-        scratch_shapes=[
-            pltpu.VMEM((levels, height, width), jnp.float32),
-            pltpu.SemaphoreType.DMA((4,)),
-        ],
-        compiler_params=params(16),
-    )(wet_mask, parts, halo_wet, *arrived)
+    return finish(groups, wet_mask, parts, halo_wet, arrived)
 
 
 def solution(mesh):

time: 50.8 us -> 45.9 us (0.904)
  the two profiles are of different devices: /device:TPU:4 before, /device:TPU:14 now
where the time goes in v5:
time: 45.9 us; the launch traced here: 45.6 us
  starting transfers between devices  17.1 us (37%)
  Pallas kernels  13.9 us (30%)
  waiting for transfers between devices  12.8 us (28%)
  local copies, waits for them, and re-layouts  0.92 us (2%)
  between operations  0.8 us (2%)
    ppermute x3, starting transfers between devices, local(): lax.ppermute(merged[g], 'grp', [(g, groups - 1), (groups - 1, g)])  7.97 us
    ppermute x3, waiting for transfers between devices, local(): lax.ppermute(packed[k], 'tile', [(i, (i // 2 ^ k) * 2 + i % 2) for i in r...  7.08 us
    pallas_call x1, Pallas kernels, solve(): pl.pallas_call(functools.partial(solve_kernel, tiles, groups), out_shape=...  5.09 us
    ppermute x3, waiting for transfers between devices, local(): lax.ppermute(merged[g], 'grp', [(g, groups - 1), (groups - 1, g)])  4.27 us
    pallas_call x1, Pallas kernels, pack(): pl.pallas_call(functools.partial(pack_kernel, tiles, slots, groups), out_...  4.03 us
    ppermute x1, starting transfers between devices, local(): below = lax.ppermute(up, axes, back)  3.64 us
    ppermute x3, starting transfers between devices, local(): lax.ppermute(packed[k], 'tile', [(i, (i // 2 ^ k) * 2 + i % 2) for i in r...  3.55 us
    pallas_call x1, Pallas kernels, edges_of(): pl.pallas_call(functools.partial(edge_kernel, groups), out_shape=(f32(lev...  2.63 us
  transfers between devices with their start and end apart: 9, of which 5 were waited for; matrix products, arithmetic and copies ran while one was open for 0% of the time, Pallas kernels for 20%

profile of v5, /device:TPU:14, one launch (start us, length us, event | category | flops | bytes accessed | tf_op | source)
XLA Modules:
  0.0 45.6 jit_solution(14915397049475333036)
XLA Ops:
  0.6 0.0 copy-start.2
  0.6 0.0 copy-start
  0.7 0.0 copy-start.4
  0.7 0.0 copy-start.1
  0.7 2.6 %shard_map.113 = (f32[98,8,128]{2,1,0:T(8,128)}, f32[98,8,128]{2,1,0:T(8,128)}) custom-call(f32[64,8,512]{2,1,0:T(8,128)} %state.5, f32[63,8,512]{2,1,0:T(8,128)} %vert.3, f32[8,512]{1,0:T(8,128)} %horiz.3, s32[8,512]{1,0:T(8,128)} %mask.7), custom_call_target="tpu_custom_call" | custom-call | bytes 30000000 | tf_op jit(solution)/shard_map/pallas_call | solution.py:477
  3.3 1.9 %collective-permute-start = (f32[98,8,128]{2,1,0:T(8,128)}, f32[98,8,128]{2,1,0:T(8,128)S(1)}, u32[]{:S(2)}, u32[]{:S(2)}) collective-permute-start(f32[98,8,128]{2,1,0:T(8,128)} %get-tuple-element.16), channel_id=1, source_target_pairs={{0,1},{1,2},{2,3},{3,4},{4,5},{5,6},{6,7},{7,8},{8,9},{9,10},{10,1... | collective-permute-start | bytes 1204232 | tf_op jit(solution)/shard_map/ppermute | solution.py:559
  5.2 3.6 %collective-permute-start.1 = (f32[98,8,128]{2,1,0:T(8,128)}, f32[98,8,128]{2,1,0:T(8,128)S(1)}, u32[]{:S(2)}, u32[]{:S(2)}) collective-permute-start(f32[98,8,128]{2,1,0:T(8,128)} %get-tuple-element.17), channel_id=1, source_target_pairs={{1,0},{2,1},{3,2},{4,3},{5,4},{6,5},{7,6},{8,7},{9,8},{10,9},{11,1... | collective-permute-start | bytes 1204232 | tf_op jit(solution)/shard_map/ppermute | solution.py:560
  8.9 4.0 %shard_map.114 = (f32[288,128]{1,0:T(8,128)}, f32[288,128]{1,0:T(8,128)}, f32[288,128]{1,0:T(8,128)}, f32[288,128]{1,0:T(8,128)}) custom-call(f32[64,8,512]{2,1,0:T(8,128)} %state.5, f32[4,8,512]{2,1,0:T(8,128)} %coupling.1, f32[4,8,512]{2,1,0:T(8,128)} %surface.1, s32[8,512]{1,0:T(8,128)} %mask.7, s32[4,32]{1,0:T(4,128)} %bitcast.5, s32[4,32]{1,0:T(4,128)} %bitcast.6, ...), custom_call_target="tpu_custom_call" | custom-call | bytes 9000000 | tf_op jit(solution)/shard_map/pallas_call | solution.py:494
  12.9 0.1 collective-permute-start.2
  13.0 3.0 %collective-permute-start.3 = (f32[288,128]{1,0:T(8,128)}, f32[288,128]{1,0:T(8,128)S(1)}, u32[]{:S(2)}, u32[]{:S(2)}) collective-permute-start(f32[288,128]{1,0:T(8,128)} %get-tuple-element.23), channel_id=1, source_target_pairs={{0,4},{1,5},{2,6},{3,7},{4,0},{5,1},{6,2},{7,3},{8,12},{9,13},{10,... | collective-permute-start | bytes 442376 | tf_op jit(solution)/shard_map/ppermute | solution.py:565
  16.0 0.4 collective-permute-start.4
  16.5 0.0 collective-permute-done.above
  16.5 0.0 collective-permute-done.1.below
  16.5 0.0 copy-done
  16.5 0.0 copy-done.4
  16.5 0.0 copy-done.1
  16.5 0.0 copy-start.3
  16.5 0.9 %copy-done.3 = f32[288,128]{1,0:T(8,128)S(1)} copy-done((f32[288,128]{1,0:T(8,128)S(1)}, f32[288,128]{1,0:T(8,128)}, u32[]{:S(2)}) %copy-start.3) | copy-done | bytes 147480
  17.4 5.1 %shard_map.115 = (f32[6,64,8,512]{3,2,1,0:T(8,128)S(1)}, f32[8,128]{1,0:T(8,128)S(1)}, f32[288,128]{1,0:T(8,128)S(1)}) custom-call(f32[64,8,512]{2,1,0:T(8,128)S(1)} %copy-done, f32[63,8,512]{2,1,0:T(8,128)S(1)} %copy-done.1, f32[8,512]{1,0:T(8,128)S(1)} %copy-done.4, s32[8,512]{1,0:T(8,128)S(1)} %copy-done.2, f32[98,8,128]{2,1,0:T(8,128)S(1)} %collective-permute-done.above, ...), custom_call_target="tpu_custom_call" | custom-call | bytes 24000000 | tf_op jit(solution)/shard_map/pallas_call | solution.py:519
  22.5 0.0 collective-permute-done.2.refs_1_
  22.5 4.2 %collective-permute-done.3.refs_2_ = f32[288,128]{1,0:T(8,128)S(1)} collective-permute-done((f32[288,128]{1,0:T(8,128)}, f32[288,128]{1,0:T(8,128)S(1)}, u32[]{:S(2)}, u32[]{:S(2)}) %collective-permute-start.3) | collective-permute-done | bytes 147488 | tf_op jit(solution)/shard_map/ppermute | solution.py:565
  26.7 2.9 %collective-permute-done.4.refs_3_ = f32[288,128]{1,0:T(8,128)S(1)} collective-permute-done((f32[288,128]{1,0:T(8,128)}, f32[288,128]{1,0:T(8,128)S(1)}, u32[]{:S(2)}, u32[]{:S(2)}) %collective-permute-start.4) | collective-permute-done | bytes 147488 | tf_op jit(solution)/shard_map/ppermute | solution.py:565
  29.6 0.3 shard_map.116
  29.9 0.1 collective-permute-start.5
  30.0 1.4 %collective-permute-done.5.theirs = f32[408,128]{1,0:T(8,128)S(1)} collective-permute-done((f32[408,128]{1,0:T(8,128)S(1)}, f32[408,128]{1,0:T(8,128)S(1)}, u32[]{:S(2)}, u32[]{:S(2)}) %collective-permute-start.5) | collective-permute-done | bytes 208928 | tf_op jit(solution)/shard_map/ppermute | solution.py:578
  31.5 4.1 %collective-permute-start.6 = (f32[136,128]{1,0:T(8,128)S(1)}, f32[136,128]{1,0:T(8,128)S(1)}, u32[]{:S(2)}, u32[]{:S(2)}) collective-permute-start(f32[136,128]{1,0:T(8,128)S(1)} %get-tuple-element.27), channel_id=1, source_target_pairs={{0,24},{24,0},{1,25},{25,1},{2,26},{26,2},{3,27},{27,3},{4,28},{28... | collective-permute-start | bytes 208904 | tf_op jit(solution)/shard_map/ppermute | solution.py:586
  35.6 1.9 %collective-permute-start.7 = (f32[136,128]{1,0:T(8,128)S(1)}, f32[136,128]{1,0:T(8,128)S(1)}, u32[]{:S(2)}, u32[]{:S(2)}) collective-permute-start(f32[136,128]{1,0:T(8,128)S(1)} %get-tuple-element.28), channel_id=1, source_target_pairs={{8,24},{24,8},{9,25},{25,9},{10,26},{26,10},{11,27},{27,11},{12,28... | collective-permute-start | bytes 208904 | tf_op jit(solution)/shard_map/ppermute | solution.py:586
  37.5 1.9 %collective-permute-start.8 = (f32[136,128]{1,0:T(8,128)S(1)}, f32[136,128]{1,0:T(8,128)S(1)}, u32[]{:S(2)}, u32[]{:S(2)}) collective-permute-start(f32[136,128]{1,0:T(8,128)S(1)} %get-tuple-element.29), channel_id=1, source_target_pairs={{16,24},{24,16},{17,25},{25,17},{18,26},{26,18},{19,27},{27,19},{2... | collective-permute-start | bytes 208904 | tf_op jit(solution)/shard_map/ppermute | solution.py:586
  39.4 0.0 collective-permute-done.6.refs_0_
  39.5 2.3 %collective-permute-done.7.refs_1_ = f32[136,128]{1,0:T(8,128)S(1)} collective-permute-done((f32[136,128]{1,0:T(8,128)S(1)}, f32[136,128]{1,0:T(8,128)S(1)}, u32[]{:S(2)}, u32[]{:S(2)}) %collective-permute-start.7) | collective-permute-done | bytes 69664 | tf_op jit(solution)/shard_map/ppermute | solution.py:586
  41.8 1.9 %collective-permute-done.8.refs_2_ = f32[136,128]{1,0:T(8,128)S(1)} collective-permute-done((f32[136,128]{1,0:T(8,128)S(1)}, f32[136,128]{1,0:T(8,128)S(1)}, u32[]{:S(2)}, u32[]{:S(2)}) %collective-permute-start.8) | collective-permute-done | bytes 69664 | tf_op jit(solution)/shard_map/ppermute | solution.py:586
  43.7 1.9 %shard_map.118 = (f32[64,8,512]{2,1,0:T(8,128)}, f32[4,8,512]{2,1,0:T(8,128)}) custom-call(s32[8,512]{1,0:T(8,128)S(1)} %copy-done.2, f32[6,64,8,512]{3,2,1,0:T(8,128)S(1)} %get-tuple-element.19.parts, f32[8,128]{1,0:T(8,128)S(1)} %get-tuple-element.20.halo_wet, f32[136,128]{1,0:T(8,128)S(1)} %collective-permute-done.6.refs_0_, ...), custom_call_target="tpu_custom_call" | custom-call | tf_op jit(solution)/shard_map/pallas_call | solution.py:531
  (2 shorter events, 0.0 us)
Async XLA Ops:
  0.6 15.9 %copy-start.2 = (s32[8,512]{1,0:T(8,128)S(1)}, s32[8,512]{1,0:T(8,128)}, u32[]{:S(2)}) copy-start(s32[8,512]{1,0:T(8,128)} %mask.7) | copy-start | bytes 49156
  0.6 15.8 %copy-start = (f32[64,8,512]{2,1,0:T(8,128)S(1)}, f32[64,8,512]{2,1,0:T(8,128)}, u32[]{:S(2)}) copy-start(f32[64,8,512]{2,1,0:T(8,128)} %state.5) | copy-start | bytes 3145732
  0.7 15.8 %copy-start.4 = (f32[8,512]{1,0:T(8,128)S(1)}, f32[8,512]{1,0:T(8,128)}, u32[]{:S(2)}) copy-start(f32[8,512]{1,0:T(8,128)} %horiz.3) | copy-start | bytes 49156
  0.7 15.8 %copy-start.1 = (f32[63,8,512]{2,1,0:T(8,128)S(1)}, f32[63,8,512]{2,1,0:T(8,128)}, u32[]{:S(2)}) copy-start(f32[63,8,512]{2,1,0:T(8,128)} %vert.3) | copy-start | bytes 3096580
  3.3 13.2 %collective-permute-start = (f32[98,8,128]{2,1,0:T(8,128)}, f32[98,8,128]{2,1,0:T(8,128)S(1)}, u32[]{:S(2)}, u32[]{:S(2)}) collective-permute-start(f32[98,8,128]{2,1,0:T(8,128)} %get-tuple-element.16), channel_id=1, source_target_pairs={{0,1},{1,2},{2,3},{3,4},{4,5},{5,6},{6,7},{7,8},{8,9},{9,10},{10,1... | collective-permute-start | bytes 1204232 | tf_op jit(solution)/shard_map/ppermute | solution.py:559
  5.2 11.2 %collective-permute-start.1 = (f32[98,8,128]{2,1,0:T(8,128)}, f32[98,8,128]{2,1,0:T(8,128)S(1)}, u32[]{:S(2)}, u32[]{:S(2)}) collective-permute-start(f32[98,8,128]{2,1,0:T(8,128)} %get-tuple-element.17), channel_id=1, source_target_pairs={{1,0},{2,1},{3,2},{4,3},{5,4},{6,5},{7,6},{8,7},{9,8},{10,9},{11,1... | collective-permute-start | bytes 1204232 | tf_op jit(solution)/shard_map/ppermute | solution.py:560
  12.9 9.6 %collective-permute-start.2 = (f32[288,128]{1,0:T(8,128)}, f32[288,128]{1,0:T(8,128)S(1)}, u32[]{:S(2)}, u32[]{:S(2)}) collective-permute-start(f32[288,128]{1,0:T(8,128)} %get-tuple-element.22), channel_id=1, source_target_pairs={{0,2},{1,3},{2,0},{3,1},{4,6},{5,7},{6,4},{7,5},{8,10},{9,11},{10,... | collective-permute-start | bytes 442376 | tf_op jit(solution)/shard_map/ppermute | solution.py:565
  13.0 13.7 %collective-permute-start.3 = (f32[288,128]{1,0:T(8,128)}, f32[288,128]{1,0:T(8,128)S(1)}, u32[]{:S(2)}, u32[]{:S(2)}) collective-permute-start(f32[288,128]{1,0:T(8,128)} %get-tuple-element.23), channel_id=1, source_target_pairs={{0,4},{1,5},{2,6},{3,7},{4,0},{5,1},{6,2},{7,3},{8,12},{9,13},{10,... | collective-permute-start | bytes 442376 | tf_op jit(solution)/shard_map/ppermute | solution.py:565
  16.0 13.6 %collective-permute-start.4 = (f32[288,128]{1,0:T(8,128)}, f32[288,128]{1,0:T(8,128)S(1)}, u32[]{:S(2)}, u32[]{:S(2)}) collective-permute-start(f32[288,128]{1,0:T(8,128)} %get-tuple-element.24), channel_id=1, source_target_pairs={{0,6},{1,7},{2,4},{3,5},{4,2},{5,3},{6,0},{7,1},{8,14},{9,15},{10,... | collective-permute-start | bytes 442376 | tf_op jit(solution)/shard_map/ppermute | solution.py:565
  16.5 0.9 %copy-start.3 = (f32[288,128]{1,0:T(8,128)S(1)}, f32[288,128]{1,0:T(8,128)}, u32[]{:S(2)}) copy-start(f32[288,128]{1,0:T(8,128)} %get-tuple-element.18.chunk) | copy-start | bytes 442372
  29.9 1.5 %collective-permute-start.5 = (f32[408,128]{1,0:T(8,128)S(1)}, f32[408,128]{1,0:T(8,128)S(1)}, u32[]{:S(2)}, u32[]{:S(2)}) collective-permute-start(f32[408,128]{1,0:T(8,128)S(1)} %get-tuple-element.26), channel_id=1, source_target_pairs={{0,1},{1,0},{2,3},{3,2},{4,5},{5,4},{6,7},{7,6},{8,9},{9,8},{10,11... | collective-permute-start | bytes 626696 | tf_op jit(solution)/shard_map/ppermute | solution.py:578
  31.5 8.0 %collective-permute-start.6 = (f32[136,128]{1,0:T(8,128)S(1)}, f32[136,128]{1,0:T(8,128)S(1)}, u32[]{:S(2)}, u32[]{:S(2)}) collective-permute-start(f32[136,128]{1,0:T(8,128)S(1)} %get-tuple-element.27), channel_id=1, source_target_pairs={{0,24},{24,0},{1,25},{25,1},{2,26},{26,2},{3,27},{27,3},{4,28},{28... | collective-permute-start | bytes 208904 | tf_op jit(solution)/shard_map/ppermute | solution.py:586
  35.6 6.2 %collective-permute-start.7 = (f32[136,128]{1,0:T(8,128)S(1)}, f32[136,128]{1,0:T(8,128)S(1)}, u32[]{:S(2)}, u32[]{:S(2)}) collective-permute-start(f32[136,128]{1,0:T(8,128)S(1)} %get-tuple-element.28), channel_id=1, source_target_pairs={{8,24},{24,8},{9,25},{25,9},{10,26},{26,10},{11,27},{27,11},{12,28... | collective-permute-start | bytes 208904 | tf_op jit(solution)/shard_map/ppermute | solution.py:586
  37.5 6.2 %collective-permute-start.8 = (f32[136,128]{1,0:T(8,128)S(1)}, f32[136,128]{1,0:T(8,128)S(1)}, u32[]{:S(2)}, u32[]{:S(2)}) collective-permute-start(f32[136,128]{1,0:T(8,128)S(1)} %get-tuple-element.29), channel_id=1, source_target_pairs={{16,24},{24,16},{17,25},{25,17},{18,26},{26,18},{19,27},{27,19},{2... | collective-permute-start | bytes 208904 | tf_op jit(solution)/shard_map/ppermute | solution.py:586

commit v6 on v5

--- a/solution.py
+++ b/solution.py
@@ -207,43 +207,49 @@
         out[rows + cols :, :] = jnp.where(even, near, far)
 
 
-def edge_kernel(groups, state, vert, horiz, mask, down, up, wet, sem):
+def edge_kernel(groups, state, vert, horiz, mask, chip, core, wet, sem):
     levels, height, width = state.shape
     half = levels // 2
     cols = width // 128
     last = height - 1
-    copies = [pltpu.make_async_copy(mask, wet, sem.at[0])]
-
-    def move(src, dst):
-        copies.append(pltpu.make_async_copy(src, dst, sem.at[len(copies)]))
-
-    for c in range(cols):
-        at, one, two = pl.ds(c * 128, 128), pl.ds(c, 1), pl.ds(cols + c, 1)
-        all_levels = pl.ds(0, levels)
-        move(state.at[:, pl.ds(last, 1), at], down.at[all_levels, one])
-        move(state.at[:, pl.ds(last - 1, 1), at], down.at[all_levels, two])
-        move(state.at[:, pl.ds(1, 1), at], up.at[all_levels, one])
-        move(state.at[:, pl.ds(0, 1), at], up.at[all_levels, two])
-        for out, row in ((down, pl.ds(last, 1)), (up, pl.ds(0, 1))):
-            move(vert.at[pl.ds(0, half), row, at], out.at[pl.ds(levels, half), one])
-            move(vert.at[pl.ds(half, half - 1), row, at], out.at[pl.ds(levels, half - 1), two])
-            move(horiz.at[row, at], out.at[levels + half + 1, one])
-            move(horiz.at[row, at], out.at[levels + half + 1, two])
-    for copy in copies:
-        copy.start()
-    copies[0].wait()
-    wet = wet_of(lax.axis_index("grp") == groups - 1, wet[...])
-    for c in range(cols):
-        at = slice(c * 128, (c + 1) * 128)
-        one, two = slice(c, c + 1), slice(cols + c, cols + c + 1)
-        down[levels + half, one, :] = wet[last:, at]
-        down[levels + half, two, :] = wet[last - 1 : last, at]
-        up[levels + half, one, :] = wet[1:2, at]
-        up[levels + half, two, :] = wet[:1, at]
-        for out in (down, up):
-            out[levels + half - 1, two, :] = jnp.zeros((1, 128), jnp.float32)
-    for copy in copies[1:]:
-        copy.wait()
+
+    def fill(down, up):
+        copies = [pltpu.make_async_copy(mask, wet, sem.at[0])]
+
+        def move(src, dst):
+            copies.append(pltpu.make_async_copy(src, dst, sem.at[len(copies)]))
+
+        for c in range(cols):
+            at, one, two = pl.ds(c * 128, 128), pl.ds(c, 1), pl.ds(cols + c, 1)
+            all_levels = pl.ds(0, levels)
+            move(state.at[:, pl.ds(last, 1), at], down.at[all_levels, one])
+            move(state.at[:, pl.ds(last - 1, 1), at], down.at[all_levels, two])
+            move(state.at[:, pl.ds(1, 1), at], up.at[all_levels, one])
+            move(state.at[:, pl.ds(0, 1), at], up.at[all_levels, two])
+            for out, row in ((down, pl.ds(last, 1)), (up, pl.ds(0, 1))):
+                move(vert.at[pl.ds(0, half), row, at], out.at[pl.ds(levels, half), one])
+                move(vert.at[pl.ds(half, half - 1), row, at], out.at[pl.ds(levels, half - 1), two])
+                move(horiz.at[row, at], out.at[levels + half + 1, one])
+                move(horiz.at[row, at], out.at[levels + half + 1, two])
+        for copy in copies:
+            copy.start()
+        copies[0].wait()
+        wet_here = wet_of(lax.axis_index("grp") == groups - 1, wet[...])
+        for c in range(cols):
+            at = slice(c * 128, (c + 1) * 128)
+            one, two = slice(c, c + 1), slice(cols + c, cols + c + 1)
+            down[levels + half, one, :] = wet_here[last:, at]
+            down[levels + half, two, :] = wet_here[last - 1 : last, at]
+            up[levels + half, one, :] = wet_here[1:2, at]
+            up[levels + half, two, :] = wet_here[:1, at]
+            for out in (down, up):
+                out[levels + half - 1, two, :] = jnp.zeros((1, 128), jnp.float32)
+        for copy in copies[1:]:
+            copy.wait()
+
+    even = lax.axis_index("tile") % 2 == 0
+    pl.when(even)(lambda: fill(core, chip))
+    pl.when(jnp.logical_not(even))(lambda: fill(chip, core))
 
 
 def weights_of(tiles, groups, horiz, wet, wet_above, wet_below):
@@ -300,7 +306,7 @@
 
 
 def solve_kernel(
-    tiles, groups, state, vert, horiz, mask, above, below, chunk, parts, halo_wet, chunk_out,
+    tiles, groups, state, vert, horiz, mask, chip, core, chunk, parts, halo_wet, chunk_out,
     upper, gain, ratio, base, impulse, halo_base, halo_impulse, halo_vert, halo_upper, rim, sem,
 ):
     levels, height, width = state.shape
@@ -309,15 +315,17 @@
     shape = (2 * cols, 128)
     low_half = iota(shape, 0) < cols
     lane = iota(shape, 1)
+    parity = lax.axis_index("tile") % 2
+    from_chip = iota(shape, 0) // cols == parity
 
     def turn(x):
         return pltpu.roll(x, cols, 0)
 
     def beside(i):
-        return jnp.where(low_half, above[i], below[i])
+        return jnp.where(from_chip, chip[i], core[i])
 
     def behind(i):
-        return turn(jnp.where(low_half, below[i], above[i]))
+        return turn(jnp.where(from_chip, core[i], chip[i]))
 
     copy = pltpu.make_async_copy(chunk, chunk_out, sem)
     copy.start()
@@ -340,7 +348,8 @@
     weight_inside = scale * jnp.concatenate(wet_inside, 0)
 
     def spread(i, _):
-        a, b = above[levels + i], below[levels + i]
+        x, y = chip[levels + i], core[levels + i]
+        a, b = jnp.where(parity == 0, x, y), jnp.where(parity == 0, y, x)
         halo_vert[i] = jnp.where(low_half, a, turn(b)) * wet_halo
         halo_vert[half + i] = jnp.where(low_half, turn(a), b) * wet_halo
         return 0
@@ -432,9 +441,10 @@
     arrived = refs[: groups - 1]
     out, received, field, sem = refs[groups - 1 :]
     _, levels, height, width = parts.shape
-    total = arrived[0][...]
-    for other in arrived[1:]:
-        total = total + other[...]
+    group = lax.axis_index("grp")
+    total = jnp.zeros(arrived[0].shape, jnp.float32)
+    for g, other in enumerate(arrived):
+        total = total + jnp.where((group == groups - 1) | (group == g), other[...], 0.0)
     for f in range(F):
         for c in range(cols):
             at = (f * cols + c) * height
@@ -512,7 +522,7 @@
     )(state, coupling, surface, mask, dtile.T, dblock.T, dgroup.T, w.reshape(height, cols, K, 128, 128))
 
 
-def solve(groups, tiles, state, vert_coef, horiz_coef, wet_mask, above, below, chunk):
+def solve(groups, tiles, state, vert_coef, horiz_coef, wet_mask, chip, core, chunk):
     levels, height, width = state.shape
     full, halo = f32(levels, height, width), f32(levels, width // 64, 128)
     scratch = [pltpu.VMEM(s.shape, jnp.float32) for s in [full] * 5 + [halo] * 5]
@@ -523,7 +533,7 @@
         scratch_shapes=scratch + [pltpu.SemaphoreType.DMA],
         compiler_params=params(24),
         cost_estimate=cost(8),
-    )(state, vert_coef, horiz_coef, wet_mask, above, below, chunk)
+    )(state, vert_coef, horiz_coef, wet_mask, chip, core, chunk)
 
 
 def finish(groups, wet_mask, parts, halo_wet, arrived):
@@ -551,22 +561,23 @@
     rim = 2 * cols
     devices = groups * tiles
     start = (groups - 1) * tiles
-    pairs = [(i, i + 1) for i in range(devices - 1) if i + 1 != start]
-    back = [(j, i) for i, j in pairs]
     axes = ("grp", "tile")
-
-    down, up = edges_of(groups, state, vert_coef, horiz_coef, wet_mask)
-    above = lax.ppermute(down, axes, pairs)
-    below = lax.ppermute(up, axes, back)
+    across = [(i, i + 1) for i in range(1, devices - 1, 2) if i + 1 != start]
+    across = across + [(j, i) for i, j in across]
+    chip, core = edges_of(groups, state, vert_coef, horiz_coef, wet_mask)
+    chip = lax.ppermute(chip, axes, across)
+    core = lax.ppermute(core, axes, [(i, i ^ 1) for i in range(devices)])
     packed = pack(
         groups, tiles, slots, state, coupling, surface_in, wet_mask, dest_tile, dest_block, dest_group, remap_w
     )
+    chips = tiles // 2
     got = [
         lax.ppermute(packed[k], "tile", [(i, ((i // 2) ^ k) * 2 + i % 2) for i in range(tiles)])
-        for k in range(1, tiles // 2)
+        for k in list(range(chips // 2, chips)) + list(range(1, chips // 2))
     ]
+    got = got[chips - chips // 2 :] + got[: chips - chips // 2]
     parts, halo_wet, chunk = solve(
-        groups, tiles, state, vert_coef, horiz_coef, wet_mask, above, below, packed[0]
+        groups, tiles, state, vert_coef, horiz_coef, wet_mask, chip, core, packed[0]
     )
     rows = (groups - 1) * (F * blocks + rim)
     mine, theirs = pl.pallas_call(
@@ -583,7 +594,7 @@
         cost_estimate=cost(1),
     )(mine, theirs)
     arrived = [
-        lax.ppermute(merged[g], "grp", [(g, groups - 1), (groups - 1, g)])
+        lax.ppermute(merged[g], "grp", [(j, (j + g + 1) % groups) for j in range(groups)])
         for g in range(groups - 1)
     ]
     return finish(groups, wet_mask, parts, halo_wet, arrived)

time: 45.9 us -> 41 us (0.89)
  the two profiles are of different devices: /device:TPU:14 before, /device:TPU:10 now
where the time goes in v6:
time: 41 us; the launch traced here: 40.8 us
  waiting for transfers between devices  15.8 us (39%)
  Pallas kernels  14 us (34%)
  starting transfers between devices  9.37 us (23%)
  local copies, waits for them, and re-layouts  0.92 us (2%)
  between operations  0.75 us (2%)
    ppermute x3, waiting for transfers between devices, local(): lax.ppermute(packed[k], 'tile', [(i, (i // 2 ^ k) * 2 + i % 2) for i in r...  8.82 us
    ppermute x3, waiting for transfers between devices, local(): lax.ppermute(merged[g], 'grp', [(j, (j + g + 1) % groups) for j in range(...  5.15 us
    pallas_call x1, Pallas kernels, solve(): pl.pallas_call(functools.partial(solve_kernel, tiles, groups), out_shape=...  5.12 us
    pallas_call x1, Pallas kernels, pack(): pl.pallas_call(functools.partial(pack_kernel, tiles, slots, groups), out_...  4.02 us
    ppermute x3, starting transfers between devices, local(): lax.ppermute(packed[k], 'tile', [(i, (i // 2 ^ k) * 2 + i % 2) for i in r...  3.55 us
    pallas_call x1, Pallas kernels, edges_of(): pl.pallas_call(functools.partial(edge_kernel, groups), out_shape=(f32(lev...  2.64 us
    ppermute x3, starting transfers between devices, local(): lax.ppermute(merged[g], 'grp', [(j, (j + g + 1) % groups) for j in range(...  2.08 us
    ppermute x1, starting transfers between devices, local(): chip = lax.ppermute(chip, axes, across)  1.92 us
  transfers between devices with their start and end apart: 9, of which 8 were waited for; matrix products, arithmetic and copies ran while one was open for 0% of the time, Pallas kernels for 22%

profile of v6, /device:TPU:10, one launch (start us, length us, event | category | flops | bytes accessed | tf_op | source)
XLA Modules:
  0.0 40.8 jit_solution(15964958734585858054)
XLA Ops:
  0.6 0.0 copy-start.2
  0.6 0.0 copy-start
  0.7 0.0 copy-start.4
  0.7 0.0 copy-start.1
  0.7 2.6 %shard_map.113 = (f32[98,8,128]{2,1,0:T(8,128)}, f32[98,8,128]{2,1,0:T(8,128)}) custom-call(f32[64,8,512]{2,1,0:T(8,128)} %state.5, f32[63,8,512]{2,1,0:T(8,128)} %vert.3, f32[8,512]{1,0:T(8,128)} %horiz.3, s32[8,512]{1,0:T(8,128)} %mask.7), custom_call_target="tpu_custom_call" | custom-call | bytes 30000000 | tf_op jit(solution)/shard_map/pallas_call | solution.py:487
  3.3 1.9 %collective-permute-start = (f32[98,8,128]{2,1,0:T(8,128)}, f32[98,8,128]{2,1,0:T(8,128)S(1)}, u32[]{:S(2)}, u32[]{:S(2)}) collective-permute-start(f32[98,8,128]{2,1,0:T(8,128)} %get-tuple-element.16), channel_id=1, source_target_pairs={{1,2},{3,4},{5,6},{7,8},{9,10},{11,12},{13,14},{15,16},{17,18},{19... | collective-permute-start | bytes 1204232 | tf_op jit(solution)/shard_map/ppermute | solution.py:568
  5.2 1.7 %collective-permute-start.1 = (f32[98,8,128]{2,1,0:T(8,128)}, f32[98,8,128]{2,1,0:T(8,128)S(1)}, u32[]{:S(2)}, u32[]{:S(2)}) collective-permute-start(f32[98,8,128]{2,1,0:T(8,128)} %get-tuple-element.17), channel_id=1, source_target_pairs={{0,1},{1,0},{2,3},{3,2},{4,5},{5,4},{6,7},{7,6},{8,9},{9,8},{10,11... | collective-permute-start | bytes 1204232 | tf_op jit(solution)/shard_map/ppermute | solution.py:569
  7.0 4.0 %shard_map.114 = (f32[288,128]{1,0:T(8,128)}, f32[288,128]{1,0:T(8,128)}, f32[288,128]{1,0:T(8,128)}, f32[288,128]{1,0:T(8,128)}) custom-call(f32[64,8,512]{2,1,0:T(8,128)} %state.5, f32[4,8,512]{2,1,0:T(8,128)} %coupling.1, f32[4,8,512]{2,1,0:T(8,128)} %surface.1, s32[8,512]{1,0:T(8,128)} %mask.7, s32[4,32]{1,0:T(4,128)} %bitcast.5, s32[4,32]{1,0:T(4,128)} %bitcast.6, ...), custom_call_target="tpu_custom_call" | custom-call | bytes 9000000 | tf_op jit(solution)/shard_map/pallas_call | solution.py:504
  11.0 1.9 %collective-permute-start.2 = (f32[288,128]{1,0:T(8,128)}, f32[288,128]{1,0:T(8,128)S(1)}, u32[]{:S(2)}, u32[]{:S(2)}) collective-permute-start(f32[288,128]{1,0:T(8,128)} %get-tuple-element.22), channel_id=1, source_target_pairs={{0,2},{1,3},{2,0},{3,1},{4,6},{5,7},{6,4},{7,5},{8,10},{9,11},{10,... | collective-permute-start | bytes 442376 | tf_op jit(solution)/shard_map/ppermute | solution.py:575
  12.9 1.2 %collective-permute-start.3 = (f32[288,128]{1,0:T(8,128)}, f32[288,128]{1,0:T(8,128)S(1)}, u32[]{:S(2)}, u32[]{:S(2)}) collective-permute-start(f32[288,128]{1,0:T(8,128)} %get-tuple-element.23), channel_id=1, source_target_pairs={{0,4},{1,5},{2,6},{3,7},{4,0},{5,1},{6,2},{7,3},{8,12},{9,13},{10,... | collective-permute-start | bytes 442376 | tf_op jit(solution)/shard_map/ppermute | solution.py:575
  14.1 0.4 %collective-permute-start.4 = (f32[288,128]{1,0:T(8,128)}, f32[288,128]{1,0:T(8,128)S(1)}, u32[]{:S(2)}, u32[]{:S(2)}) collective-permute-start(f32[288,128]{1,0:T(8,128)} %get-tuple-element.24), channel_id=1, source_target_pairs={{0,6},{1,7},{2,4},{3,5},{4,2},{5,3},{6,0},{7,1},{8,14},{9,15},{10,... | collective-permute-start | bytes 442376 | tf_op jit(solution)/shard_map/ppermute | solution.py:575
  14.6 0.4 collective-permute-done.chip
  14.9 0.0 collective-permute-done.1.core
  14.9 0.0 copy-done.2
  14.9 0.0 copy-done
  14.9 0.0 copy-done.4
  15.0 0.0 copy-done.1
  15.0 0.9 %copy-done.3 = f32[288,128]{1,0:T(8,128)S(1)} copy-done((f32[288,128]{1,0:T(8,128)S(1)}, f32[288,128]{1,0:T(8,128)}, u32[]{:S(2)}) %copy-start.3) | copy-done | bytes 147480
  15.9 5.1 %shard_map.115 = (f32[6,64,8,512]{3,2,1,0:T(8,128)S(1)}, f32[8,128]{1,0:T(8,128)S(1)}, f32[288,128]{1,0:T(8,128)S(1)}) custom-call(f32[64,8,512]{2,1,0:T(8,128)S(1)} %copy-done, f32[63,8,512]{2,1,0:T(8,128)S(1)} %copy-done.1, f32[8,512]{1,0:T(8,128)S(1)} %copy-done.4, s32[8,512]{1,0:T(8,128)S(1)} %copy-done.2, f32[98,8,128]{2,1,0:T(8,128)S(1)} %collective-permute-done.chip, ...), custom_call_target="tpu_custom_call" | custom-call | bytes 24000000 | tf_op jit(solution)/shard_map/pallas_call | solution.py:529
  21.0 1.3 %collective-permute-done.2.refs_1_ = f32[288,128]{1,0:T(8,128)S(1)} collective-permute-done((f32[288,128]{1,0:T(8,128)}, f32[288,128]{1,0:T(8,128)S(1)}, u32[]{:S(2)}, u32[]{:S(2)}) %collective-permute-start.2) | collective-permute-done | bytes 147488 | tf_op jit(solution)/shard_map/ppermute | solution.py:575
  22.3 4.0 %collective-permute-done.3.refs_2_ = f32[288,128]{1,0:T(8,128)S(1)} collective-permute-done((f32[288,128]{1,0:T(8,128)}, f32[288,128]{1,0:T(8,128)S(1)}, u32[]{:S(2)}, u32[]{:S(2)}) %collective-permute-start.3) | collective-permute-done | bytes 147488 | tf_op jit(solution)/shard_map/ppermute | solution.py:575
  26.2 3.6 %collective-permute-done.4.refs_3_ = f32[288,128]{1,0:T(8,128)S(1)} collective-permute-done((f32[288,128]{1,0:T(8,128)}, f32[288,128]{1,0:T(8,128)S(1)}, u32[]{:S(2)}, u32[]{:S(2)}) %collective-permute-start.4) | collective-permute-done | bytes 147488 | tf_op jit(solution)/shard_map/ppermute | solution.py:575
  29.8 0.3 shard_map.116
  30.1 0.1 collective-permute-start.5
  30.2 1.4 %collective-permute-done.5.theirs = f32[408,128]{1,0:T(8,128)S(1)} collective-permute-done((f32[408,128]{1,0:T(8,128)S(1)}, f32[408,128]{1,0:T(8,128)S(1)}, u32[]{:S(2)}, u32[]{:S(2)}) %collective-permute-start.5) | collective-permute-done | bytes 208928 | tf_op jit(solution)/shard_map/ppermute | solution.py:589
  31.7 1.0 %collective-permute-start.6 = (f32[136,128]{1,0:T(8,128)S(1)}, f32[136,128]{1,0:T(8,128)S(1)}, u32[]{:S(2)}, u32[]{:S(2)}) collective-permute-start(f32[136,128]{1,0:T(8,128)S(1)} %get-tuple-element.27), channel_id=1, source_target_pairs={{0,8},{8,16},{16,24},{24,0},{1,9},{9,17},{17,25},{25,1},{2,10},{10... | collective-permute-start | bytes 208904 | tf_op jit(solution)/shard_map/ppermute | solution.py:597
  32.7 1.0 %collective-permute-start.7 = (f32[136,128]{1,0:T(8,128)S(1)}, f32[136,128]{1,0:T(8,128)S(1)}, u32[]{:S(2)}, u32[]{:S(2)}) collective-permute-start(f32[136,128]{1,0:T(8,128)S(1)} %get-tuple-element.28), channel_id=1, source_target_pairs={{0,16},{8,24},{16,0},{24,8},{1,17},{9,25},{17,1},{25,9},{2,18},{10... | collective-permute-start | bytes 208904 | tf_op jit(solution)/shard_map/ppermute | solution.py:597
  33.7 0.1 collective-permute-start.8
  33.7 2.3 %collective-permute-done.6.refs_0_ = f32[136,128]{1,0:T(8,128)S(1)} collective-permute-done((f32[136,128]{1,0:T(8,128)S(1)}, f32[136,128]{1,0:T(8,128)S(1)}, u32[]{:S(2)}, u32[]{:S(2)}) %collective-permute-start.6) | collective-permute-done | bytes 69664 | tf_op jit(solution)/shard_map/ppermute | solution.py:597
  36.0 1.7 %collective-permute-done.7.refs_1_ = f32[136,128]{1,0:T(8,128)S(1)} collective-permute-done((f32[136,128]{1,0:T(8,128)S(1)}, f32[136,128]{1,0:T(8,128)S(1)}, u32[]{:S(2)}, u32[]{:S(2)}) %collective-permute-start.7) | collective-permute-done | bytes 69664 | tf_op jit(solution)/shard_map/ppermute | solution.py:597
  37.7 1.2 %collective-permute-done.8.refs_2_ = f32[136,128]{1,0:T(8,128)S(1)} collective-permute-done((f32[136,128]{1,0:T(8,128)S(1)}, f32[136,128]{1,0:T(8,128)S(1)}, u32[]{:S(2)}, u32[]{:S(2)}) %collective-permute-start.8) | collective-permute-done | bytes 69664 | tf_op jit(solution)/shard_map/ppermute | solution.py:597
  38.9 1.9 %shard_map.118 = (f32[64,8,512]{2,1,0:T(8,128)}, f32[4,8,512]{2,1,0:T(8,128)}) custom-call(s32[8,512]{1,0:T(8,128)S(1)} %copy-done.2, f32[6,64,8,512]{3,2,1,0:T(8,128)S(1)} %get-tuple-element.19.parts, f32[8,128]{1,0:T(8,128)S(1)} %get-tuple-element.20.halo_wet, f32[136,128]{1,0:T(8,128)S(1)} %collective-permute-done.6.refs_0_, ...), custom_call_target="tpu_custom_call" | custom-call | tf_op jit(solution)/shard_map/pallas_call | solution.py:541
  (2 shorter events, 0.0 us)
Async XLA Ops:
  0.6 14.3 %copy-start.2 = (s32[8,512]{1,0:T(8,128)S(1)}, s32[8,512]{1,0:T(8,128)}, u32[]{:S(2)}) copy-start(s32[8,512]{1,0:T(8,128)} %mask.7) | copy-start | bytes 49156
  0.6 14.3 %copy-start = (f32[64,8,512]{2,1,0:T(8,128)S(1)}, f32[64,8,512]{2,1,0:T(8,128)}, u32[]{:S(2)}) copy-start(f32[64,8,512]{2,1,0:T(8,128)} %state.5) | copy-start | bytes 3145732
  0.7 14.3 %copy-start.4 = (f32[8,512]{1,0:T(8,128)S(1)}, f32[8,512]{1,0:T(8,128)}, u32[]{:S(2)}) copy-start(f32[8,512]{1,0:T(8,128)} %horiz.3) | copy-start | bytes 49156
  0.7 14.3 %copy-start.1 = (f32[63,8,512]{2,1,0:T(8,128)S(1)}, f32[63,8,512]{2,1,0:T(8,128)}, u32[]{:S(2)}) copy-start(f32[63,8,512]{2,1,0:T(8,128)} %vert.3) | copy-start | bytes 3096580
  3.3 11.6 %collective-permute-start = (f32[98,8,128]{2,1,0:T(8,128)}, f32[98,8,128]{2,1,0:T(8,128)S(1)}, u32[]{:S(2)}, u32[]{:S(2)}) collective-permute-start(f32[98,8,128]{2,1,0:T(8,128)} %get-tuple-element.16), channel_id=1, source_target_pairs={{1,2},{3,4},{5,6},{7,8},{9,10},{11,12},{13,14},{15,16},{17,18},{19... | collective-permute-start | bytes 1204232 | tf_op jit(solution)/shard_map/ppermute | solution.py:568
  5.2 9.7 %collective-permute-start.1 = (f32[98,8,128]{2,1,0:T(8,128)}, f32[98,8,128]{2,1,0:T(8,128)S(1)}, u32[]{:S(2)}, u32[]{:S(2)}) collective-permute-start(f32[98,8,128]{2,1,0:T(8,128)} %get-tuple-element.17), channel_id=1, source_target_pairs={{0,1},{1,0},{2,3},{3,2},{4,5},{5,4},{6,7},{7,6},{8,9},{9,8},{10,11... | collective-permute-start | bytes 1204232 | tf_op jit(solution)/shard_map/ppermute | solution.py:569
  11.0 11.2 %collective-permute-start.2 = (f32[288,128]{1,0:T(8,128)}, f32[288,128]{1,0:T(8,128)S(1)}, u32[]{:S(2)}, u32[]{:S(2)}) collective-permute-start(f32[288,128]{1,0:T(8,128)} %get-tuple-element.22), channel_id=1, source_target_pairs={{0,2},{1,3},{2,0},{3,1},{4,6},{5,7},{6,4},{7,5},{8,10},{9,11},{10,... | collective-permute-start | bytes 442376 | tf_op jit(solution)/shard_map/ppermute | solution.py:575
  12.9 13.3 %collective-permute-start.3 = (f32[288,128]{1,0:T(8,128)}, f32[288,128]{1,0:T(8,128)S(1)}, u32[]{:S(2)}, u32[]{:S(2)}) collective-permute-start(f32[288,128]{1,0:T(8,128)} %get-tuple-element.23), channel_id=1, source_target_pairs={{0,4},{1,5},{2,6},{3,7},{4,0},{5,1},{6,2},{7,3},{8,12},{9,13},{10,... | collective-permute-start | bytes 442376 | tf_op jit(solution)/shard_map/ppermute | solution.py:575
  14.1 15.7 %collective-permute-start.4 = (f32[288,128]{1,0:T(8,128)}, f32[288,128]{1,0:T(8,128)S(1)}, u32[]{:S(2)}, u32[]{:S(2)}) collective-permute-start(f32[288,128]{1,0:T(8,128)} %get-tuple-element.24), channel_id=1, source_target_pairs={{0,6},{1,7},{2,4},{3,5},{4,2},{5,3},{6,0},{7,1},{8,14},{9,15},{10,... | collective-permute-start | bytes 442376 | tf_op jit(solution)/shard_map/ppermute | solution.py:575
  15.0 0.9 %copy-start.3 = (f32[288,128]{1,0:T(8,128)S(1)}, f32[288,128]{1,0:T(8,128)}, u32[]{:S(2)}) copy-start(f32[288,128]{1,0:T(8,128)} %get-tuple-element.18.chunk) | copy-start | bytes 442372
  30.1 1.5 %collective-permute-start.5 = (f32[408,128]{1,0:T(8,128)S(1)}, f32[408,128]{1,0:T(8,128)S(1)}, u32[]{:S(2)}, u32[]{:S(2)}) collective-permute-start(f32[408,128]{1,0:T(8,128)S(1)} %get-tuple-element.26), channel_id=1, source_target_pairs={{0,1},{1,0},{2,3},{3,2},{4,5},{5,4},{6,7},{7,6},{8,9},{9,8},{10,11... | collective-permute-start | bytes 626696 | tf_op jit(solution)/shard_map/ppermute | solution.py:589
  31.7 4.4 %collective-permute-start.6 = (f32[136,128]{1,0:T(8,128)S(1)}, f32[136,128]{1,0:T(8,128)S(1)}, u32[]{:S(2)}, u32[]{:S(2)}) collective-permute-start(f32[136,128]{1,0:T(8,128)S(1)} %get-tuple-element.27), channel_id=1, source_target_pairs={{0,8},{8,16},{16,24},{24,0},{1,9},{9,17},{17,25},{25,1},{2,10},{10... | collective-permute-start | bytes 208904 | tf_op jit(solution)/shard_map/ppermute | solution.py:597
  32.7 5.1 %collective-permute-start.7 = (f32[136,128]{1,0:T(8,128)S(1)}, f32[136,128]{1,0:T(8,128)S(1)}, u32[]{:S(2)}, u32[]{:S(2)}) collective-permute-start(f32[136,128]{1,0:T(8,128)S(1)} %get-tuple-element.28), channel_id=1, source_target_pairs={{0,16},{8,24},{16,0},{24,8},{1,17},{9,25},{17,1},{25,9},{2,18},{10... | collective-permute-start | bytes 208904 | tf_op jit(solution)/shard_map/ppermute | solution.py:597
  33.7 5.2 %collective-permute-start.8 = (f32[136,128]{1,0:T(8,128)S(1)}, f32[136,128]{1,0:T(8,128)S(1)}, u32[]{:S(2)}, u32[]{:S(2)}) collective-permute-start(f32[136,128]{1,0:T(8,128)S(1)} %get-tuple-element.29), channel_id=1, source_target_pairs={{0,24},{8,0},{16,8},{24,16},{1,25},{9,1},{17,9},{25,17},{2,26},{10... | collective-permute-start | bytes 208904 | tf_op jit(solution)/shard_map/ppermute | solution.py:597

commit v7 on v6

--- a/solution.py
+++ b/solution.py
@@ -207,49 +207,41 @@
         out[rows + cols :, :] = jnp.where(even, near, far)
 
 
-def edge_kernel(groups, state, vert, horiz, mask, chip, core, wet, sem):
+def edge_kernel(groups, state, vert, horiz, mask, _, chip, core):
     levels, height, width = state.shape
     half = levels // 2
     cols = width // 128
     last = height - 1
+    wet = wet_of(lax.axis_index("grp") == groups - 1, mask[...])
 
     def fill(down, up):
-        copies = [pltpu.make_async_copy(mask, wet, sem.at[0])]
-
-        def move(src, dst):
-            copies.append(pltpu.make_async_copy(src, dst, sem.at[len(copies)]))
-
-        for c in range(cols):
-            at, one, two = pl.ds(c * 128, 128), pl.ds(c, 1), pl.ds(cols + c, 1)
-            all_levels = pl.ds(0, levels)
-            move(state.at[:, pl.ds(last, 1), at], down.at[all_levels, one])
-            move(state.at[:, pl.ds(last - 1, 1), at], down.at[all_levels, two])
-            move(state.at[:, pl.ds(1, 1), at], up.at[all_levels, one])
-            move(state.at[:, pl.ds(0, 1), at], up.at[all_levels, two])
-            for out, row in ((down, pl.ds(last, 1)), (up, pl.ds(0, 1))):
-                move(vert.at[pl.ds(0, half), row, at], out.at[pl.ds(levels, half), one])
-                move(vert.at[pl.ds(half, half - 1), row, at], out.at[pl.ds(levels, half - 1), two])
-                move(horiz.at[row, at], out.at[levels + half + 1, one])
-                move(horiz.at[row, at], out.at[levels + half + 1, two])
-        for copy in copies:
-            copy.start()
-        copies[0].wait()
-        wet_here = wet_of(lax.axis_index("grp") == groups - 1, wet[...])
         for c in range(cols):
             at = slice(c * 128, (c + 1) * 128)
-            one, two = slice(c, c + 1), slice(cols + c, cols + c + 1)
-            down[levels + half, one, :] = wet_here[last:, at]
-            down[levels + half, two, :] = wet_here[last - 1 : last, at]
-            up[levels + half, one, :] = wet_here[1:2, at]
-            up[levels + half, two, :] = wet_here[:1, at]
-            for out in (down, up):
-                out[levels + half - 1, two, :] = jnp.zeros((1, 128), jnp.float32)
-        for copy in copies[1:]:
-            copy.wait()
+            for out, beside, behind, one, two in (
+                (down, last, last - 1, c, cols + c),
+                (up, 0, 1, cols + c, c),
+            ):
+                out[:levels, one, :] = state[:, beside, at]
+                out[:levels, two, :] = state[:, behind, at]
+                out[levels + half, one : one + 1, :] = wet[beside : beside + 1, at]
+                out[levels + half, two : two + 1, :] = wet[behind : behind + 1, at]
+                out[levels : levels + half, c, :] = vert[:half, beside, at]
+                out[levels : levels + half - 1, cols + c, :] = vert[half:, beside, at]
+                out[levels + half - 1, cols + c : cols + c + 1, :] = jnp.zeros((1, 128), jnp.float32)
+                for row in (c, cols + c):
+                    out[levels + half + 1, row : row + 1, :] = horiz[beside : beside + 1, at]
 
     even = lax.axis_index("tile") % 2 == 0
     pl.when(even)(lambda: fill(core, chip))
     pl.when(jnp.logical_not(even))(lambda: fill(chip, core))
+
+
+def side_weights(horiz, wet):
+    height, width = wet.shape
+    column = iota((height, width), 1)
+    left = jnp.where(column == 0, 0.0, pltpu.roll(wet, 1, 1))
+    right = jnp.where(column == width - 1, 0.0, pltpu.roll(wet, width - 1, 1))
+    return horiz * wet * left, horiz * wet * right
 
 
 def weights_of(tiles, groups, horiz, wet, wet_above, wet_below):
@@ -262,25 +254,30 @@
     below = jnp.concatenate([wet[1:], wet_below], 0)
     above = jnp.where((rows > 0) & (rows != start), above, 0.0)
     below = jnp.where((rows < last) & (rows + 1 != start), below, 0.0)
-    column = iota((height, width), 1)
-    left = jnp.where(column == 0, 0.0, pltpu.roll(wet, 1, 1))
-    right = jnp.where(column == width - 1, 0.0, pltpu.roll(wet, width - 1, 1))
     scale = horiz * wet
-    return scale * left, scale * right, scale * above, scale * below
+    return side_weights(horiz, wet) + (scale * above, scale * below)
 
 
 def line_of(halo, first, cols):
     return jnp.concatenate([halo[first + c : first + c + 1, :] for c in range(cols)], 1)
 
 
+def row_above(field, halo):
+    return jnp.concatenate([line_of(halo, 0, field.shape[1] // 128), field[:-1]], 0)
+
+
+def row_below(field, halo):
+    cols = field.shape[1] // 128
+    return jnp.concatenate([field[1:], line_of(halo, cols, cols)], 0)
+
+
 def around(field, halo):
-    height, width = field.shape
-    cols = width // 128
+    width = field.shape[1]
     return (
         pltpu.roll(field, 1, 1),
         pltpu.roll(field, width - 1, 1),
-        jnp.concatenate([line_of(halo, 0, cols), field[:-1]], 0),
-        jnp.concatenate([field[1:], line_of(halo, cols, cols)], 0),
+        row_above(field, halo),
+        row_below(field, halo),
     )
 
 
@@ -305,9 +302,72 @@
     return y * (2.0 - x * y)
 
 
-def solve_kernel(
-    tiles, groups, state, vert, horiz, mask, chip, core, chunk, parts, halo_wet, chunk_out,
-    upper, gain, ratio, base, impulse, halo_base, halo_impulse, halo_vert, halo_upper, rim, sem,
+def early_kernel(
+    groups, vert, horiz, mask, chunk, upper, gain, ratio, impulse, sides, chunk_out, sem
+):
+    levels, height, width = upper.shape
+    copy = pltpu.make_async_copy(chunk, chunk_out, sem)
+    copy.start()
+    wet = wet_of(lax.axis_index("grp") == groups - 1, mask[...])
+    weights = side_weights(horiz[...], wet)
+    zero = jnp.zeros((height, width), jnp.float32)
+
+    def forward(level, carry, last=False, first=False):
+        low, c, e = carry
+        upp = zero if last else vert[level] * wet
+        inverse = inverse_of(1.0 + low + upp + low * c)
+        c = -upp * inverse
+        step = low * inverse
+        e = inverse if first else step * e
+        upper[level] = c
+        gain[level] = inverse
+        ratio[level] = step
+        impulse[level] = e
+        return upp, c, e
+
+    carry = forward(0, (zero,) * 3, first=True)
+    carry = lax.fori_loop(1, levels - 1, forward, carry, unroll=31)
+    _, _, e = forward(levels - 1, carry, last=True)
+
+    def backward(i, x):
+        level = levels - 2 - i
+        x = impulse[level] - upper[level] * x
+        impulse[level] = x
+        return x
+
+    lax.fori_loop(0, levels - 1, backward, e, unroll=9)
+
+    def forward_parts(level, carry):
+        g = impulse[level]
+        rhs = (weights[0] * pltpu.roll(g, 1, 1), weights[1] * pltpu.roll(g, width - 1, 1))
+        inverse, step = gain[level], ratio[level]
+        made = tuple(x * inverse + step * r for x, r in zip(rhs, carry))
+        for i in range(2):
+            sides[i, level] = made[i]
+        return made
+
+    carry = lax.fori_loop(0, levels, forward_parts, (zero,) * 2, unroll=8)
+    back_parts(sides, upper, carry)
+    copy.wait()
+
+
+def back_parts(parts, upper, carry):
+    count, levels = parts.shape[:2]
+
+    def backward(i, carry):
+        level = levels - 2 - i
+        c = upper[level]
+        made = tuple(parts[j, level] - c * carry[j] for j in range(count))
+        for j in range(count):
+            parts[j, level] = made[j]
+        return made
+
+    lax.fori_loop(0, levels - 1, backward, carry, unroll=9)
+
+
+def late_kernel(
+    tiles, groups, state, horiz, mask, chip, core, upper, gain, ratio, impulse, _, parts, halo_wet,
+    base, halo_base, halo_impulse, halo_vert, halo_upper, rim,
 ):
     levels, height, width = state.shape
     cols = width // 128
@@ -327,8 +387,6 @@
     def behind(i):
         return turn(jnp.where(from_chip, core[i], chip[i]))
 
-    copy = pltpu.make_async_copy(chunk, chunk_out, sem)
-    copy.start()
     for c in range(cols):
         rim[:, c, :] = state[:, 0, c * 128 : (c + 1) * 128]
         rim[:, cols + c, :] = state[:, height - 1, c * 128 : (c + 1) * 128]
@@ -359,23 +417,14 @@
     zero_halo = jnp.zeros(shape, jnp.float32)
 
     def forward(level, carry, last=False, first=False):
-        low, c, r, e, low_h, c_h, r_h, e_h = carry
-        upp = zero if last else vert[level] * wet
+        r, low, c, x, e = carry
+        halo = beside(level)
+        r = stencil(state[level], halo, weights) * gain[level] + ratio[level] * r
+        base[level] = r
+        upp = zero_halo if last else halo_vert[level]
         inverse = inverse_of(1.0 + low + upp + low * c)
         c = -upp * inverse
         step = low * inverse
-        halo = beside(level)
-        r = stencil(state[level], halo, weights) * inverse + step * r
-        e = inverse if first else step * e
-        upper[level] = c
-        gain[level] = inverse
-        ratio[level] = step
-        base[level] = r
-        impulse[level] = e
-        upp_h = zero_halo if last else halo_vert[level]
-        inverse = inverse_of(1.0 + low_h + upp_h + low_h * c_h)
-        c_h = -upp_h * inverse
-        step = low_h * inverse
         left, right = shifted(halo, lane)
         field = (
             halo
@@ -384,60 +433,51 @@
             + weight_behind * (behind(level) - halo)
             + weight_inside * (rim[level] - halo)
         )
-        r_h = field * inverse + step * r_h
-        e_h = inverse if first else step * e_h
-        halo_upper[level] = c_h
-        halo_base[level] = r_h
-        halo_impulse[level] = e_h
-        return upp, c, r, e, upp_h, c_h, r_h, e_h
-
-    carry = forward(0, (zero,) * 4 + (zero_halo,) * 4, first=True)
+        x = field * inverse + step * x
+        e = inverse if first else step * e
+        halo_upper[level] = c
+        halo_base[level] = x
+        halo_impulse[level] = e
+        return r, upp, c, x, e
+
+    carry = forward(0, (zero,) + (zero_halo,) * 4, first=True)
     carry = lax.fori_loop(1, levels - 1, forward, carry, unroll=31)
-    carry = forward(levels - 1, carry, last=True)
+    r, _, _, x, e = forward(levels - 1, carry, last=True)
 
     def backward(i, carry):
         level = levels - 2 - i
-        c, c_h = upper[level], halo_upper[level]
-        x = base[level] - c * carry[0]
-        y = impulse[level] - c * carry[1]
-        x_h = halo_base[level] - c_h * carry[2]
-        y_h = halo_impulse[level] - c_h * carry[3]
-        base[level] = x
-        impulse[level] = y
-        halo_base[level] = x_h
-        halo_impulse[level] = y_h
-        return x, y, x_h, y_h
-
-    lax.fori_loop(0, levels - 1, backward, (carry[2], carry[3], carry[6], carry[7]), unroll=9)
-
+        c = halo_upper[level]
+        r = base[level] - upper[level] * carry[0]
+        x = halo_base[level] - c * carry[1]
+        e = halo_impulse[level] - c * carry[2]
+        base[level] = r
+        halo_base[level] = x
+        halo_impulse[level] = e
+        return r, x, e
+
+    lax.fori_loop(0, levels - 1, backward, (r, x, e), unroll=9)
     rest = 1.0 - weights[0] - weights[1] - weights[2] - weights[3]
 
     def forward_parts(level, carry, first=False):
-        g = impulse[level]
-        rhs = [stencil(base[level], halo_base[level], weights), rest * g + (1.0 if first else 0.0)]
-        rhs += [w * x for w, x in zip(weights, around(g, halo_impulse[level]))]
+        g, halo = impulse[level], halo_impulse[level]
+        rhs = (
+            stencil(base[level], halo_base[level], weights),
+            rest * g + (1.0 if first else 0.0),
+            weights[2] * row_above(g, halo),
+            weights[3] * row_below(g, halo),
+        )
         inverse, step = gain[level], ratio[level]
         made = tuple(x * inverse + step * r for x, r in zip(rhs, carry))
-        for i in range(6):
+        for i in range(4):
             parts[i, level] = made[i]
         return made
 
-    carry = forward_parts(0, (zero,) * 6, first=True)
+    carry = forward_parts(0, (zero,) * 4, first=True)
     carry = lax.fori_loop(1, levels, forward_parts, carry, unroll=7)
-
-    def backward_parts(i, carry):
-        level = levels - 2 - i
-        c = upper[level]
-        made = tuple(parts[j, level] - c * carry[j] for j in range(6))
-        for j in range(6):
-            parts[j, level] = made[j]
-        return made
-
-    lax.fori_loop(0, levels - 1, backward_parts, carry, unroll=9)
-    copy.wait()
-
-
-def last_kernel(cols, groups, mask, parts, halo_wet, *refs):
+    back_parts(parts, upper, carry)
+
+
+def last_kernel(cols, groups, mask, sides, parts, halo_wet, *refs):
     arrived = refs[: groups - 1]
     out, received, field, sem = refs[groups - 1 :]
     _, levels, height, width = parts.shape
@@ -452,13 +492,12 @@
     wet = wet_of(lax.axis_index("grp") == groups - 1, mask[...])
     force = FORCING_GAIN * wet * jnp.sum(received[...], 0)
     force_halo = FORCING_GAIN * halo_wet[...] * total[F * cols * height :, :]
-    factors = (force,) + around(force, force_halo)
+    left, right, above, below = around(force, force_halo)
 
     def level_of(level, _):
-        x = parts[0, level]
-        for i in range(5):
-            x = x + parts[i + 1, level] * factors[i]
-        field[level] = x
+        x = parts[0, level] + parts[1, level] * force
+        x = x + parts[2, level] * above + parts[3, level] * below
+        field[level] = x + sides[0, level] * left + sides[1, level] * right
         return 0
 
     chunks = 4
@@ -481,20 +520,15 @@
     return pl.CostEstimate(flops=0, bytes_accessed=int(us * 3e6), transcendentals=0)
 
 
-def edges_of(groups, state, vert_coef, horiz_coef, wet_mask):
+def edges_of(groups, state, vert_coef, horiz_coef, wet_mask, after):
     levels, height, width = state.shape
-    cols = width // 128
     return pl.pallas_call(
         functools.partial(edge_kernel, groups),
-        out_shape=(f32(levels + levels // 2 + 2, 2 * cols, 128),) * 2,
-        in_specs=[HBM] * 4,
-        scratch_shapes=[
-            pltpu.VMEM((height, width), jnp.int32),
-            pltpu.SemaphoreType.DMA((1 + 12 * cols,)),
-        ],
-        compiler_params=params(60),
-        cost_estimate=cost(10),
-    )(state, vert_coef, horiz_coef, wet_mask)
+        out_shape=(f32(levels + levels // 2 + 2, width // 64, 128),) * 2,
+        in_specs=[VM] * 4 + [HBM],
+        compiler_params=params(8),
+        cost_estimate=cost(1),
+    )(state, vert_coef, horiz_coef, wet_mask, after)
 
 
 def pack(groups, tiles, slots, state, coupling, surface, mask, dtile, dblock, dgroup, w):
@@ -522,21 +556,33 @@
     )(state, coupling, surface, mask, dtile.T, dblock.T, dgroup.T, w.reshape(height, cols, K, 128, 128))
 
 
-def solve(groups, tiles, state, vert_coef, horiz_coef, wet_mask, chip, core, chunk):
+def early(groups, vert_coef, horiz_coef, wet_mask, chunk):
+    levels, height, width = vert_coef.shape
+    full = f32(levels + 1, height, width)
+    return pl.pallas_call(
+        functools.partial(early_kernel, groups),
+        out_shape=(full,) * 4 + (f32(2, levels + 1, height, width), f32(*chunk.shape)),
+        in_specs=[VM] * 3 + [HBM],
+        scratch_shapes=[pltpu.SemaphoreType.DMA],
+        compiler_params=params(16),
+        cost_estimate=cost(3),
+    )(vert_coef, horiz_coef, wet_mask, chunk)
+
+
+def late(groups, tiles, state, horiz_coef, wet_mask, chip, core, solved, after):
     levels, height, width = state.shape
     full, halo = f32(levels, height, width), f32(levels, width // 64, 128)
-    scratch = [pltpu.VMEM(s.shape, jnp.float32) for s in [full] * 5 + [halo] * 5]
     return pl.pallas_call(
-        functools.partial(solve_kernel, tiles, groups),
-        out_shape=(f32(6, levels, height, width), f32(width // 64, 128), f32(*chunk.shape)),
-        in_specs=[VM] * 6 + [HBM],
-        scratch_shapes=scratch + [pltpu.SemaphoreType.DMA],
-        compiler_params=params(24),
-        cost_estimate=cost(8),
-    )(state, vert_coef, horiz_coef, wet_mask, chip, core, chunk)
-
-
-def finish(groups, wet_mask, parts, halo_wet, arrived):
+        functools.partial(late_kernel, tiles, groups),
+        out_shape=(f32(4, levels, height, width), f32(width // 64, 128)),
+        in_specs=[VM] * 10,
+        scratch_shapes=[pltpu.VMEM(s.shape, jnp.float32) for s in [full] + [halo] * 5],
+        compiler_params=params(16),
+        cost_estimate=cost(4),
+    )(state, horiz_coef, wet_mask, chip, core, *solved, after)
+
+
+def finish(groups, wet_mask, sides, parts, halo_wet, arrived):
     _, levels, height, width = parts.shape
     return pl.pallas_call(
         functools.partial(last_kernel, width // 128, groups),
@@ -547,7 +593,7 @@
             pltpu.SemaphoreType.DMA((4,)),
         ],
         compiler_params=params(16),
-    )(wet_mask, parts, halo_wet, *arrived)
+    )(wet_mask, sides, parts, halo_wet, *arrived)
 
 
 def local(
@@ -564,21 +610,19 @@
     axes = ("grp", "tile")
     across = [(i, i + 1) for i in range(1, devices - 1, 2) if i + 1 != start]
     across = across + [(j, i) for i, j in across]
-    chip, core = edges_of(groups, state, vert_coef, horiz_coef, wet_mask)
+    packed = pack(
+        groups, tiles, slots, state, coupling, surface_in, wet_mask, dest_tile, dest_block, dest_group, remap_w
+    )
+    chips = tiles // 2
+    moved = {
+        k: lax.ppermute(packed[k], "tile", [(i, ((i // 2) ^ k) * 2 + i % 2) for i in range(tiles)])
+        for k in sorted(range(1, chips), key=lambda k: (k != chips // 2, k))
+    }
+    got = [moved[k] for k in range(1, chips)]
+    *solved, sides, chunk = early(groups, vert_coef, horiz_coef, wet_mask, packed[0])
+    chip, core = edges_of(groups, state, vert_coef, horiz_coef, wet_mask, chunk)
     chip = lax.ppermute(chip, axes, across)
     core = lax.ppermute(core, axes, [(i, i ^ 1) for i in range(devices)])
-    packed = pack(
-        groups, tiles, slots, state, coupling, surface_in, wet_mask, dest_tile, dest_block, dest_group, remap_w
-    )
-    chips = tiles // 2
-    got = [
-        lax.ppermute(packed[k], "tile", [(i, ((i // 2) ^ k) * 2 + i % 2) for i in range(tiles)])
-        for k in list(range(chips // 2, chips)) + list(range(1, chips // 2))
-    ]
-    got = got[chips - chips // 2 :] + got[: chips - chips // 2]
-    parts, halo_wet, chunk = solve(
-        groups, tiles, state, vert_coef, horiz_coef, wet_mask, chip, core, packed[0]
-    )
     rows = (groups - 1) * (F * blocks + rim)
     mine, theirs = pl.pallas_call(
         functools.partial(merge_kernel, slots, height, cols, groups),
@@ -597,7 +641,8 @@
         lax.ppermute(merged[g], "grp", [(j, (j + g + 1) % groups) for j in range(groups)])
         for g in range(groups - 1)
     ]
-    return finish(groups, wet_mask, parts, halo_wet, arrived)
+    parts, halo_wet = late(groups, tiles, state, horiz_coef, wet_mask, chip, core, solved, merged[0])
+    return finish(groups, wet_mask, sides, parts, halo_wet, arrived)
 
 
 def solution(mesh):

time: 41 us -> 39.6 us (0.966)
  the two profiles are of different devices: /device:TPU:10 before, /device:TPU:16 now
where the time goes in v7:
time: 39.6 us; the launch traced here: 39.4 us
  starting transfers between devices  17 us (43%)
  Pallas kernels  13.8 us (35%)
  waiting for transfers between devices  6.95 us (18%)
  local copies, waits for them, and re-layouts  0.92 us (2%)
  between operations  0.77 us (2%)
    ppermute x3, starting transfers between devices, local(): lax.ppermute(merged[g], 'grp', [(j, (j + g + 1) % groups) for j in range(...  8.8 us
    ppermute x3, waiting for transfers between devices, local(): lax.ppermute(packed[k], 'tile', [(i, (i // 2 ^ k) * 2 + i % 2) for i in r...  5.49 us
    pallas_call x1, Pallas kernels, pack(): pl.pallas_call(functools.partial(pack_kernel, tiles, slots, groups), out_...  4.24 us
    pallas_call x1, Pallas kernels, late(): pl.pallas_call(functools.partial(late_kernel, tiles, groups), out_shape=(...  3.95 us
    ppermute x3, starting transfers between devices, local(): lax.ppermute(packed[k], 'tile', [(i, (i // 2 ^ k) * 2 + i % 2) for i in r...  3.55 us
    pallas_call x1, Pallas kernels, early(): pl.pallas_call(functools.partial(early_kernel, groups), out_shape=(full,)...  2.67 us
    ppermute x1, starting transfers between devices, local(): core = lax.ppermute(core, axes, [(i, i ^ 1) for i in range(devices)])  2.65 us
    pallas_call x1, Pallas kernels, finish(): pl.pallas_call(functools.partial(last_kernel, width // 128, groups), out_...  2.06 us
  transfers between devices with their start and end apart: 9, of which 3 were waited for; matrix products, arithmetic and copies ran while one was open for 0% of the time, Pallas kernels for 19%

profile of v7, /device:TPU:16, one launch (start us, length us, event | category | flops | bytes accessed | tf_op | source)
XLA Modules:
  0.0 39.4 jit_solution(1494649720045279887)
XLA Ops:
  0.6 0.0 copy-start.2
  0.6 0.0 copy-start
  0.7 0.0 copy-start.1
  0.7 0.0 copy-start.3
  0.7 4.2 %shard_map.113 = (f32[288,128]{1,0:T(8,128)}, f32[288,128]{1,0:T(8,128)}, f32[288,128]{1,0:T(8,128)}, f32[288,128]{1,0:T(8,128)}) custom-call(f32[64,8,512]{2,1,0:T(8,128)} %state.5, f32[4,8,512]{2,1,0:T(8,128)} %coupling.1, f32[4,8,512]{2,1,0:T(8,128)} %surface.1, s32[8,512]{1,0:T(8,128)} %mask.9, s32[4,32]{1,0:T(4,128)} %bitcast.5, s32[4,32]{1,0:T(4,128)} %bitcast.6, ...), custom_call_target="tpu_custom_call" | custom-call | bytes 9000000 | tf_op jit(solution)/shard_map/pallas_call | solution.py:538
  4.9 1.6 %collective-permute-start.2 = (f32[288,128]{1,0:T(8,128)}, f32[288,128]{1,0:T(8,128)S(1)}, u32[]{:S(2)}, u32[]{:S(2)}) collective-permute-start(f32[288,128]{1,0:T(8,128)} %get-tuple-element.30), channel_id=1, source_target_pairs={{0,2},{1,3},{2,0},{3,1},{4,6},{5,7},{6,4},{7,5},{8,10},{9,11},{10,... | collective-permute-start | bytes 442376 | tf_op jit(solution)/shard_map/ppermute | solution.py:618
  6.6 0.3 collective-permute-start.3
  6.9 1.6 %collective-permute-start.4 = (f32[288,128]{1,0:T(8,128)}, f32[288,128]{1,0:T(8,128)S(1)}, u32[]{:S(2)}, u32[]{:S(2)}) collective-permute-start(f32[288,128]{1,0:T(8,128)} %get-tuple-element.32), channel_id=1, source_target_pairs={{0,6},{1,7},{2,4},{3,5},{4,2},{5,3},{6,0},{7,1},{8,14},{9,15},{10,... | collective-permute-start | bytes 442376 | tf_op jit(solution)/shard_map/ppermute | solution.py:618
  8.5 0.0 copy-done.2
  8.5 0.0 copy-done.1
  8.5 0.0 copy-done.3
  8.5 0.9 %copy-done.4 = f32[288,128]{1,0:T(8,128)S(1)} copy-done((f32[288,128]{1,0:T(8,128)S(1)}, f32[288,128]{1,0:T(8,128)}, u32[]{:S(2)}) %copy-start.4) | copy-done | bytes 147480
  9.4 2.7 %shard_map.114 = (f32[64,8,512]{2,1,0:T(8,128)S(1)}, f32[64,8,512]{2,1,0:T(8,128)S(1)}, f32[64,8,512]{2,1,0:T(8,128)S(1)}, f32[64,8,512]{2,1,0:T(8,128)S(1)}, f3...) custom-call(f32[63,8,512]{2,1,0:T(8,128)S(1)} %copy-done.1, f32[8,512]{1,0:T(8,128)S(1)} %copy-done.3, ...), custom_call_target="tpu_custom_call" | custom-call | bytes 9000000 | tf_op jit(solution)/shard_map/pallas_call | solution.py:562
  12.1 0.6 %shard_map.115 = (f32[98,8,128]{2,1,0:T(8,128)S(1)}, f32[98,8,128]{2,1,0:T(8,128)S(1)}) custom-call(f32[64,8,512]{2,1,0:T(8,128)S(1)} %copy-done, f32[63,8,512]{2,1,0:T(8,128)S(1)} %copy-done.1, f32[8,512]{1,0:T(8,128)S(1)} %copy-done.3, s32[8,512]{1,0:T(8,128)S(1)} %copy-done.2, f32[288,128]{1,0:T(8,128)S(1)} %get-tuple-element.23._.refs_0_), custom_call_target="tpu_custom_call" | custom-call | bytes 3000000 | tf_op jit(solution)/shard_map/pallas_call | solution.py:525
  12.7 1.9 %collective-permute-start = (f32[98,8,128]{2,1,0:T(8,128)S(1)}, f32[98,8,128]{2,1,0:T(8,128)S(1)}, u32[]{:S(2)}, u32[]{:S(2)}) collective-permute-start(f32[98,8,128]{2,1,0:T(8,128)S(1)} %get-tuple-element.24), channel_id=1, source_target_pairs={{1,2},{3,4},{5,6},{7,8},{9,10},{11,12},{13,14},{15,16},{17,18},{19... | collective-permute-start | bytes 1204232 | tf_op jit(solution)/shard_map/ppermute | solution.py:624
  14.6 2.6 %collective-permute-start.1 = (f32[98,8,128]{2,1,0:T(8,128)S(1)}, f32[98,8,128]{2,1,0:T(8,128)S(1)}, u32[]{:S(2)}, u32[]{:S(2)}) collective-permute-start(f32[98,8,128]{2,1,0:T(8,128)S(1)} %get-tuple-element.25), channel_id=1, source_target_pairs={{0,1},{1,0},{2,3},{3,2},{4,5},{5,4},{6,7},{7,6},{8,9},{9,8},{10,11... | collective-permute-start | bytes 1204232 | tf_op jit(solution)/shard_map/ppermute | solution.py:625
  17.2 0.0 collective-permute-done.2.refs_1_
  17.2 0.6 %collective-permute-done.3.refs_2_ = f32[288,128]{1,0:T(8,128)S(1)} collective-permute-done((f32[288,128]{1,0:T(8,128)}, f32[288,128]{1,0:T(8,128)S(1)}, u32[]{:S(2)}, u32[]{:S(2)}) %collective-permute-start.3) | collective-permute-done | bytes 147488 | tf_op jit(solution)/shard_map/ppermute | solution.py:618
  17.8 4.9 %collective-permute-done.4.refs_3_ = f32[288,128]{1,0:T(8,128)S(1)} collective-permute-done((f32[288,128]{1,0:T(8,128)}, f32[288,128]{1,0:T(8,128)S(1)}, u32[]{:S(2)}, u32[]{:S(2)}) %collective-permute-start.4) | collective-permute-done | bytes 147488 | tf_op jit(solution)/shard_map/ppermute | solution.py:618
  22.7 0.3 shard_map.116
  23.0 0.1 collective-permute-start.5
  23.1 1.4 %collective-permute-done.5.theirs = f32[408,128]{1,0:T(8,128)S(1)} collective-permute-done((f32[408,128]{1,0:T(8,128)S(1)}, f32[408,128]{1,0:T(8,128)S(1)}, u32[]{:S(2)}, u32[]{:S(2)}) %collective-permute-start.5) | collective-permute-done | bytes 208928 | tf_op jit(solution)/shard_map/ppermute | solution.py:633
  24.6 5.8 %collective-permute-start.6 = (f32[136,128]{1,0:T(8,128)S(1)}, f32[136,128]{1,0:T(8,128)S(1)}, u32[]{:S(2)}, u32[]{:S(2)}) collective-permute-start(f32[136,128]{1,0:T(8,128)S(1)} %get-tuple-element.35._), channel_id=1, source_target_pairs={{0,8},{8,16},{16,24},{24,0},{1,9},{9,17},{17,25},{25,1},{2,10},{10... | collective-permute-start | bytes 208904 | tf_op jit(solution)/shard_map/ppermute | solution.py:641
  30.4 0.1 collective-permute-start.7
  30.5 2.8 %collective-permute-start.8 = (f32[136,128]{1,0:T(8,128)S(1)}, f32[136,128]{1,0:T(8,128)S(1)}, u32[]{:S(2)}, u32[]{:S(2)}) collective-permute-start(f32[136,128]{1,0:T(8,128)S(1)} %get-tuple-element.39), channel_id=1, source_target_pairs={{0,24},{8,0},{16,8},{24,16},{1,25},{9,1},{17,9},{25,17},{2,26},{10... | collective-permute-start | bytes 208904 | tf_op jit(solution)/shard_map/ppermute | solution.py:641
  33.4 0.0 collective-permute-done.chip
  33.4 0.0 collective-permute-done.1.core
  33.4 4.0 %shard_map.118 = (f32[4,64,8,512]{3,2,1,0:T(8,128)S(1)}, f32[8,128]{1,0:T(8,128)S(1)}) custom-call(f32[64,8,512]{2,1,0:T(8,128)S(1)} %copy-done, f32[8,512]{1,0:T(8,128)S(1)} %copy-done.3, s32[8,512]{1,0:T(8,128)S(1)} %copy-done.2, f32[98,8,128]{2,1,0:T(8,128)S(1)} %collective-permute-done.chip, f32[98,8,128]{2,1,0:T(8,128)S(1)} %collective-permute-done.1.core, ...), custom_call_target="tpu_custom_call" | custom-call | bytes 12000000 | tf_op jit(solution)/shard_map/pallas_call | solution.py:575
  37.3 0.0 collective-permute-done.6.refs_0_
  37.3 0.0 collective-permute-done.7.refs_1_
  37.4 0.0 collective-permute-done.8.refs_2_
  37.4 2.1 %shard_map.119 = (f32[64,8,512]{2,1,0:T(8,128)}, f32[4,8,512]{2,1,0:T(8,128)}) custom-call(s32[8,512]{1,0:T(8,128)S(1)} %copy-done.2, f32[2,64,8,512]{3,2,1,0:T(8,128)S(1)} %get-tuple-element.22.sides, f32[4,64,8,512]{3,2,1,0:T(8,128)S(1)} %get-tuple-element.36.parts, f32[8,128]{1,0:T(8,128)S(1)} %get-tuple-element.37.halo_wet, ...), custom_call_target="tpu_custom_call" | custom-call | tf_op jit(solution)/shard_map/pallas_call | solution.py:587
  (3 shorter events, 0.0 us)
Async XLA Ops:
  0.6 7.8 %copy-start.2 = (s32[8,512]{1,0:T(8,128)S(1)}, s32[8,512]{1,0:T(8,128)}, u32[]{:S(2)}) copy-start(s32[8,512]{1,0:T(8,128)} %mask.9) | copy-start | bytes 49156
  0.6 11.4 %copy-start = (f32[64,8,512]{2,1,0:T(8,128)S(1)}, f32[64,8,512]{2,1,0:T(8,128)}, u32[]{:S(2)}) copy-start(f32[64,8,512]{2,1,0:T(8,128)} %state.5) | copy-start | bytes 3145732
  0.7 7.8 %copy-start.1 = (f32[63,8,512]{2,1,0:T(8,128)S(1)}, f32[63,8,512]{2,1,0:T(8,128)}, u32[]{:S(2)}) copy-start(f32[63,8,512]{2,1,0:T(8,128)} %vert.3) | copy-start | bytes 3096580
  0.7 7.8 %copy-start.3 = (f32[8,512]{1,0:T(8,128)S(1)}, f32[8,512]{1,0:T(8,128)}, u32[]{:S(2)}) copy-start(f32[8,512]{1,0:T(8,128)} %horiz.5) | copy-start | bytes 49156
  4.9 12.3 %collective-permute-start.2 = (f32[288,128]{1,0:T(8,128)}, f32[288,128]{1,0:T(8,128)S(1)}, u32[]{:S(2)}, u32[]{:S(2)}) collective-permute-start(f32[288,128]{1,0:T(8,128)} %get-tuple-element.30), channel_id=1, source_target_pairs={{0,2},{1,3},{2,0},{3,1},{4,6},{5,7},{6,4},{7,5},{8,10},{9,11},{10,... | collective-permute-start | bytes 442376 | tf_op jit(solution)/shard_map/ppermute | solution.py:618
  6.6 11.3 %collective-permute-start.3 = (f32[288,128]{1,0:T(8,128)}, f32[288,128]{1,0:T(8,128)S(1)}, u32[]{:S(2)}, u32[]{:S(2)}) collective-permute-start(f32[288,128]{1,0:T(8,128)} %get-tuple-element.31), channel_id=1, source_target_pairs={{0,4},{1,5},{2,6},{3,7},{4,0},{5,1},{6,2},{7,3},{8,12},{9,13},{10,... | collective-permute-start | bytes 442376 | tf_op jit(solution)/shard_map/ppermute | solution.py:618
  6.9 15.8 %collective-permute-start.4 = (f32[288,128]{1,0:T(8,128)}, f32[288,128]{1,0:T(8,128)S(1)}, u32[]{:S(2)}, u32[]{:S(2)}) collective-permute-start(f32[288,128]{1,0:T(8,128)} %get-tuple-element.32), channel_id=1, source_target_pairs={{0,6},{1,7},{2,4},{3,5},{4,2},{5,3},{6,0},{7,1},{8,14},{9,15},{10,... | collective-permute-start | bytes 442376 | tf_op jit(solution)/shard_map/ppermute | solution.py:618
  8.5 0.9 %copy-start.4 = (f32[288,128]{1,0:T(8,128)S(1)}, f32[288,128]{1,0:T(8,128)}, u32[]{:S(2)}) copy-start(f32[288,128]{1,0:T(8,128)} %get-tuple-element.21.chunk) | copy-start | bytes 442372
  12.7 20.7 %collective-permute-start = (f32[98,8,128]{2,1,0:T(8,128)S(1)}, f32[98,8,128]{2,1,0:T(8,128)S(1)}, u32[]{:S(2)}, u32[]{:S(2)}) collective-permute-start(f32[98,8,128]{2,1,0:T(8,128)S(1)} %get-tuple-element.24), channel_id=1, source_target_pairs={{1,2},{3,4},{5,6},{7,8},{9,10},{11,12},{13,14},{15,16},{17,18},{19... | collective-permute-start | bytes 1204232 | tf_op jit(solution)/shard_map/ppermute | solution.py:624
  14.6 18.8 %collective-permute-start.1 = (f32[98,8,128]{2,1,0:T(8,128)S(1)}, f32[98,8,128]{2,1,0:T(8,128)S(1)}, u32[]{:S(2)}, u32[]{:S(2)}) collective-permute-start(f32[98,8,128]{2,1,0:T(8,128)S(1)} %get-tuple-element.25), channel_id=1, source_target_pairs={{0,1},{1,0},{2,3},{3,2},{4,5},{5,4},{6,7},{7,6},{8,9},{9,8},{10,11... | collective-permute-start | bytes 1204232 | tf_op jit(solution)/shard_map/ppermute | solution.py:625
  23.0 1.5 %collective-permute-start.5 = (f32[408,128]{1,0:T(8,128)S(1)}, f32[408,128]{1,0:T(8,128)S(1)}, u32[]{:S(2)}, u32[]{:S(2)}) collective-permute-start(f32[408,128]{1,0:T(8,128)S(1)} %get-tuple-element.34), channel_id=1, source_target_pairs={{0,1},{1,0},{2,3},{3,2},{4,5},{5,4},{6,7},{7,6},{8,9},{9,8},{10,11... | collective-permute-start | bytes 626696 | tf_op jit(solution)/shard_map/ppermute | solution.py:633
  24.6 12.8 %collective-permute-start.6 = (f32[136,128]{1,0:T(8,128)S(1)}, f32[136,128]{1,0:T(8,128)S(1)}, u32[]{:S(2)}, u32[]{:S(2)}) collective-permute-start(f32[136,128]{1,0:T(8,128)S(1)} %get-tuple-element.35._), channel_id=1, source_target_pairs={{0,8},{8,16},{16,24},{24,0},{1,9},{9,17},{17,25},{25,1},{2,10},{10... | collective-permute-start | bytes 208904 | tf_op jit(solution)/shard_map/ppermute | solution.py:641
  30.4 6.9 %collective-permute-start.7 = (f32[136,128]{1,0:T(8,128)S(1)}, f32[136,128]{1,0:T(8,128)S(1)}, u32[]{:S(2)}, u32[]{:S(2)}) collective-permute-start(f32[136,128]{1,0:T(8,128)S(1)} %get-tuple-element.38), channel_id=1, source_target_pairs={{0,16},{8,24},{16,0},{24,8},{1,17},{9,25},{17,1},{25,9},{2,18},{10... | collective-permute-start | bytes 208904 | tf_op jit(solution)/shard_map/ppermute | solution.py:641
  30.5 6.8 %collective-permute-start.8 = (f32[136,128]{1,0:T(8,128)S(1)}, f32[136,128]{1,0:T(8,128)S(1)}, u32[]{:S(2)}, u32[]{:S(2)}) collective-permute-start(f32[136,128]{1,0:T(8,128)S(1)} %get-tuple-element.39), channel_id=1, source_target_pairs={{0,24},{8,0},{16,8},{24,16},{1,25},{9,1},{17,9},{25,17},{2,26},{10... | collective-permute-start | bytes 208904 | tf_op jit(solution)/shard_map/ppermute | solution.py:641

commit v8 on v7

--- a/solution.py
+++ b/solution.py
@@ -207,7 +207,8 @@
         out[rows + cols :, :] = jnp.where(even, near, far)
 
 
-def edge_kernel(groups, state, vert, horiz, mask, _, chip, core):
+def edge_kernel(groups, state, vert, horiz, mask, *refs):
+    chip, core = refs[-2:]
     levels, height, width = state.shape
     half = levels // 2
     cols = width // 128
@@ -520,15 +521,15 @@
     return pl.CostEstimate(flops=0, bytes_accessed=int(us * 3e6), transcendentals=0)
 
 
-def edges_of(groups, state, vert_coef, horiz_coef, wet_mask, after):
+def edges_of(groups, state, vert_coef, horiz_coef, wet_mask, *after):
     levels, height, width = state.shape
     return pl.pallas_call(
         functools.partial(edge_kernel, groups),
         out_shape=(f32(levels + levels // 2 + 2, width // 64, 128),) * 2,
-        in_specs=[VM] * 4 + [HBM],
+        in_specs=[VM] * 4 + [HBM] * len(after),
         compiler_params=params(8),
         cost_estimate=cost(1),
-    )(state, vert_coef, horiz_coef, wet_mask, after)
+    )(state, vert_coef, horiz_coef, wet_mask, *after)
 
 
 def pack(groups, tiles, slots, state, coupling, surface, mask, dtile, dblock, dgroup, w):
@@ -620,7 +621,7 @@
     }
     got = [moved[k] for k in range(1, chips)]
     *solved, sides, chunk = early(groups, vert_coef, horiz_coef, wet_mask, packed[0])
-    chip, core = edges_of(groups, state, vert_coef, horiz_coef, wet_mask, chunk)
+    chip, core = edges_of(groups, state, vert_coef, horiz_coef, wet_mask, chunk, got[2])
     chip = lax.ppermute(chip, axes, across)
     core = lax.ppermute(core, axes, [(i, i ^ 1) for i in range(devices)])
     rows = (groups - 1) * (F * blocks + rim)

time: 39.6 us -> 37.1 us (0.937)
  the two profiles are of different devices: /device:TPU:16 before, /device:TPU:4 now
where the time goes in v8:
time: 37.1 us; the launch traced here: 37 us
  starting transfers between devices  13.9 us (37%)
  Pallas kernels  13.8 us (37%)
  waiting for transfers between devices  7.6 us (20%)
  local copies, waits for them, and re-layouts  0.92 us (2%)
  between operations  0.76 us (2%)
    ppermute x3, starting transfers between devices, local(): lax.ppermute(packed[k], 'tile', [(i, (i // 2 ^ k) * 2 + i % 2) for i in r...  4.45 us
    ppermute x1, waiting for transfers between devices, local(): chip = lax.ppermute(chip, axes, across)  4.31 us
    ppermute x1, starting transfers between devices, local(): chip = lax.ppermute(chip, axes, across)  4.25 us
    pallas_call x1, Pallas kernels, pack(): pl.pallas_call(functools.partial(pack_kernel, tiles, slots, groups), out_...  4.25 us
    pallas_call x1, Pallas kernels, late(): pl.pallas_call(functools.partial(late_kernel, tiles, groups), out_shape=(...  3.95 us
    ppermute x3, starting transfers between devices, local(): lax.ppermute(merged[g], 'grp', [(j, (j + g + 1) % groups) for j in range(...  3.48 us
    pallas_call x1, Pallas kernels, early(): pl.pallas_call(functools.partial(early_kernel, groups), out_shape=(full,)...  2.67 us
    pallas_call x1, Pallas kernels, finish(): pl.pallas_call(functools.partial(last_kernel, width // 128, groups), out_...  2.06 us
  transfers between devices with their start and end apart: 9, of which 4 were waited for; matrix products, arithmetic and copies ran while one was open for 0% of the time, Pallas kernels for 20%

profile of v8, /device:TPU:4, one launch (start us, length us, event | category | flops | bytes accessed | tf_op | source)
XLA Modules:
  0.0 37.0 jit_solution(14064546279450322768)
XLA Ops:
  0.6 0.0 copy-start.2
  0.6 0.0 copy-start
  0.7 0.0 copy-start.1
  0.7 0.0 copy-start.3
  0.7 4.2 %shard_map.113 = (f32[288,128]{1,0:T(8,128)}, f32[288,128]{1,0:T(8,128)}, f32[288,128]{1,0:T(8,128)}, f32[288,128]{1,0:T(8,128)}) custom-call(f32[64,8,512]{2,1,0:T(8,128)} %state.5, f32[4,8,512]{2,1,0:T(8,128)} %coupling.1, f32[4,8,512]{2,1,0:T(8,128)} %surface.1, s32[8,512]{1,0:T(8,128)} %mask.9, s32[4,32]{1,0:T(4,128)} %bitcast.5, s32[4,32]{1,0:T(4,128)} %bitcast.6, ...), custom_call_target="tpu_custom_call" | custom-call | bytes 9000000 | tf_op jit(solution)/shard_map/pallas_call | solution.py:539
  4.9 3.7 %collective-permute-start = (f32[288,128]{1,0:T(8,128)}, f32[288,128]{1,0:T(8,128)S(1)}, u32[]{:S(2)}, u32[]{:S(2)}) collective-permute-start(f32[288,128]{1,0:T(8,128)} %get-tuple-element.24), channel_id=1, source_target_pairs={{0,6},{1,7},{2,4},{3,5},{4,2},{5,3},{6,0},{7,1},{8,14},{9,15},{10,... | collective-permute-start | bytes 442376 | tf_op jit(solution)/shard_map/ppermute | solution.py:619
  8.6 0.0 collective-permute-start.3
  8.6 0.8 %collective-permute-start.4 = (f32[288,128]{1,0:T(8,128)}, f32[288,128]{1,0:T(8,128)S(1)}, u32[]{:S(2)}, u32[]{:S(2)}) collective-permute-start(f32[288,128]{1,0:T(8,128)} %get-tuple-element.32), channel_id=1, source_target_pairs={{0,4},{1,5},{2,6},{3,7},{4,0},{5,1},{6,2},{7,3},{8,12},{9,13},{10,... | collective-permute-start | bytes 442376 | tf_op jit(solution)/shard_map/ppermute | solution.py:619
  9.4 0.0 copy-done.2
  9.4 0.0 copy-done.1
  9.4 0.0 copy-done.3
  9.4 0.9 %copy-done.4 = f32[288,128]{1,0:T(8,128)S(1)} copy-done((f32[288,128]{1,0:T(8,128)S(1)}, f32[288,128]{1,0:T(8,128)}, u32[]{:S(2)}) %copy-start.4) | copy-done | bytes 147480
  10.3 2.7 %shard_map.114 = (f32[64,8,512]{2,1,0:T(8,128)S(1)}, f32[64,8,512]{2,1,0:T(8,128)S(1)}, f32[64,8,512]{2,1,0:T(8,128)S(1)}, f32[64,8,512]{2,1,0:T(8,128)S(1)}, f3...) custom-call(f32[63,8,512]{2,1,0:T(8,128)S(1)} %copy-done.1, f32[8,512]{1,0:T(8,128)S(1)} %copy-done.3, ...), custom_call_target="tpu_custom_call" | custom-call | bytes 9000000 | tf_op jit(solution)/shard_map/pallas_call | solution.py:563
  13.0 0.8 %collective-permute-done.refs_1_.refs_3_ = f32[288,128]{1,0:T(8,128)S(1)} collective-permute-done((f32[288,128]{1,0:T(8,128)}, f32[288,128]{1,0:T(8,128)S(1)}, u32[]{:S(2)}, u32[]{:S(2)}) %collective-permute-start) | collective-permute-done | bytes 147488 | tf_op jit(solution)/shard_map/ppermute | solution.py:619
  13.7 0.6 %shard_map.115 = (f32[98,8,128]{2,1,0:T(8,128)S(1)}, f32[98,8,128]{2,1,0:T(8,128)S(1)}) custom-call(f32[64,8,512]{2,1,0:T(8,128)S(1)} %copy-done, f32[63,8,512]{2,1,0:T(8,128)S(1)} %copy-done.1, f32[8,512]{1,0:T(8,128)S(1)} %copy-done.3, s32[8,512]{1,0:T(8,128)S(1)} %copy-done.2, f32[288,128]{1,0:T(8,128)S(1)} %get-tuple-element.23.refs_0_, ...), custom_call_target="tpu_custom_call" | custom-call | bytes 3000000 | tf_op jit(solution)/shard_map/pallas_call | solution.py:526
  14.3 4.3 %collective-permute-start.1 = (f32[98,8,128]{2,1,0:T(8,128)S(1)}, f32[98,8,128]{2,1,0:T(8,128)S(1)}, u32[]{:S(2)}, u32[]{:S(2)}) collective-permute-start(f32[98,8,128]{2,1,0:T(8,128)S(1)} %get-tuple-element.25), channel_id=1, source_target_pairs={{1,2},{3,4},{5,6},{7,8},{9,10},{11,12},{13,14},{15,16},{17,18},{19... | collective-permute-start | bytes 1204232 | tf_op jit(solution)/shard_map/ppermute | solution.py:625
  18.6 1.6 %collective-permute-start.2 = (f32[98,8,128]{2,1,0:T(8,128)S(1)}, f32[98,8,128]{2,1,0:T(8,128)S(1)}, u32[]{:S(2)}, u32[]{:S(2)}) collective-permute-start(f32[98,8,128]{2,1,0:T(8,128)S(1)} %get-tuple-element.26), channel_id=1, source_target_pairs={{0,1},{1,0},{2,3},{3,2},{4,5},{5,4},{6,7},{7,6},{8,9},{9,8},{10,11... | collective-permute-start | bytes 1204232 | tf_op jit(solution)/shard_map/ppermute | solution.py:626
  20.2 0.0 collective-permute-done.3.refs_1_
  20.2 1.1 %collective-permute-done.4.refs_2_ = f32[288,128]{1,0:T(8,128)S(1)} collective-permute-done((f32[288,128]{1,0:T(8,128)}, f32[288,128]{1,0:T(8,128)S(1)}, u32[]{:S(2)}, u32[]{:S(2)}) %collective-permute-start.4) | collective-permute-done | bytes 147488 | tf_op jit(solution)/shard_map/ppermute | solution.py:619
  21.3 0.3 shard_map.116
  21.6 0.1 collective-permute-start.5
  21.6 1.4 %collective-permute-done.5.theirs = f32[408,128]{1,0:T(8,128)S(1)} collective-permute-done((f32[408,128]{1,0:T(8,128)S(1)}, f32[408,128]{1,0:T(8,128)S(1)}, u32[]{:S(2)}, u32[]{:S(2)}) %collective-permute-start.5) | collective-permute-done | bytes 208928 | tf_op jit(solution)/shard_map/ppermute | solution.py:634
  23.1 1.5 %collective-permute-start.6 = (f32[136,128]{1,0:T(8,128)S(1)}, f32[136,128]{1,0:T(8,128)S(1)}, u32[]{:S(2)}, u32[]{:S(2)}) collective-permute-start(f32[136,128]{1,0:T(8,128)S(1)} %get-tuple-element.35._), channel_id=1, source_target_pairs={{0,8},{8,16},{16,24},{24,0},{1,9},{9,17},{17,25},{25,1},{2,10},{10... | collective-permute-start | bytes 208904 | tf_op jit(solution)/shard_map/ppermute | solution.py:642
  24.7 0.5 %collective-permute-start.7 = (f32[136,128]{1,0:T(8,128)S(1)}, f32[136,128]{1,0:T(8,128)S(1)}, u32[]{:S(2)}, u32[]{:S(2)}) collective-permute-start(f32[136,128]{1,0:T(8,128)S(1)} %get-tuple-element.38), channel_id=1, source_target_pairs={{0,16},{8,24},{16,0},{24,8},{1,17},{9,25},{17,1},{25,9},{2,18},{10... | collective-permute-start | bytes 208904 | tf_op jit(solution)/shard_map/ppermute | solution.py:642
  25.2 1.4 %collective-permute-start.8 = (f32[136,128]{1,0:T(8,128)S(1)}, f32[136,128]{1,0:T(8,128)S(1)}, u32[]{:S(2)}, u32[]{:S(2)}) collective-permute-start(f32[136,128]{1,0:T(8,128)S(1)} %get-tuple-element.39), channel_id=1, source_target_pairs={{0,24},{8,0},{16,8},{24,16},{1,25},{9,1},{17,9},{25,17},{2,26},{10... | collective-permute-start | bytes 208904 | tf_op jit(solution)/shard_map/ppermute | solution.py:642
  26.6 4.3 %collective-permute-done.1.chip = f32[98,8,128]{2,1,0:T(8,128)S(1)} collective-permute-done((f32[98,8,128]{2,1,0:T(8,128)S(1)}, f32[98,8,128]{2,1,0:T(8,128)S(1)}, u32[]{:S(2)}, u32[]{:S(2)}) %collective-permute-start.1) | collective-permute-done | bytes 401440 | tf_op jit(solution)/shard_map/ppermute | solution.py:625
  30.9 0.0 collective-permute-done.2.core
  30.9 4.0 %shard_map.118 = (f32[4,64,8,512]{3,2,1,0:T(8,128)S(1)}, f32[8,128]{1,0:T(8,128)S(1)}) custom-call(f32[64,8,512]{2,1,0:T(8,128)S(1)} %copy-done, f32[8,512]{1,0:T(8,128)S(1)} %copy-done.3, s32[8,512]{1,0:T(8,128)S(1)} %copy-done.2, f32[98,8,128]{2,1,0:T(8,128)S(1)} %collective-permute-done.1.chip, f32[98,8,128]{2,1,0:T(8,128)S(1)} %collective-permute-done.2.core, ...), custom_call_target="tpu_custom_call" | custom-call | bytes 12000000 | tf_op jit(solution)/shard_map/pallas_call | solution.py:576
  34.9 0.0 collective-permute-done.6.refs_0_
  34.9 0.0 collective-permute-done.7.refs_1_
  34.9 0.0 collective-permute-done.8.refs_2_
  34.9 2.1 %shard_map.119 = (f32[64,8,512]{2,1,0:T(8,128)}, f32[4,8,512]{2,1,0:T(8,128)}) custom-call(s32[8,512]{1,0:T(8,128)S(1)} %copy-done.2, f32[2,64,8,512]{3,2,1,0:T(8,128)S(1)} %get-tuple-element.22.sides, f32[4,64,8,512]{3,2,1,0:T(8,128)S(1)} %get-tuple-element.36.parts, f32[8,128]{1,0:T(8,128)S(1)} %get-tuple-element.37.halo_wet, ...), custom_call_target="tpu_custom_call" | custom-call | tf_op jit(solution)/shard_map/pallas_call | solution.py:588
  (3 shorter events, 0.0 us)
Async XLA Ops:
  0.6 8.8 %copy-start.2 = (s32[8,512]{1,0:T(8,128)S(1)}, s32[8,512]{1,0:T(8,128)}, u32[]{:S(2)}) copy-start(s32[8,512]{1,0:T(8,128)} %mask.9) | copy-start | bytes 49156
  0.6 13.1 %copy-start = (f32[64,8,512]{2,1,0:T(8,128)S(1)}, f32[64,8,512]{2,1,0:T(8,128)}, u32[]{:S(2)}) copy-start(f32[64,8,512]{2,1,0:T(8,128)} %state.5) | copy-start | bytes 3145732
  0.7 8.7 %copy-start.1 = (f32[63,8,512]{2,1,0:T(8,128)S(1)}, f32[63,8,512]{2,1,0:T(8,128)}, u32[]{:S(2)}) copy-start(f32[63,8,512]{2,1,0:T(8,128)} %vert.3) | copy-start | bytes 3096580
  0.7 8.7 %copy-start.3 = (f32[8,512]{1,0:T(8,128)S(1)}, f32[8,512]{1,0:T(8,128)}, u32[]{:S(2)}) copy-start(f32[8,512]{1,0:T(8,128)} %horiz.5) | copy-start | bytes 49156
  4.9 8.8 %collective-permute-start = (f32[288,128]{1,0:T(8,128)}, f32[288,128]{1,0:T(8,128)S(1)}, u32[]{:S(2)}, u32[]{:S(2)}) collective-permute-start(f32[288,128]{1,0:T(8,128)} %get-tuple-element.24), channel_id=1, source_target_pairs={{0,6},{1,7},{2,4},{3,5},{4,2},{5,3},{6,0},{7,1},{8,14},{9,15},{10,... | collective-permute-start | bytes 442376 | tf_op jit(solution)/shard_map/ppermute | solution.py:619
  8.6 11.6 %collective-permute-start.3 = (f32[288,128]{1,0:T(8,128)}, f32[288,128]{1,0:T(8,128)S(1)}, u32[]{:S(2)}, u32[]{:S(2)}) collective-permute-start(f32[288,128]{1,0:T(8,128)} %get-tuple-element.31), channel_id=1, source_target_pairs={{0,2},{1,3},{2,0},{3,1},{4,6},{5,7},{6,4},{7,5},{8,10},{9,11},{10,... | collective-permute-start | bytes 442376 | tf_op jit(solution)/shard_map/ppermute | solution.py:619
  8.6 12.7 %collective-permute-start.4 = (f32[288,128]{1,0:T(8,128)}, f32[288,128]{1,0:T(8,128)S(1)}, u32[]{:S(2)}, u32[]{:S(2)}) collective-permute-start(f32[288,128]{1,0:T(8,128)} %get-tuple-element.32), channel_id=1, source_target_pairs={{0,4},{1,5},{2,6},{3,7},{4,0},{5,1},{6,2},{7,3},{8,12},{9,13},{10,... | collective-permute-start | bytes 442376 | tf_op jit(solution)/shard_map/ppermute | solution.py:619
  9.4 0.9 %copy-start.4 = (f32[288,128]{1,0:T(8,128)S(1)}, f32[288,128]{1,0:T(8,128)}, u32[]{:S(2)}) copy-start(f32[288,128]{1,0:T(8,128)} %get-tuple-element.21.chunk) | copy-start | bytes 442372
  14.3 16.6 %collective-permute-start.1 = (f32[98,8,128]{2,1,0:T(8,128)S(1)}, f32[98,8,128]{2,1,0:T(8,128)S(1)}, u32[]{:S(2)}, u32[]{:S(2)}) collective-permute-start(f32[98,8,128]{2,1,0:T(8,128)S(1)} %get-tuple-element.25), channel_id=1, source_target_pairs={{1,2},{3,4},{5,6},{7,8},{9,10},{11,12},{13,14},{15,16},{17,18},{19... | collective-permute-start | bytes 1204232 | tf_op jit(solution)/shard_map/ppermute | solution.py:625
  18.6 12.3 %collective-permute-start.2 = (f32[98,8,128]{2,1,0:T(8,128)S(1)}, f32[98,8,128]{2,1,0:T(8,128)S(1)}, u32[]{:S(2)}, u32[]{:S(2)}) collective-permute-start(f32[98,8,128]{2,1,0:T(8,128)S(1)} %get-tuple-element.26), channel_id=1, source_target_pairs={{0,1},{1,0},{2,3},{3,2},{4,5},{5,4},{6,7},{7,6},{8,9},{9,8},{10,11... | collective-permute-start | bytes 1204232 | tf_op jit(solution)/shard_map/ppermute | solution.py:626
  21.6 1.5 %collective-permute-start.5 = (f32[408,128]{1,0:T(8,128)S(1)}, f32[408,128]{1,0:T(8,128)S(1)}, u32[]{:S(2)}, u32[]{:S(2)}) collective-permute-start(f32[408,128]{1,0:T(8,128)S(1)} %get-tuple-element.34), channel_id=1, source_target_pairs={{0,1},{1,0},{2,3},{3,2},{4,5},{5,4},{6,7},{7,6},{8,9},{9,8},{10,11... | collective-permute-start | bytes 626696 | tf_op jit(solution)/shard_map/ppermute | solution.py:634
  23.1 11.8 %collective-permute-start.6 = (f32[136,128]{1,0:T(8,128)S(1)}, f32[136,128]{1,0:T(8,128)S(1)}, u32[]{:S(2)}, u32[]{:S(2)}) collective-permute-start(f32[136,128]{1,0:T(8,128)S(1)} %get-tuple-element.35._), channel_id=1, source_target_pairs={{0,8},{8,16},{16,24},{24,0},{1,9},{9,17},{17,25},{25,1},{2,10},{10... | collective-permute-start | bytes 208904 | tf_op jit(solution)/shard_map/ppermute | solution.py:642
  24.7 10.2 %collective-permute-start.7 = (f32[136,128]{1,0:T(8,128)S(1)}, f32[136,128]{1,0:T(8,128)S(1)}, u32[]{:S(2)}, u32[]{:S(2)}) collective-permute-start(f32[136,128]{1,0:T(8,128)S(1)} %get-tuple-element.38), channel_id=1, source_target_pairs={{0,16},{8,24},{16,0},{24,8},{1,17},{9,25},{17,1},{25,9},{2,18},{10... | collective-permute-start | bytes 208904 | tf_op jit(solution)/shard_map/ppermute | solution.py:642
  25.2 9.7 %collective-permute-start.8 = (f32[136,128]{1,0:T(8,128)S(1)}, f32[136,128]{1,0:T(8,128)S(1)}, u32[]{:S(2)}, u32[]{:S(2)}) collective-permute-start(f32[136,128]{1,0:T(8,128)S(1)} %get-tuple-element.39), channel_id=1, source_target_pairs={{0,24},{8,0},{16,8},{24,16},{1,25},{9,1},{17,9},{25,17},{2,26},{10... | collective-permute-start | bytes 208904 | tf_op jit(solution)/shard_map/ppermute | solution.py:642

commit v9 on v8

--- a/solution.py
+++ b/solution.py
@@ -237,65 +237,34 @@
     pl.when(jnp.logical_not(even))(lambda: fill(chip, core))
 
 
-def side_weights(horiz, wet):
+def weights_of(horiz, wet):
     height, width = wet.shape
-    column = iota((height, width), 1)
-    left = jnp.where(column == 0, 0.0, pltpu.roll(wet, 1, 1))
-    right = jnp.where(column == width - 1, 0.0, pltpu.roll(wet, width - 1, 1))
-    return horiz * wet * left, horiz * wet * right
-
-
-def weights_of(tiles, groups, horiz, wet, wet_above, wet_below):
-    height, width = wet.shape
-    device = lax.axis_index("grp") * tiles + lax.axis_index("tile")
-    rows = device * height + iota((height, width), 0)
-    start = (groups - 1) * tiles * height
-    last = groups * tiles * height - 1
-    above = jnp.concatenate([wet_above, wet[:-1]], 0)
-    below = jnp.concatenate([wet[1:], wet_below], 0)
-    above = jnp.where((rows > 0) & (rows != start), above, 0.0)
-    below = jnp.where((rows < last) & (rows + 1 != start), below, 0.0)
+    row, column = iota((height, width), 0), iota((height, width), 1)
+    left, right, above, below = around(wet)
     scale = horiz * wet
-    return side_weights(horiz, wet) + (scale * above, scale * below)
-
-
-def line_of(halo, first, cols):
-    return jnp.concatenate([halo[first + c : first + c + 1, :] for c in range(cols)], 1)
-
-
-def row_above(field, halo):
-    return jnp.concatenate([line_of(halo, 0, field.shape[1] // 128), field[:-1]], 0)
-
-
-def row_below(field, halo):
-    cols = field.shape[1] // 128
-    return jnp.concatenate([field[1:], line_of(halo, cols, cols)], 0)
-
-
-def around(field, halo):
-    width = field.shape[1]
+    return (
+        scale * jnp.where(column == 0, 0.0, left),
+        scale * jnp.where(column == width - 1, 0.0, right),
+        scale * jnp.where(row == 0, 0.0, above),
+        scale * jnp.where(row == height - 1, 0.0, below),
+    )
+
+
+def around(field):
+    height, width = field.shape
     return (
         pltpu.roll(field, 1, 1),
         pltpu.roll(field, width - 1, 1),
-        row_above(field, halo),
-        row_below(field, halo),
+        pltpu.roll(field, 1, 0),
+        pltpu.roll(field, height - 1, 0),
     )
 
 
-def stencil(field, halo, weights):
+def stencil(field, weights):
     total = field
-    for other, weight in zip(around(field, halo), weights):
+    for other, weight in zip(around(field), weights):
         total = total + weight * (other - field)
     return total
-
-
-def shifted(halo, lane):
-    rows = halo.shape[0]
-    to_right, to_left = pltpu.roll(halo, 1, 1), pltpu.roll(halo, 127, 1)
-    return (
-        jnp.where(lane == 0, pltpu.roll(to_right, 1, 0), to_right),
-        jnp.where(lane == 127, pltpu.roll(to_left, rows - 1, 0), to_left),
-    )
 
 
 def inverse_of(x):
@@ -304,52 +273,75 @@
 
 
 def early_kernel(
-    groups, vert, horiz, mask, chunk, upper, gain, ratio, impulse, sides, chunk_out, sem
+    groups, state, vert, horiz, mask, chunk, packs, chunk_out, upper, gain, ratio, base, impulse, sem,
 ):
-    levels, height, width = upper.shape
+    levels, height, width = state.shape
+    cols = width // 128
     copy = pltpu.make_async_copy(chunk, chunk_out, sem)
     copy.start()
     wet = wet_of(lax.axis_index("grp") == groups - 1, mask[...])
-    weights = side_weights(horiz[...], wet)
     zero = jnp.zeros((height, width), jnp.float32)
+    weights = weights_of(horiz[...], wet)
 
     def forward(level, carry, last=False, first=False):
-        low, c, e = carry
+        low, c, r, e = carry
         upp = zero if last else vert[level] * wet
         inverse = inverse_of(1.0 + low + upp + low * c)
         c = -upp * inverse
         step = low * inverse
+        r = stencil(state[level], weights) * inverse + step * r
         e = inverse if first else step * e
         upper[level] = c
         gain[level] = inverse
         ratio[level] = step
+        base[level] = r
         impulse[level] = e
-        return upp, c, e
-
-    carry = forward(0, (zero,) * 3, first=True)
+        return upp, c, r, e
+
+    carry = forward(0, (zero,) * 4, first=True)
     carry = lax.fori_loop(1, levels - 1, forward, carry, unroll=31)
-    _, _, e = forward(levels - 1, carry, last=True)
-
-    def backward(i, x):
+    _, _, r, e = forward(levels - 1, carry, last=True)
+
+    def backward(i, carry):
         level = levels - 2 - i
-        x = impulse[level] - upper[level] * x
-        impulse[level] = x
-        return x
-
-    lax.fori_loop(0, levels - 1, backward, e, unroll=9)
-
-    def forward_parts(level, carry):
+        c = upper[level]
+        r = base[level] - c * carry[0]
+        e = impulse[level] - c * carry[1]
+        base[level] = r
+        impulse[level] = e
+        return r, e
+
+    lax.fori_loop(0, levels - 1, backward, (r, e), unroll=9)
+    for i, (source, low, high) in enumerate(
+        [(x, 0, height - 1) for x in (upper, gain, ratio)]
+        + [(x, 1, height - 2) for x in (upper, gain, ratio)]
+        + [(x, 0, height - 1) for x in (impulse, base, state)]
+    ):
+        for c in range(cols):
+            at = slice(c * 128, (c + 1) * 128)
+            packs[i, :, c, :] = source[:, low, at]
+            packs[i, :, cols + c, :] = source[:, high, at]
+    copy.wait()
+
+
+def parts_kernel(groups, horiz, mask, upper, gain, ratio, base, impulse, _, parts):
+    levels = base.shape[0]
+    weights = weights_of(horiz[...], wet_of(lax.axis_index("grp") == groups - 1, mask[...]))
+    rest = 1.0 - weights[0] - weights[1] - weights[2] - weights[3]
+
+    def forward_parts(level, carry, first=False):
         g = impulse[level]
-        rhs = (weights[0] * pltpu.roll(g, 1, 1), weights[1] * pltpu.roll(g, width - 1, 1))
+        rhs = [stencil(base[level], weights), rest * g + (1.0 if first else 0.0)]
+        rhs += [w * x for w, x in zip(weights, around(g))]
         inverse, step = gain[level], ratio[level]
         made = tuple(x * inverse + step * r for x, r in zip(rhs, carry))
-        for i in range(2):
-            sides[i, level] = made[i]
+        for i in range(6):
+            parts[i, level] = made[i]
         return made
 
-    carry = lax.fori_loop(0, levels, forward_parts, (zero,) * 2, unroll=8)
-    back_parts(sides, upper, carry)
-    copy.wait()
+    carry = forward_parts(0, (jnp.zeros(mask.shape, jnp.float32),) * 6, first=True)
+    carry = lax.fori_loop(1, levels, forward_parts, carry, unroll=7)
+    back_parts(parts, upper, carry)
 
 
 def back_parts(parts, upper, carry):
@@ -367,15 +359,17 @@
 
 
 def late_kernel(
-    tiles, groups, state, horiz, mask, chip, core, upper, gain, ratio, impulse, _, parts, halo_wet,
-    base, halo_base, halo_impulse, halo_vert, halo_upper, rim,
+    groups, horiz, mask, chip, core, packs, _, fixes, halo_wet,
+    delta, halo_base, halo_impulse, halo_vert, halo_upper,
 ):
-    levels, height, width = state.shape
+    levels = packs.shape[1]
+    height, width = mask.shape
     cols = width // 128
     half = levels // 2
     shape = (2 * cols, 128)
     low_half = iota(shape, 0) < cols
     lane = iota(shape, 1)
+    place = iota(shape, 0) % cols
     parity = lax.axis_index("tile") % 2
     from_chip = iota(shape, 0) // cols == parity
 
@@ -388,23 +382,40 @@
     def behind(i):
         return turn(jnp.where(from_chip, core[i], chip[i]))
 
-    for c in range(cols):
-        rim[:, c, :] = state[:, 0, c * 128 : (c + 1) * 128]
-        rim[:, cols + c, :] = state[:, height - 1, c * 128 : (c + 1) * 128]
+    def packed(x, low, high):
+        return jnp.concatenate(
+            [x[r : r + 1, c * 128 : (c + 1) * 128] for r in (low, high) for c in range(cols)], 0
+        )
+
+    def shifted(x):
+        rows = x.shape[0]
+        to_right, to_left = pltpu.roll(x, 1, 1), pltpu.roll(x, 127, 1)
+        return (
+            jnp.where(lane == 0, pltpu.roll(to_right, 1, 0), to_right),
+            jnp.where(lane == 127, pltpu.roll(to_left, rows - 1, 0), to_left),
+        )
+
+    def along(scale, wet):
+        left, right = shifted(wet)
+        return (
+            scale * jnp.where((place == 0) & (lane == 0), 0.0, left),
+            scale * jnp.where((place == cols - 1) & (lane == 127), 0.0, right),
+        )
+
     wet = wet_of(lax.axis_index("grp") == groups - 1, mask[...])
+    nu = horiz[...]
+    rim_wet, next_wet = packed(wet, 0, height - 1), packed(wet, 1, height - 2)
     wet_halo = beside(levels + half)
     halo_wet[...] = wet_halo
-    weights = weights_of(
-        tiles, groups, horiz[...], wet, line_of(wet_halo, 0, cols), line_of(wet_halo, cols, cols)
-    )
     scale = beside(levels + half + 1) * wet_halo
-    wet_left, wet_right = shifted(wet_halo, lane)
-    place = iota(shape, 0) % cols
-    weight_left = scale * jnp.where((place == 0) & (lane == 0), 0.0, wet_left)
-    weight_right = scale * jnp.where((place == cols - 1) & (lane == 127), 0.0, wet_right)
-    weight_behind = scale * behind(levels + half)
-    wet_inside = [wet[r : r + 1, c * 128 : (c + 1) * 128] for r in (0, height - 1) for c in range(cols)]
-    weight_inside = scale * jnp.concatenate(wet_inside, 0)
+    halo_left, halo_right = along(scale, wet_halo)
+    halo_behind = scale * behind(levels + half)
+    halo_inside = scale * rim_wet
+    scale = packed(nu, 0, height - 1) * rim_wet
+    rim_left, rim_right = along(scale, rim_wet)
+    rim_inside = scale * next_wet
+    outside = scale * wet_halo
+    next_outside = packed(nu, 1, height - 2) * next_wet * rim_wet
 
     def spread(i, _):
         x, y = chip[levels + i], core[levels + i]
@@ -414,73 +425,87 @@
         return 0
 
     lax.fori_loop(0, half, spread, 0, unroll=4)
-    zero = jnp.zeros((height, width), jnp.float32)
-    zero_halo = jnp.zeros(shape, jnp.float32)
+    zero = jnp.zeros(shape, jnp.float32)
 
     def forward(level, carry, last=False, first=False):
-        r, low, c, x, e = carry
-        halo = beside(level)
-        r = stencil(state[level], halo, weights) * gain[level] + ratio[level] * r
-        base[level] = r
-        upp = zero_halo if last else halo_vert[level]
+        low, c, x, e, d = carry
+        halo, rim = beside(level), packs[8, level]
+        upp = zero if last else halo_vert[level]
         inverse = inverse_of(1.0 + low + upp + low * c)
         c = -upp * inverse
         step = low * inverse
-        left, right = shifted(halo, lane)
+        left, right = shifted(halo)
         field = (
             halo
-            + weight_left * (left - halo)
-            + weight_right * (right - halo)
-            + weight_behind * (behind(level) - halo)
-            + weight_inside * (rim[level] - halo)
+            + halo_left * (left - halo)
+            + halo_right * (right - halo)
+            + halo_behind * (behind(level) - halo)
+            + halo_inside * (rim - halo)
         )
         x = field * inverse + step * x
         e = inverse if first else step * e
+        d = outside * (halo - rim) * packs[1, level] + packs[2, level] * d
         halo_upper[level] = c
         halo_base[level] = x
         halo_impulse[level] = e
-        return r, upp, c, x, e
-
-    carry = forward(0, (zero,) + (zero_halo,) * 4, first=True)
+        delta[level] = d
+        return upp, c, x, e, d
+
+    carry = forward(0, (zero,) * 5, first=True)
     carry = lax.fori_loop(1, levels - 1, forward, carry, unroll=31)
-    r, _, _, x, e = forward(levels - 1, carry, last=True)
+    _, _, x, e, d = forward(levels - 1, carry, last=True)
 
     def backward(i, carry):
         level = levels - 2 - i
         c = halo_upper[level]
-        r = base[level] - upper[level] * carry[0]
-        x = halo_base[level] - c * carry[1]
-        e = halo_impulse[level] - c * carry[2]
-        base[level] = r
+        x = halo_base[level] - c * carry[0]
+        e = halo_impulse[level] - c * carry[1]
+        d = delta[level] - packs[0, level] * carry[2]
         halo_base[level] = x
         halo_impulse[level] = e
-        return r, x, e
-
-    lax.fori_loop(0, levels - 1, backward, (r, x, e), unroll=9)
-    rest = 1.0 - weights[0] - weights[1] - weights[2] - weights[3]
-
-    def forward_parts(level, carry, first=False):
-        g, halo = impulse[level], halo_impulse[level]
+        delta[level] = d
+        return x, e, d
+
+    lax.fori_loop(0, levels - 1, backward, (x, e, d), unroll=9)
+
+    def forward_fixes(level, carry):
+        d = delta[level]
+        left, right = shifted(d)
         rhs = (
-            stencil(base[level], halo_base[level], weights),
-            rest * g + (1.0 if first else 0.0),
-            weights[2] * row_above(g, halo),
-            weights[3] * row_below(g, halo),
+            d
+            + rim_left * (left - d)
+            + rim_right * (right - d)
+            - rim_inside * d
+            + outside * (halo_base[level] - (packs[7, level] + d)),
+            outside * halo_impulse[level],
+            outside * packs[6, level],
+            next_outside * d,
         )
-        inverse, step = gain[level], ratio[level]
-        made = tuple(x * inverse + step * r for x, r in zip(rhs, carry))
+        made = tuple(
+            x * packs[1 if i < 3 else 4, level] + packs[2 if i < 3 else 5, level] * r
+            for i, (x, r) in enumerate(zip(rhs, carry))
+        )
         for i in range(4):
-            parts[i, level] = made[i]
+            fixes[i, level] = made[i]
         return made
 
-    carry = forward_parts(0, (zero,) * 4, first=True)
-    carry = lax.fori_loop(1, levels, forward_parts, carry, unroll=7)
-    back_parts(parts, upper, carry)
-
-
-def last_kernel(cols, groups, mask, sides, parts, halo_wet, *refs):
+    carry = lax.fori_loop(0, levels, forward_fixes, (zero,) * 4, unroll=8)
+
+    def backward_fixes(i, carry):
+        level = levels - 2 - i
+        made = tuple(
+            fixes[j, level] - packs[0 if j < 3 else 3, level] * carry[j] for j in range(4)
+        )
+        for j in range(4):
+            fixes[j, level] = made[j]
+        return made
+
+    lax.fori_loop(0, levels - 1, backward_fixes, carry, unroll=9)
+
+
+def last_kernel(cols, groups, mask, parts, fixes, halo_wet, *refs):
     arrived = refs[: groups - 1]
-    out, received, field, sem = refs[groups - 1 :]
+    out, received_out, field, received, sem = refs[groups - 1 :]
     _, levels, height, width = parts.shape
     group = lax.axis_index("grp")
     total = jnp.zeros(arrived[0].shape, jnp.float32)
@@ -490,24 +515,36 @@
         for c in range(cols):
             at = (f * cols + c) * height
             received[f, :, c * 128 : (c + 1) * 128] = total[at : at + height, :]
+    copies = [pltpu.make_async_copy(received, received_out, sem.at[0])]
+    copies[0].start()
     wet = wet_of(lax.axis_index("grp") == groups - 1, mask[...])
     force = FORCING_GAIN * wet * jnp.sum(received[...], 0)
     force_halo = FORCING_GAIN * halo_wet[...] * total[F * cols * height :, :]
-    left, right, above, below = around(force, force_halo)
+    factors = (force,) + around(force)
+    force_rim = jnp.concatenate(
+        [force[r : r + 1, c * 128 : (c + 1) * 128] for r in (0, height - 1) for c in range(cols)], 0
+    )
 
     def level_of(level, _):
-        x = parts[0, level] + parts[1, level] * force
-        x = x + parts[2, level] * above + parts[3, level] * below
-        field[level] = x + sides[0, level] * left + sides[1, level] * right
+        x = parts[0, level]
+        for i in range(5):
+            x = x + parts[i + 1, level] * factors[i]
+        field[level] = x
         return 0
 
-    chunks = 4
+    chunks = 8
     size = levels // chunks
-    copies = []
     for i in range(chunks):
-        lax.fori_loop(i * size, (i + 1) * size, level_of, 0, unroll=4)
+        lax.fori_loop(i * size, (i + 1) * size, level_of, 0, unroll=8)
         at = pl.ds(i * size, size)
-        copies.append(pltpu.make_async_copy(field.at[at], out.at[at], sem.at[i]))
+        rims = fixes[0, at] + fixes[1, at] * force_halo[None] - fixes[2, at] * force_rim[None]
+        for c in range(cols):
+            block = pl.ds(c * 128, 128)
+            for row, fix in ((0, rims[:, c]), (height - 1, rims[:, cols + c])):
+                field[at, row, block] = field[at, row, block] + fix
+            for row, fix in ((1, c), (height - 2, cols + c)):
+                field[at, row, block] = field[at, row, block] + fixes[3, at, fix, :]
+        copies.append(pltpu.make_async_copy(field.at[at], out.at[at], sem.at[i + 1]))
         copies[-1].start()
     for copy in copies:
         copy.wait()
@@ -557,44 +594,54 @@
     )(state, coupling, surface, mask, dtile.T, dblock.T, dgroup.T, w.reshape(height, cols, K, 128, 128))
 
 
-def early(groups, vert_coef, horiz_coef, wet_mask, chunk):
-    levels, height, width = vert_coef.shape
-    full = f32(levels + 1, height, width)
+def early(groups, state, vert_coef, horiz_coef, wet_mask, chunk):
+    levels, height, width = state.shape
     return pl.pallas_call(
         functools.partial(early_kernel, groups),
-        out_shape=(full,) * 4 + (f32(2, levels + 1, height, width), f32(*chunk.shape)),
-        in_specs=[VM] * 3 + [HBM],
+        out_shape=(f32(9, levels, width // 64, 128), f32(*chunk.shape))
+        + (f32(levels, height, width),) * 5,
+        in_specs=[VM] * 4 + [HBM],
         scratch_shapes=[pltpu.SemaphoreType.DMA],
         compiler_params=params(16),
         cost_estimate=cost(3),
-    )(vert_coef, horiz_coef, wet_mask, chunk)
-
-
-def late(groups, tiles, state, horiz_coef, wet_mask, chip, core, solved, after):
-    levels, height, width = state.shape
-    full, halo = f32(levels, height, width), f32(levels, width // 64, 128)
+    )(state, vert_coef, horiz_coef, wet_mask, chunk)
+
+
+def parts_of(groups, horiz_coef, wet_mask, solved, after):
     return pl.pallas_call(
-        functools.partial(late_kernel, tiles, groups),
-        out_shape=(f32(4, levels, height, width), f32(width // 64, 128)),
-        in_specs=[VM] * 10,
-        scratch_shapes=[pltpu.VMEM(s.shape, jnp.float32) for s in [full] + [halo] * 5],
+        functools.partial(parts_kernel, groups),
+        out_shape=f32(6, *solved[0].shape),
+        in_specs=[VM] * 8,
         compiler_params=params(16),
-        cost_estimate=cost(4),
-    )(state, horiz_coef, wet_mask, chip, core, *solved, after)
-
-
-def finish(groups, wet_mask, sides, parts, halo_wet, arrived):
+        cost_estimate=cost(3),
+    )(horiz_coef, wet_mask, *solved, after)
+
+
+def late(groups, horiz_coef, wet_mask, chip, core, packs, after):
+    _, levels, rows, lanes = packs.shape
+    return pl.pallas_call(
+        functools.partial(late_kernel, groups),
+        out_shape=(f32(4, levels, rows, lanes), f32(rows, lanes)),
+        in_specs=[VM] * 6,
+        scratch_shapes=[pltpu.VMEM((levels, rows, lanes), jnp.float32)] * 5,
+        compiler_params=params(12),
+        cost_estimate=cost(2),
+    )(horiz_coef, wet_mask, chip, core, packs, after)
+
+
+def finish(groups, wet_mask, parts, fixes, halo_wet, arrived):
     _, levels, height, width = parts.shape
     return pl.pallas_call(
         functools.partial(last_kernel, width // 128, groups),
         out_shape=(f32(levels, height, width), f32(F, height, width)),
-        out_specs=(HBM, VM),
+        out_specs=(HBM, HBM),
         scratch_shapes=[
             pltpu.VMEM((levels, height, width), jnp.float32),
-            pltpu.SemaphoreType.DMA((4,)),
+            pltpu.VMEM((F, height, width), jnp.float32),
+            pltpu.SemaphoreType.DMA((8 + 1,)),
         ],
         compiler_params=params(16),
-    )(wet_mask, sides, parts, halo_wet, *arrived)
+    )(wet_mask, parts, fixes, halo_wet, *arrived)
 
 
 def local(
@@ -620,7 +667,7 @@
         for k in sorted(range(1, chips), key=lambda k: (k != chips // 2, k))
     }
     got = [moved[k] for k in range(1, chips)]
-    *solved, sides, chunk = early(groups, vert_coef, horiz_coef, wet_mask, packed[0])
+    packs, chunk, *solved = early(groups, state, vert_coef, horiz_coef, wet_mask, packed[0])
     chip, core = edges_of(groups, state, vert_coef, horiz_coef, wet_mask, chunk, got[2])
     chip = lax.ppermute(chip, axes, across)
     core = lax.ppermute(core, axes, [(i, i ^ 1) for i in range(devices)])
@@ -631,6 +678,7 @@
         compiler_params=params(8),
         cost_estimate=cost(1),
     )(chunk, *got)
+    parts = parts_of(groups, horiz_coef, wet_mask, solved, mine)
     theirs = lax.ppermute(theirs, "tile", [(i, i ^ 1) for i in range(tiles)])
     merged = pl.pallas_call(
         functools.partial(add_kernel, cols),
@@ -642,8 +690,8 @@
         lax.ppermute(merged[g], "grp", [(j, (j + g + 1) % groups) for j in range(groups)])
         for g in range(groups - 1)
     ]
-    parts, halo_wet = late(groups, tiles, state, horiz_coef, wet_mask, chip, core, solved, merged[0])
-    return finish(groups, wet_mask, sides, parts, halo_wet, arrived)
+    fixes, halo_wet = late(groups, horiz_coef, wet_mask, chip, core, packs, merged[0])
+    return finish(groups, wet_mask, parts, fixes, halo_wet, arrived)
 
 
 def solution(mesh):

time: 37.1 us -> 35.3 us (0.951)
  waiting for transfers between devices: 7.6 us -> 4.77 us
  Pallas kernels: 13.8 us -> 15.3 us
  starting transfers between devices: 13.9 us -> 13.4 us
    ppermute x1, waiting for transfers between devices: 4.31 us -> 2.2 us  [local(): chip = lax.ppermute(chip, axes, across)]
    pallas_call x2 -> x3, Pallas kernels: 6.62 us -> 8.45 us  [the longest x1 3.38 us: early(): pl.pallas_call(functools.partial(early_kernel, groups), out_shape=(f32(9,...]
    ppermute x3, waiting for transfers between devices: 1.83 us -> 1.11 us  [local(): lax.ppermute(packed[k], 'tile', [(i, (i // 2 ^ k) * 2 + i % 2) for i in r...]
    ppermute x1, starting transfers between devices: 4.25 us -> 4.97 us  [local(): chip = lax.ppermute(chip, axes, across)]
    ppermute x1, starting transfers between devices: 1.64 us -> 0.92 us  [local(): core = lax.ppermute(core, axes, [(i, i ^ 1) for i in range(devices)])]
    ppermute x3, starting transfers between devices: 3.48 us -> 3.02 us  [local(): lax.ppermute(merged[g], 'grp', [(j, (j + g + 1) % groups) for j in range(...]
  transfers between devices with their start and end apart: 9 -> 9, of which waited for: 4 -> 3; matrix products, arithmetic and copies ran while one was open for 0% -> 0% of each run, Pallas kernels for 20% -> 26%
where the time goes in v9:
time: 35.3 us; the launch traced here: 35.2 us
  Pallas kernels  15.3 us (43%)
  starting transfers between devices  13.4 us (38%)
  waiting for transfers between devices  4.77 us (14%)
  local copies, waits for them, and re-layouts  0.92 us (3%)
  between operations  0.77 us (2%)
    ppermute x1, starting transfers between devices, local(): chip = lax.ppermute(chip, axes, across)  4.97 us
    ppermute x3, starting transfers between devices, local(): lax.ppermute(packed[k], 'tile', [(i, (i // 2 ^ k) * 2 + i % 2) for i in r...  4.45 us
    pallas_call x1, Pallas kernels, pack(): pl.pallas_call(functools.partial(pack_kernel, tiles, slots, groups), out_...  4.25 us
    pallas_call x1, Pallas kernels, early(): pl.pallas_call(functools.partial(early_kernel, groups), out_shape=(f32(9,...  3.38 us
    ppermute x3, starting transfers between devices, local(): lax.ppermute(merged[g], 'grp', [(j, (j + g + 1) % groups) for j in range(...  3.02 us
    pallas_call x1, Pallas kernels, parts_of(): pl.pallas_call(functools.partial(parts_kernel, groups), out_shape=f32(6,...  2.58 us
    pallas_call x1, Pallas kernels, late(): pl.pallas_call(functools.partial(late_kernel, groups), out_shape=(f32(4,...  2.49 us
    ppermute x1, waiting for transfers between devices, local(): chip = lax.ppermute(chip, axes, across)  2.2 us
  transfers between devices with their start and end apart: 9, of which 3 were waited for; matrix products, arithmetic and copies ran while one was open for 0% of the time, Pallas kernels for 26%

profile of v9, /device:TPU:4, one launch (start us, length us, event | category | flops | bytes accessed | tf_op | source)
XLA Modules:
  0.0 35.2 jit_solution(17242212838081849511)
XLA Ops:
  0.6 0.0 copy-start.2
  0.6 0.0 copy-start
  0.7 0.0 copy-start.3
  0.7 0.0 copy-start.1
  0.7 4.2 %shard_map.113 = (f32[288,128]{1,0:T(8,128)}, f32[288,128]{1,0:T(8,128)}, f32[288,128]{1,0:T(8,128)}, f32[288,128]{1,0:T(8,128)}) custom-call(f32[64,8,512]{2,1,0:T(8,128)} %state.5, f32[4,8,512]{2,1,0:T(8,128)} %coupling.1, f32[4,8,512]{2,1,0:T(8,128)} %surface.1, s32[8,512]{1,0:T(8,128)} %mask.11, s32[4,32]{1,0:T(4,128)} %bitcast.5, s32[4,32]{1,0:T(4,128)} %bitcast.6, ...), custom_call_target="tpu_custom_call" | custom-call | bytes 9000000 | tf_op jit(solution)/shard_map/pallas_call | solution.py:576
  4.9 3.7 %collective-permute-start.2 = (f32[288,128]{1,0:T(8,128)}, f32[288,128]{1,0:T(8,128)S(1)}, u32[]{:S(2)}, u32[]{:S(2)}) collective-permute-start(f32[288,128]{1,0:T(8,128)} %get-tuple-element.31), channel_id=1, source_target_pairs={{0,6},{1,7},{2,4},{3,5},{4,2},{5,3},{6,0},{7,1},{8,14},{9,15},{10,... | collective-permute-start | bytes 442376 | tf_op jit(solution)/shard_map/ppermute | solution.py:666
  8.6 0.0 collective-permute-start
  8.6 0.8 %collective-permute-start.1 = (f32[288,128]{1,0:T(8,128)}, f32[288,128]{1,0:T(8,128)S(1)}, u32[]{:S(2)}, u32[]{:S(2)}) collective-permute-start(f32[288,128]{1,0:T(8,128)} %get-tuple-element.30), channel_id=1, source_target_pairs={{0,4},{1,5},{2,6},{3,7},{4,0},{5,1},{6,2},{7,3},{8,12},{9,13},{10,... | collective-permute-start | bytes 442376 | tf_op jit(solution)/shard_map/ppermute | solution.py:666
  9.4 0.0 copy-done.3
  9.4 0.0 copy-start.4
  9.4 0.9 %copy-done.4 = f32[288,128]{1,0:T(8,128)S(1)} copy-done((f32[288,128]{1,0:T(8,128)S(1)}, f32[288,128]{1,0:T(8,128)}, u32[]{:S(2)}) %copy-start.4) | copy-done | bytes 147480
  10.3 3.4 %shard_map.114 = (f32[9,64,8,128]{3,2,1,0:T(8,128)S(1)}, f32[288,128]{1,0:T(8,128)S(1)}, f32[64,8,512]{2,1,0:T(8,128)S(1)}, f32[64,8,512]{2,1,0:T(8,128)S(1)}, f...) custom-call(f32[64,8,512]{2,1,0:T(8,128)S(1)} %copy-done, ...), custom_call_target="tpu_custom_call" | custom-call | bytes 9000000 | tf_op jit(solution)/shard_map/pallas_call | solution.py:599
  13.7 0.0 collective-permute-done.2.refs_3_.refs_1_
  13.7 0.6 %shard_map.117 = (f32[98,8,128]{2,1,0:T(8,128)S(1)}, f32[98,8,128]{2,1,0:T(8,128)S(1)}) custom-call(f32[64,8,512]{2,1,0:T(8,128)S(1)} %copy-done, f32[63,8,512]{2,1,0:T(8,128)S(1)} %copy-done.1, f32[8,512]{1,0:T(8,128)S(1)} %copy-done.3, s32[8,512]{1,0:T(8,128)S(1)} %copy-done.2, f32[288,128]{1,0:T(8,128)S(1)} %get-tuple-element.28.refs_0_, ...), custom_call_target="tpu_custom_call" | custom-call | bytes 3000000 | tf_op jit(solution)/shard_map/pallas_call | solution.py:563
  14.3 5.0 %collective-permute-start.3 = (f32[98,8,128]{2,1,0:T(8,128)S(1)}, f32[98,8,128]{2,1,0:T(8,128)S(1)}, u32[]{:S(2)}, u32[]{:S(2)}) collective-permute-start(f32[98,8,128]{2,1,0:T(8,128)S(1)} %get-tuple-element.33), channel_id=1, source_target_pairs={{1,2},{3,4},{5,6},{7,8},{9,10},{11,12},{13,14},{15,16},{17,18},{19... | collective-permute-start | bytes 1204232 | tf_op jit(solution)/shard_map/ppermute | solution.py:672
  19.3 0.9 %collective-permute-start.4 = (f32[98,8,128]{2,1,0:T(8,128)S(1)}, f32[98,8,128]{2,1,0:T(8,128)S(1)}, u32[]{:S(2)}, u32[]{:S(2)}) collective-permute-start(f32[98,8,128]{2,1,0:T(8,128)S(1)} %get-tuple-element.34), channel_id=1, source_target_pairs={{0,1},{1,0},{2,3},{3,2},{4,5},{5,4},{6,7},{7,6},{8,9},{9,8},{10,11... | collective-permute-start | bytes 1204232 | tf_op jit(solution)/shard_map/ppermute | solution.py:673
  20.2 0.0 collective-permute-done.refs_1_
  20.2 1.1 %collective-permute-done.1.refs_2_ = f32[288,128]{1,0:T(8,128)S(1)} collective-permute-done((f32[288,128]{1,0:T(8,128)}, f32[288,128]{1,0:T(8,128)S(1)}, u32[]{:S(2)}, u32[]{:S(2)}) %collective-permute-start.1) | collective-permute-done | bytes 147488 | tf_op jit(solution)/shard_map/ppermute | solution.py:666
  21.3 0.3 shard_map.115
  21.6 0.1 collective-permute-start.5
  21.6 1.4 %collective-permute-done.5.theirs = f32[408,128]{1,0:T(8,128)S(1)} collective-permute-done((f32[408,128]{1,0:T(8,128)S(1)}, f32[408,128]{1,0:T(8,128)S(1)}, u32[]{:S(2)}, u32[]{:S(2)}) %collective-permute-start.5) | collective-permute-done | bytes 208928 | tf_op jit(solution)/shard_map/ppermute | solution.py:682
  23.1 0.6 %collective-permute-start.7 = (f32[136,128]{1,0:T(8,128)S(1)}, f32[136,128]{1,0:T(8,128)S(1)}, u32[]{:S(2)}, u32[]{:S(2)}) collective-permute-start(f32[136,128]{1,0:T(8,128)S(1)} %get-tuple-element.40), channel_id=1, source_target_pairs={{0,16},{8,24},{16,0},{24,8},{1,17},{9,25},{17,1},{25,9},{2,18},{10... | collective-permute-start | bytes 208904 | tf_op jit(solution)/shard_map/ppermute | solution.py:690
  23.7 2.4 %collective-permute-start.8 = (f32[136,128]{1,0:T(8,128)S(1)}, f32[136,128]{1,0:T(8,128)S(1)}, u32[]{:S(2)}, u32[]{:S(2)}) collective-permute-start(f32[136,128]{1,0:T(8,128)S(1)} %get-tuple-element.41), channel_id=1, source_target_pairs={{0,24},{8,0},{16,8},{24,16},{1,25},{9,1},{17,9},{25,17},{2,26},{10... | collective-permute-start | bytes 208904 | tf_op jit(solution)/shard_map/ppermute | solution.py:690
  26.1 0.0 collective-permute-start.6
  26.1 2.6 %shard_map.116.parts = f32[6,64,8,512]{3,2,1,0:T(8,128)S(1)} custom-call(f32[8,512]{1,0:T(8,128)S(1)} %copy-done.3, s32[8,512]{1,0:T(8,128)S(1)} %copy-done.2, f32[64,8,512]{2,1,0:T(8,128)S(1)} %get-tuple-element.23.upper, f32[64,8,512]{2,1,0:T(8,128)S(1)} %get-tuple-element.24.gain, f32[64,8,512]{2,1,0:T(8,128)S(1)} %get-tuple-element.25.ratio, ...), custom_call_target="tpu_custom_call" | custom-call | bytes 9000000 | tf_op jit(solution)/shard_map/pallas_call | solution.py:611
  28.7 2.2 %collective-permute-done.3.chip = f32[98,8,128]{2,1,0:T(8,128)S(1)} collective-permute-done((f32[98,8,128]{2,1,0:T(8,128)S(1)}, f32[98,8,128]{2,1,0:T(8,128)S(1)}, u32[]{:S(2)}, u32[]{:S(2)}) %collective-permute-start.3) | collective-permute-done | bytes 401440 | tf_op jit(solution)/shard_map/ppermute | solution.py:672
  30.9 0.0 collective-permute-done.4.core
  30.9 2.5 %shard_map.119 = (f32[4,64,8,128]{3,2,1,0:T(8,128)S(1)}, f32[8,128]{1,0:T(8,128)S(1)}) custom-call(f32[8,512]{1,0:T(8,128)S(1)} %copy-done.3, s32[8,512]{1,0:T(8,128)S(1)} %copy-done.2, f32[98,8,128]{2,1,0:T(8,128)S(1)} %collective-permute-done.3.chip, f32[98,8,128]{2,1,0:T(8,128)S(1)} %collective-permute-done.4.core, ...), custom_call_target="tpu_custom_call" | custom-call | bytes 6000000 | tf_op jit(solution)/shard_map/pallas_call | solution.py:622
  33.4 0.0 collective-permute-done.7.refs_1_
  33.4 0.0 collective-permute-done.8.refs_2_
  33.4 0.0 collective-permute-done.6.refs_0_
  33.5 1.7 %shard_map.120 = (f32[64,8,512]{2,1,0:T(8,128)}, f32[4,8,512]{2,1,0:T(8,128)}) custom-call(s32[8,512]{1,0:T(8,128)S(1)} %copy-done.2, f32[6,64,8,512]{3,2,1,0:T(8,128)S(1)} %shard_map.116.parts, f32[4,64,8,128]{3,2,1,0:T(8,128)S(1)} %get-tuple-element.38.fixes, f32[8,128]{1,0:T(8,128)S(1)} %get-tuple-element.39.halo_wet, ...), custom_call_target="tpu_custom_call" | custom-call | tf_op jit(solution)/shard_map/pallas_call | solution.py:634
  (4 shorter events, 0.0 us)
Async XLA Ops:
  0.6 8.8 %copy-start.2 = (s32[8,512]{1,0:T(8,128)S(1)}, s32[8,512]{1,0:T(8,128)}, u32[]{:S(2)}) copy-start(s32[8,512]{1,0:T(8,128)} %mask.11) | copy-start | bytes 49156
  0.6 8.7 %copy-start = (f32[64,8,512]{2,1,0:T(8,128)S(1)}, f32[64,8,512]{2,1,0:T(8,128)}, u32[]{:S(2)}) copy-start(f32[64,8,512]{2,1,0:T(8,128)} %state.5) | copy-start | bytes 3145732
  0.7 8.7 %copy-start.3 = (f32[8,512]{1,0:T(8,128)S(1)}, f32[8,512]{1,0:T(8,128)}, u32[]{:S(2)}) copy-start(f32[8,512]{1,0:T(8,128)} %horiz.7) | copy-start | bytes 49156
  0.7 8.7 %copy-start.1 = (f32[63,8,512]{2,1,0:T(8,128)S(1)}, f32[63,8,512]{2,1,0:T(8,128)}, u32[]{:S(2)}) copy-start(f32[63,8,512]{2,1,0:T(8,128)} %vert.3) | copy-start | bytes 3096580
  4.9 8.8 %collective-permute-start.2 = (f32[288,128]{1,0:T(8,128)}, f32[288,128]{1,0:T(8,128)S(1)}, u32[]{:S(2)}, u32[]{:S(2)}) collective-permute-start(f32[288,128]{1,0:T(8,128)} %get-tuple-element.31), channel_id=1, source_target_pairs={{0,6},{1,7},{2,4},{3,5},{4,2},{5,3},{6,0},{7,1},{8,14},{9,15},{10,... | collective-permute-start | bytes 442376 | tf_op jit(solution)/shard_map/ppermute | solution.py:666
  8.6 11.6 %collective-permute-start = (f32[288,128]{1,0:T(8,128)}, f32[288,128]{1,0:T(8,128)S(1)}, u32[]{:S(2)}, u32[]{:S(2)}) collective-permute-start(f32[288,128]{1,0:T(8,128)} %get-tuple-element.29), channel_id=1, source_target_pairs={{0,2},{1,3},{2,0},{3,1},{4,6},{5,7},{6,4},{7,5},{8,10},{9,11},{10,... | collective-permute-start | bytes 442376 | tf_op jit(solution)/shard_map/ppermute | solution.py:666
  8.6 12.7 %collective-permute-start.1 = (f32[288,128]{1,0:T(8,128)}, f32[288,128]{1,0:T(8,128)S(1)}, u32[]{:S(2)}, u32[]{:S(2)}) collective-permute-start(f32[288,128]{1,0:T(8,128)} %get-tuple-element.30), channel_id=1, source_target_pairs={{0,4},{1,5},{2,6},{3,7},{4,0},{5,1},{6,2},{7,3},{8,12},{9,13},{10,... | collective-permute-start | bytes 442376 | tf_op jit(solution)/shard_map/ppermute | solution.py:666
  9.4 0.9 %copy-start.4 = (f32[288,128]{1,0:T(8,128)S(1)}, f32[288,128]{1,0:T(8,128)}, u32[]{:S(2)}) copy-start(f32[288,128]{1,0:T(8,128)} %get-tuple-element.22.chunk) | copy-start | bytes 442372
  14.3 16.6 %collective-permute-start.3 = (f32[98,8,128]{2,1,0:T(8,128)S(1)}, f32[98,8,128]{2,1,0:T(8,128)S(1)}, u32[]{:S(2)}, u32[]{:S(2)}) collective-permute-start(f32[98,8,128]{2,1,0:T(8,128)S(1)} %get-tuple-element.33), channel_id=1, source_target_pairs={{1,2},{3,4},{5,6},{7,8},{9,10},{11,12},{13,14},{15,16},{17,18},{19... | collective-permute-start | bytes 1204232 | tf_op jit(solution)/shard_map/ppermute | solution.py:672
  19.3 11.6 %collective-permute-start.4 = (f32[98,8,128]{2,1,0:T(8,128)S(1)}, f32[98,8,128]{2,1,0:T(8,128)S(1)}, u32[]{:S(2)}, u32[]{:S(2)}) collective-permute-start(f32[98,8,128]{2,1,0:T(8,128)S(1)} %get-tuple-element.34), channel_id=1, source_target_pairs={{0,1},{1,0},{2,3},{3,2},{4,5},{5,4},{6,7},{7,6},{8,9},{9,8},{10,11... | collective-permute-start | bytes 1204232 | tf_op jit(solution)/shard_map/ppermute | solution.py:673
  21.6 1.5 %collective-permute-start.5 = (f32[408,128]{1,0:T(8,128)S(1)}, f32[408,128]{1,0:T(8,128)S(1)}, u32[]{:S(2)}, u32[]{:S(2)}) collective-permute-start(f32[408,128]{1,0:T(8,128)S(1)} %get-tuple-element.36), channel_id=1, source_target_pairs={{0,1},{1,0},{2,3},{3,2},{4,5},{5,4},{6,7},{7,6},{8,9},{9,8},{10,11... | collective-permute-start | bytes 626696 | tf_op jit(solution)/shard_map/ppermute | solution.py:682
  23.1 10.3 %collective-permute-start.7 = (f32[136,128]{1,0:T(8,128)S(1)}, f32[136,128]{1,0:T(8,128)S(1)}, u32[]{:S(2)}, u32[]{:S(2)}) collective-permute-start(f32[136,128]{1,0:T(8,128)S(1)} %get-tuple-element.40), channel_id=1, source_target_pairs={{0,16},{8,24},{16,0},{24,8},{1,17},{9,25},{17,1},{25,9},{2,18},{10... | collective-permute-start | bytes 208904 | tf_op jit(solution)/shard_map/ppermute | solution.py:690
  23.7 9.8 %collective-permute-start.8 = (f32[136,128]{1,0:T(8,128)S(1)}, f32[136,128]{1,0:T(8,128)S(1)}, u32[]{:S(2)}, u32[]{:S(2)}) collective-permute-start(f32[136,128]{1,0:T(8,128)S(1)} %get-tuple-element.41), channel_id=1, source_target_pairs={{0,24},{8,0},{16,8},{24,16},{1,25},{9,1},{17,9},{25,17},{2,26},{10... | collective-permute-start | bytes 208904 | tf_op jit(solution)/shard_map/ppermute | solution.py:690
  26.1 7.3 %collective-permute-start.6 = (f32[136,128]{1,0:T(8,128)S(1)}, f32[136,128]{1,0:T(8,128)S(1)}, u32[]{:S(2)}, u32[]{:S(2)}) collective-permute-start(f32[136,128]{1,0:T(8,128)S(1)} %get-tuple-element.37._), channel_id=1, source_target_pairs={{0,8},{8,16},{16,24},{24,0},{1,9},{9,17},{17,25},{25,1},{2,10},{10... | collective-permute-start | bytes 208904 | tf_op jit(solution)/shard_map/ppermute | solution.py:690

commit v10 on v9

--- a/solution.py
+++ b/solution.py
@@ -340,7 +340,7 @@
         return made
 
     carry = forward_parts(0, (jnp.zeros(mask.shape, jnp.float32),) * 6, first=True)
-    carry = lax.fori_loop(1, levels, forward_parts, carry, unroll=7)
+    carry = lax.fori_loop(1, levels, forward_parts, carry, unroll=21)
     back_parts(parts, upper, carry)
 
 
@@ -355,7 +355,7 @@
             parts[j, level] = made[j]
         return made
 
-    lax.fori_loop(0, levels - 1, backward, carry, unroll=9)
+    lax.fori_loop(0, levels - 1, backward, carry, unroll=21)
 
 
 def late_kernel(
@@ -417,56 +417,82 @@
     outside = scale * wet_halo
     next_outside = packed(nu, 1, height - 2) * next_wet * rim_wet
 
+    zero = jnp.zeros(shape, jnp.float32)
+    halo_vert[0] = zero
+
     def spread(i, _):
         x, y = chip[levels + i], core[levels + i]
         a, b = jnp.where(parity == 0, x, y), jnp.where(parity == 0, y, x)
-        halo_vert[i] = jnp.where(low_half, a, turn(b)) * wet_halo
-        halo_vert[half + i] = jnp.where(low_half, turn(a), b) * wet_halo
+        halo_vert[i + 1] = jnp.where(low_half, a, turn(b)) * wet_halo
+        halo_vert[half + i + 1] = jnp.where(low_half, turn(a), b) * wet_halo
         return 0
 
     lax.fori_loop(0, half, spread, 0, unroll=4)
-    zero = jnp.zeros(shape, jnp.float32)
-
-    def forward(level, carry, last=False, first=False):
-        low, c, x, e, d = carry
-        halo, rim = beside(level), packs[8, level]
-        upp = zero if last else halo_vert[level]
-        inverse = inverse_of(1.0 + low + upp + low * c)
-        c = -upp * inverse
-        step = low * inverse
+
+    def moved(level):
+        halo = beside(level)
         left, right = shifted(halo)
-        field = (
+        return (
             halo
             + halo_left * (left - halo)
             + halo_right * (right - halo)
             + halo_behind * (behind(level) - halo)
-            + halo_inside * (rim - halo)
+            + halo_inside * (packs[8, level] - halo)
         )
-        x = field * inverse + step * x
-        e = inverse if first else step * e
-        d = outside * (halo - rim) * packs[1, level] + packs[2, level] * d
-        halo_upper[level] = c
-        halo_base[level] = x
-        halo_impulse[level] = e
-        delta[level] = d
-        return upp, c, x, e, d
-
-    carry = forward(0, (zero,) * 5, first=True)
-    carry = lax.fori_loop(1, levels - 1, forward, carry, unroll=31)
-    _, _, x, e, d = forward(levels - 1, carry, last=True)
+
+    def forward(i, carry):
+        c, x, e, b, y, d = carry
+        j = levels - 1 - i
+        low, upp = halo_vert[i], halo_vert[i + 1]
+        inverse = inverse_of(1.0 + low + upp + low * c)
+        c = -upp * inverse
+        step = low * inverse
+        x = moved(i) * inverse + step * x
+        e = jnp.where(i == 0, inverse, 0.0) + step * e
+        halo_upper[i] = c
+        halo_base[i] = x
+        halo_impulse[i] = e
+        low, upp = halo_vert[j], halo_vert[j + 1]
+        inverse = inverse_of(1.0 + low + upp + upp * b)
+        b = -low * inverse
+        y = moved(j) * inverse + upp * inverse * y
+        halo_upper[j] = b
+        halo_base[j] = y
+        for level in (2 * i, 2 * i + 1):
+            rhs = outside * (beside(level) - packs[8, level])
+            d = rhs * packs[1, level] + packs[2, level] * d
+            delta[level] = d
+        return c, x, e, b, y, d
+
+    c, x, e, b, y, d = lax.fori_loop(0, half, forward, (zero,) * 6, unroll=16)
+    inverse = 1.0 / (1.0 - c * b)
+    x = (x - c * y) * inverse
+    e = e * inverse
+    y = y - b * x
+    h = -b * e
+    for level, base, impulse in ((half - 1, x, e), (half, y, h)):
+        halo_base[level] = base
+        halo_impulse[level] = impulse
 
     def backward(i, carry):
-        level = levels - 2 - i
-        c = halo_upper[level]
-        x = halo_base[level] - c * carry[0]
-        e = halo_impulse[level] - c * carry[1]
-        d = delta[level] - packs[0, level] * carry[2]
-        halo_base[level] = x
-        halo_impulse[level] = e
-        delta[level] = d
-        return x, e, d
-
-    lax.fori_loop(0, levels - 1, backward, (x, e, d), unroll=9)
+        x, e, y, h, d = carry
+        at, j = half - 2 - i, half + 1 + i
+        c, b = halo_upper[at], halo_upper[j]
+        x = halo_base[at] - c * x
+        e = halo_impulse[at] - c * e
+        y = halo_base[j] - b * y
+        h = -b * h
+        halo_base[at] = x
+        halo_impulse[at] = e
+        halo_base[j] = y
+        halo_impulse[j] = h
+        for level in (levels - 2 - 2 * i, levels - 3 - 2 * i):
+            d = delta[level] - packs[0, level] * d
+            delta[level] = d
+        return x, e, y, h, d
+
+    *_, d = lax.fori_loop(0, half - 1, backward, (x, e, y, h, d), unroll=31)
+    delta[0] = delta[0] - packs[0, 0] * d
 
     def forward_fixes(level, carry):
         d = delta[level]
@@ -489,7 +515,7 @@
             fixes[i, level] = made[i]
         return made
 
-    carry = lax.fori_loop(0, levels, forward_fixes, (zero,) * 4, unroll=8)
+    carry = lax.fori_loop(0, levels, forward_fixes, (zero,) * 4, unroll=16)
 
     def backward_fixes(i, carry):
         level = levels - 2 - i
@@ -500,12 +526,12 @@
             fixes[j, level] = made[j]
         return made
 
-    lax.fori_loop(0, levels - 1, backward_fixes, carry, unroll=9)
+    lax.fori_loop(0, levels - 1, backward_fixes, carry, unroll=21)
 
 
 def last_kernel(cols, groups, mask, parts, fixes, halo_wet, *refs):
     arrived = refs[: groups - 1]
-    out, received_out, field, received, sem = refs[groups - 1 :]
+    out, received_out, field, received, rims, sem = refs[groups - 1 :]
     _, levels, height, width = parts.shape
     group = lax.axis_index("grp")
     total = jnp.zeros(arrived[0].shape, jnp.float32)
@@ -525,11 +551,20 @@
         [force[r : r + 1, c * 128 : (c + 1) * 128] for r in (0, height - 1) for c in range(cols)], 0
     )
 
+    rims[...] = fixes[0] + fixes[1] * force_halo[None] - fixes[2] * force_rim[None]
+    row = iota((height, 128), 0)
+
     def level_of(level, _):
-        x = parts[0, level]
-        for i in range(5):
-            x = x + parts[i + 1, level] * factors[i]
-        field[level] = x
+        for c in range(cols):
+            at = slice(c * 128, (c + 1) * 128)
+            x = parts[0, level, :, at]
+            for i in range(5):
+                x = x + parts[i + 1, level, :, at] * factors[i][:, at]
+            one, two = slice(c, c + 1), slice(cols + c, cols + c + 1)
+            fix = jnp.where(row == 0, rims[level, one, :], rims[level, two, :])
+            near = jnp.where(row == 1, fixes[3, level, one, :], fixes[3, level, two, :])
+            x = x + jnp.where((row == 0) | (row == height - 1), fix, 0.0)
+            field[level, :, at] = x + jnp.where((row == 1) | (row == height - 2), near, 0.0)
         return 0
 
     chunks = 8
@@ -537,13 +572,6 @@
     for i in range(chunks):
         lax.fori_loop(i * size, (i + 1) * size, level_of, 0, unroll=8)
         at = pl.ds(i * size, size)
-        rims = fixes[0, at] + fixes[1, at] * force_halo[None] - fixes[2, at] * force_rim[None]
-        for c in range(cols):
-            block = pl.ds(c * 128, 128)
-            for row, fix in ((0, rims[:, c]), (height - 1, rims[:, cols + c])):
-                field[at, row, block] = field[at, row, block] + fix
-            for row, fix in ((1, c), (height - 2, cols + c)):
-                field[at, row, block] = field[at, row, block] + fixes[3, at, fix, :]
         copies.append(pltpu.make_async_copy(field.at[at], out.at[at], sem.at[i + 1]))
         copies[-1].start()
     for copy in copies:
@@ -623,7 +651,9 @@
         functools.partial(late_kernel, groups),
         out_shape=(f32(4, levels, rows, lanes), f32(rows, lanes)),
         in_specs=[VM] * 6,
-        scratch_shapes=[pltpu.VMEM((levels, rows, lanes), jnp.float32)] * 5,
+        scratch_shapes=[pltpu.VMEM((levels, rows, lanes), jnp.float32)] * 3
+        + [pltpu.VMEM((levels + 1, rows, lanes), jnp.float32)]
+        + [pltpu.VMEM((levels, rows, lanes), jnp.float32)],
         compiler_params=params(12),
         cost_estimate=cost(2),
     )(horiz_coef, wet_mask, chip, core, packs, after)
@@ -638,6 +668,7 @@
         scratch_shapes=[
             pltpu.VMEM((levels, height, width), jnp.float32),
             pltpu.VMEM((F, height, width), jnp.float32),
+            pltpu.VMEM((levels, width // 64, 128), jnp.float32),
             pltpu.SemaphoreType.DMA((8 + 1,)),
         ],
         compiler_params=params(16),

time: 35.3 us -> 34.4 us (0.975)
  Pallas kernels: 15.3 us -> 13.9 us
    pallas_call x1, Pallas kernels: 2.49 us -> 1.61 us  [late(): pl.pallas_call(functools.partial(late_kernel, groups), out_shape=(f32(4,...]
  transfers between devices with their start and end apart: 9 -> 9, of which waited for: 3 -> 3; matrix products, arithmetic and copies ran while one was open for 0% -> 0% of each run, Pallas kernels for 26% -> 24%
where the time goes in v10:
time: 34.4 us; the launch traced here: 34 us
  Pallas kernels  13.9 us (40%)
  starting transfers between devices  13.4 us (39%)
  waiting for transfers between devices  5.01 us (15%)
  local copies, waits for them, and re-layouts  0.92 us (3%)
  between operations  0.77 us (2%)
    ppermute x1, starting transfers between devices, local(): chip = lax.ppermute(chip, axes, across)  4.97 us
    ppermute x3, starting transfers between devices, local(): lax.ppermute(packed[k], 'tile', [(i, (i // 2 ^ k) * 2 + i % 2) for i in r...  4.45 us
    pallas_call x1, Pallas kernels, pack(): pl.pallas_call(functools.partial(pack_kernel, tiles, slots, groups), out_...  4.25 us
    pallas_call x1, Pallas kernels, early(): pl.pallas_call(functools.partial(early_kernel, groups), out_shape=(f32(9,...  3.38 us
    ppermute x3, starting transfers between devices, local(): lax.ppermute(merged[g], 'grp', [(j, (j + g + 1) % groups) for j in range(...  3.02 us
    ppermute x1, waiting for transfers between devices, local(): chip = lax.ppermute(chip, axes, across)  2.44 us
    pallas_call x1, Pallas kernels, parts_of(): pl.pallas_call(functools.partial(parts_kernel, groups), out_shape=f32(6,...  2.34 us
    pallas_call x1, Pallas kernels, late(): pl.pallas_call(functools.partial(late_kernel, groups), out_shape=(f32(4,...  1.61 us
  transfers between devices with their start and end apart: 9, of which 3 were waited for; matrix products, arithmetic and copies ran while one was open for 0% of the time, Pallas kernels for 24%

profile of v10, /device:TPU:4, one launch (start us, length us, event | category | flops | bytes accessed | tf_op | source)
XLA Modules:
  0.0 34.0 jit_solution(6951940817208844963)
XLA Ops:
  0.6 0.0 copy-start.2
  0.6 0.0 copy-start
  0.7 0.0 copy-start.3
  0.7 0.0 copy-start.1
  0.7 4.2 %shard_map.113 = (f32[288,128]{1,0:T(8,128)}, f32[288,128]{1,0:T(8,128)}, f32[288,128]{1,0:T(8,128)}, f32[288,128]{1,0:T(8,128)}) custom-call(f32[64,8,512]{2,1,0:T(8,128)} %state.5, f32[4,8,512]{2,1,0:T(8,128)} %coupling.1, f32[4,8,512]{2,1,0:T(8,128)} %surface.1, s32[8,512]{1,0:T(8,128)} %mask.11, s32[4,32]{1,0:T(4,128)} %bitcast.5, s32[4,32]{1,0:T(4,128)} %bitcast.6, ...), custom_call_target="tpu_custom_call" | custom-call | bytes 9000000 | tf_op jit(solution)/shard_map/pallas_call | solution.py:604
  4.9 3.7 %collective-permute-start.2 = (f32[288,128]{1,0:T(8,128)}, f32[288,128]{1,0:T(8,128)S(1)}, u32[]{:S(2)}, u32[]{:S(2)}) collective-permute-start(f32[288,128]{1,0:T(8,128)} %get-tuple-element.31), channel_id=1, source_target_pairs={{0,6},{1,7},{2,4},{3,5},{4,2},{5,3},{6,0},{7,1},{8,14},{9,15},{10,... | collective-permute-start | bytes 442376 | tf_op jit(solution)/shard_map/ppermute | solution.py:697
  8.6 0.0 collective-permute-start
  8.6 0.8 %collective-permute-start.1 = (f32[288,128]{1,0:T(8,128)}, f32[288,128]{1,0:T(8,128)S(1)}, u32[]{:S(2)}, u32[]{:S(2)}) collective-permute-start(f32[288,128]{1,0:T(8,128)} %get-tuple-element.30), channel_id=1, source_target_pairs={{0,4},{1,5},{2,6},{3,7},{4,0},{5,1},{6,2},{7,3},{8,12},{9,13},{10,... | collective-permute-start | bytes 442376 | tf_op jit(solution)/shard_map/ppermute | solution.py:697
  9.4 0.0 copy-done.2
  9.4 0.0 copy-start.4
  9.4 0.9 %copy-done.4 = f32[288,128]{1,0:T(8,128)S(1)} copy-done((f32[288,128]{1,0:T(8,128)S(1)}, f32[288,128]{1,0:T(8,128)}, u32[]{:S(2)}) %copy-start.4) | copy-done | bytes 147480
  10.3 3.4 %shard_map.114 = (f32[9,64,8,128]{3,2,1,0:T(8,128)S(1)}, f32[288,128]{1,0:T(8,128)S(1)}, f32[64,8,512]{2,1,0:T(8,128)S(1)}, f32[64,8,512]{2,1,0:T(8,128)S(1)}, f...) custom-call(f32[64,8,512]{2,1,0:T(8,128)S(1)} %copy-done, ...), custom_call_target="tpu_custom_call" | custom-call | bytes 9000000 | tf_op jit(solution)/shard_map/pallas_call | solution.py:627
  13.7 0.0 collective-permute-done.2.refs_3_.refs_1_
  13.7 0.6 %shard_map.117 = (f32[98,8,128]{2,1,0:T(8,128)S(1)}, f32[98,8,128]{2,1,0:T(8,128)S(1)}) custom-call(f32[64,8,512]{2,1,0:T(8,128)S(1)} %copy-done, f32[63,8,512]{2,1,0:T(8,128)S(1)} %copy-done.1, f32[8,512]{1,0:T(8,128)S(1)} %copy-done.3, s32[8,512]{1,0:T(8,128)S(1)} %copy-done.2, f32[288,128]{1,0:T(8,128)S(1)} %get-tuple-element.28.refs_0_, ...), custom_call_target="tpu_custom_call" | custom-call | bytes 3000000 | tf_op jit(solution)/shard_map/pallas_call | solution.py:591
  14.3 5.0 %collective-permute-start.3 = (f32[98,8,128]{2,1,0:T(8,128)S(1)}, f32[98,8,128]{2,1,0:T(8,128)S(1)}, u32[]{:S(2)}, u32[]{:S(2)}) collective-permute-start(f32[98,8,128]{2,1,0:T(8,128)S(1)} %get-tuple-element.33), channel_id=1, source_target_pairs={{1,2},{3,4},{5,6},{7,8},{9,10},{11,12},{13,14},{15,16},{17,18},{19... | collective-permute-start | bytes 1204232 | tf_op jit(solution)/shard_map/ppermute | solution.py:703
  19.3 0.9 %collective-permute-start.4 = (f32[98,8,128]{2,1,0:T(8,128)S(1)}, f32[98,8,128]{2,1,0:T(8,128)S(1)}, u32[]{:S(2)}, u32[]{:S(2)}) collective-permute-start(f32[98,8,128]{2,1,0:T(8,128)S(1)} %get-tuple-element.34), channel_id=1, source_target_pairs={{0,1},{1,0},{2,3},{3,2},{4,5},{5,4},{6,7},{7,6},{8,9},{9,8},{10,11... | collective-permute-start | bytes 1204232 | tf_op jit(solution)/shard_map/ppermute | solution.py:704
  20.2 0.0 collective-permute-done.refs_1_
  20.2 1.1 %collective-permute-done.1.refs_2_ = f32[288,128]{1,0:T(8,128)S(1)} collective-permute-done((f32[288,128]{1,0:T(8,128)}, f32[288,128]{1,0:T(8,128)S(1)}, u32[]{:S(2)}, u32[]{:S(2)}) %collective-permute-start.1) | collective-permute-done | bytes 147488 | tf_op jit(solution)/shard_map/ppermute | solution.py:697
  21.3 0.3 shard_map.115
  21.6 0.1 collective-permute-start.5
  21.6 1.4 %collective-permute-done.5.theirs = f32[408,128]{1,0:T(8,128)S(1)} collective-permute-done((f32[408,128]{1,0:T(8,128)S(1)}, f32[408,128]{1,0:T(8,128)S(1)}, u32[]{:S(2)}, u32[]{:S(2)}) %collective-permute-start.5) | collective-permute-done | bytes 208928 | tf_op jit(solution)/shard_map/ppermute | solution.py:713
  23.1 0.6 %collective-permute-start.7 = (f32[136,128]{1,0:T(8,128)S(1)}, f32[136,128]{1,0:T(8,128)S(1)}, u32[]{:S(2)}, u32[]{:S(2)}) collective-permute-start(f32[136,128]{1,0:T(8,128)S(1)} %get-tuple-element.40), channel_id=1, source_target_pairs={{0,16},{8,24},{16,0},{24,8},{1,17},{9,25},{17,1},{25,9},{2,18},{10... | collective-permute-start | bytes 208904 | tf_op jit(solution)/shard_map/ppermute | solution.py:721
  23.7 2.4 %collective-permute-start.8 = (f32[136,128]{1,0:T(8,128)S(1)}, f32[136,128]{1,0:T(8,128)S(1)}, u32[]{:S(2)}, u32[]{:S(2)}) collective-permute-start(f32[136,128]{1,0:T(8,128)S(1)} %get-tuple-element.41), channel_id=1, source_target_pairs={{0,24},{8,0},{16,8},{24,16},{1,25},{9,1},{17,9},{25,17},{2,26},{10... | collective-permute-start | bytes 208904 | tf_op jit(solution)/shard_map/ppermute | solution.py:721
  26.1 0.0 collective-permute-start.6
  26.1 2.3 %shard_map.116.parts = f32[6,64,8,512]{3,2,1,0:T(8,128)S(1)} custom-call(f32[8,512]{1,0:T(8,128)S(1)} %copy-done.3, s32[8,512]{1,0:T(8,128)S(1)} %copy-done.2, f32[64,8,512]{2,1,0:T(8,128)S(1)} %get-tuple-element.23.upper, f32[64,8,512]{2,1,0:T(8,128)S(1)} %get-tuple-element.24.gain, f32[64,8,512]{2,1,0:T(8,128)S(1)} %get-tuple-element.25.ratio, ...), custom_call_target="tpu_custom_call" | custom-call | bytes 9000000 | tf_op jit(solution)/shard_map/pallas_call | solution.py:639
  28.5 2.4 %collective-permute-done.3.chip = f32[98,8,128]{2,1,0:T(8,128)S(1)} collective-permute-done((f32[98,8,128]{2,1,0:T(8,128)S(1)}, f32[98,8,128]{2,1,0:T(8,128)S(1)}, u32[]{:S(2)}, u32[]{:S(2)}) %collective-permute-start.3) | collective-permute-done | bytes 401440 | tf_op jit(solution)/shard_map/ppermute | solution.py:703
  30.9 0.0 collective-permute-done.4.core
  30.9 1.6 %shard_map.119 = (f32[4,64,8,128]{3,2,1,0:T(8,128)S(1)}, f32[8,128]{1,0:T(8,128)S(1)}) custom-call(f32[8,512]{1,0:T(8,128)S(1)} %copy-done.3, s32[8,512]{1,0:T(8,128)S(1)} %copy-done.2, f32[98,8,128]{2,1,0:T(8,128)S(1)} %collective-permute-done.3.chip, f32[98,8,128]{2,1,0:T(8,128)S(1)} %collective-permute-done.4.core, ...), custom_call_target="tpu_custom_call" | custom-call | bytes 6000000 | tf_op jit(solution)/shard_map/pallas_call | solution.py:650
  32.5 0.0 collective-permute-done.7.refs_1_
  32.6 0.0 collective-permute-done.8.refs_2_
  32.6 0.0 collective-permute-done.6.refs_0_
  32.6 1.5 %shard_map.120 = (f32[64,8,512]{2,1,0:T(8,128)}, f32[4,8,512]{2,1,0:T(8,128)}) custom-call(s32[8,512]{1,0:T(8,128)S(1)} %copy-done.2, f32[6,64,8,512]{3,2,1,0:T(8,128)S(1)} %shard_map.116.parts, f32[4,64,8,128]{3,2,1,0:T(8,128)S(1)} %get-tuple-element.38.fixes, f32[8,128]{1,0:T(8,128)S(1)} %get-tuple-element.39.halo_wet, ...), custom_call_target="tpu_custom_call" | custom-call | tf_op jit(solution)/shard_map/pallas_call | solution.py:664
  (4 shorter events, 0.0 us)
Async XLA Ops:
  0.6 8.8 %copy-start.2 = (s32[8,512]{1,0:T(8,128)S(1)}, s32[8,512]{1,0:T(8,128)}, u32[]{:S(2)}) copy-start(s32[8,512]{1,0:T(8,128)} %mask.11) | copy-start | bytes 49156
  0.6 8.7 %copy-start = (f32[64,8,512]{2,1,0:T(8,128)S(1)}, f32[64,8,512]{2,1,0:T(8,128)}, u32[]{:S(2)}) copy-start(f32[64,8,512]{2,1,0:T(8,128)} %state.5) | copy-start | bytes 3145732
  0.7 8.7 %copy-start.3 = (f32[8,512]{1,0:T(8,128)S(1)}, f32[8,512]{1,0:T(8,128)}, u32[]{:S(2)}) copy-start(f32[8,512]{1,0:T(8,128)} %horiz.7) | copy-start | bytes 49156
  0.7 8.7 %copy-start.1 = (f32[63,8,512]{2,1,0:T(8,128)S(1)}, f32[63,8,512]{2,1,0:T(8,128)}, u32[]{:S(2)}) copy-start(f32[63,8,512]{2,1,0:T(8,128)} %vert.3) | copy-start | bytes 3096580
  4.9 8.8 %collective-permute-start.2 = (f32[288,128]{1,0:T(8,128)}, f32[288,128]{1,0:T(8,128)S(1)}, u32[]{:S(2)}, u32[]{:S(2)}) collective-permute-start(f32[288,128]{1,0:T(8,128)} %get-tuple-element.31), channel_id=1, source_target_pairs={{0,6},{1,7},{2,4},{3,5},{4,2},{5,3},{6,0},{7,1},{8,14},{9,15},{10,... | collective-permute-start | bytes 442376 | tf_op jit(solution)/shard_map/ppermute | solution.py:697
  8.6 11.6 %collective-permute-start = (f32[288,128]{1,0:T(8,128)}, f32[288,128]{1,0:T(8,128)S(1)}, u32[]{:S(2)}, u32[]{:S(2)}) collective-permute-start(f32[288,128]{1,0:T(8,128)} %get-tuple-element.29), channel_id=1, source_target_pairs={{0,2},{1,3},{2,0},{3,1},{4,6},{5,7},{6,4},{7,5},{8,10},{9,11},{10,... | collective-permute-start | bytes 442376 | tf_op jit(solution)/shard_map/ppermute | solution.py:697
  8.6 12.7 %collective-permute-start.1 = (f32[288,128]{1,0:T(8,128)}, f32[288,128]{1,0:T(8,128)S(1)}, u32[]{:S(2)}, u32[]{:S(2)}) collective-permute-start(f32[288,128]{1,0:T(8,128)} %get-tuple-element.30), channel_id=1, source_target_pairs={{0,4},{1,5},{2,6},{3,7},{4,0},{5,1},{6,2},{7,3},{8,12},{9,13},{10,... | collective-permute-start | bytes 442376 | tf_op jit(solution)/shard_map/ppermute | solution.py:697
  9.4 0.9 %copy-start.4 = (f32[288,128]{1,0:T(8,128)S(1)}, f32[288,128]{1,0:T(8,128)}, u32[]{:S(2)}) copy-start(f32[288,128]{1,0:T(8,128)} %get-tuple-element.22.chunk) | copy-start | bytes 442372
  14.3 16.6 %collective-permute-start.3 = (f32[98,8,128]{2,1,0:T(8,128)S(1)}, f32[98,8,128]{2,1,0:T(8,128)S(1)}, u32[]{:S(2)}, u32[]{:S(2)}) collective-permute-start(f32[98,8,128]{2,1,0:T(8,128)S(1)} %get-tuple-element.33), channel_id=1, source_target_pairs={{1,2},{3,4},{5,6},{7,8},{9,10},{11,12},{13,14},{15,16},{17,18},{19... | collective-permute-start | bytes 1204232 | tf_op jit(solution)/shard_map/ppermute | solution.py:703
  19.3 11.6 %collective-permute-start.4 = (f32[98,8,128]{2,1,0:T(8,128)S(1)}, f32[98,8,128]{2,1,0:T(8,128)S(1)}, u32[]{:S(2)}, u32[]{:S(2)}) collective-permute-start(f32[98,8,128]{2,1,0:T(8,128)S(1)} %get-tuple-element.34), channel_id=1, source_target_pairs={{0,1},{1,0},{2,3},{3,2},{4,5},{5,4},{6,7},{7,6},{8,9},{9,8},{10,11... | collective-permute-start | bytes 1204232 | tf_op jit(solution)/shard_map/ppermute | solution.py:704
  21.6 1.5 %collective-permute-start.5 = (f32[408,128]{1,0:T(8,128)S(1)}, f32[408,128]{1,0:T(8,128)S(1)}, u32[]{:S(2)}, u32[]{:S(2)}) collective-permute-start(f32[408,128]{1,0:T(8,128)S(1)} %get-tuple-element.36), channel_id=1, source_target_pairs={{0,1},{1,0},{2,3},{3,2},{4,5},{5,4},{6,7},{7,6},{8,9},{9,8},{10,11... | collective-permute-start | bytes 626696 | tf_op jit(solution)/shard_map/ppermute | solution.py:713
  23.1 9.4 %collective-permute-start.7 = (f32[136,128]{1,0:T(8,128)S(1)}, f32[136,128]{1,0:T(8,128)S(1)}, u32[]{:S(2)}, u32[]{:S(2)}) collective-permute-start(f32[136,128]{1,0:T(8,128)S(1)} %get-tuple-element.40), channel_id=1, source_target_pairs={{0,16},{8,24},{16,0},{24,8},{1,17},{9,25},{17,1},{25,9},{2,18},{10... | collective-permute-start | bytes 208904 | tf_op jit(solution)/shard_map/ppermute | solution.py:721
  23.7 8.9 %collective-permute-start.8 = (f32[136,128]{1,0:T(8,128)S(1)}, f32[136,128]{1,0:T(8,128)S(1)}, u32[]{:S(2)}, u32[]{:S(2)}) collective-permute-start(f32[136,128]{1,0:T(8,128)S(1)} %get-tuple-element.41), channel_id=1, source_target_pairs={{0,24},{8,0},{16,8},{24,16},{1,25},{9,1},{17,9},{25,17},{2,26},{10... | collective-permute-start | bytes 208904 | tf_op jit(solution)/shard_map/ppermute | solution.py:721
  26.1 6.4 %collective-permute-start.6 = (f32[136,128]{1,0:T(8,128)S(1)}, f32[136,128]{1,0:T(8,128)S(1)}, u32[]{:S(2)}, u32[]{:S(2)}) collective-permute-start(f32[136,128]{1,0:T(8,128)S(1)} %get-tuple-element.37._), channel_id=1, source_target_pairs={{0,8},{8,16},{16,24},{24,0},{1,9},{9,17},{17,25},{25,1},{2,10},{10... | collective-permute-start | bytes 208904 | tf_op jit(solution)/shard_map/ppermute | solution.py:721
